TPU v7x, 512 devices: a whole 4x8x8 slice. The times are simulated.
512 devices in a mesh: elem: 8 (over z_lo, core), band: 64 (over y, z_hi, x).
Axes of the slice: x: 4, y: 8, z: 8 (z_hi: 2, z_lo: 4; z = z_hi * 4 + z_lo), core: 2. Of those that a mesh axis runs over, the one named last changes fastest.
Arguments:
- coefficients: bfloat16 [32, 128, 8192], P('elem', None, 'band'), may hold values from -6 to 6
- hamiltonian: bfloat16 [32, 27, 128, 128], P('elem'), may hold values from -0.0546875 to 0.0546875
- neighbours: int32 [32, 27], P('elem'), may hold values from 0 to 31, as said below
- basis_values: bfloat16 [32, 4096, 128], P('elem'), may hold values from -0.5 to 0.5
Outputs:
- filtered: bfloat16 [32, 128, 8192], P('elem', None, 'band')
- density: float32 [32, 4096], P('elem', 'band')
Inputs may be any that keep to these rules, and one draw needn't show every extreme that they name: `neighbours`: elements sit on a periodic grid of 8 x 2 x 2 cells in an order drawn from the seed; row e lists the elements at offsets (dx, dy, dz) in -1..1, with k = 9 (dx + 1) + 3 (dy + 1) + dz + 1.
All inputs are finite; a program needn't handle non-finite values.
Results may differ from a plain program's by a relative error of at most 0.0065.
Values may be sent and summed in bfloat16 or wider, within the bound.
No kernel may reach another device: no remote copies, remote signals or barrier semaphores. Data moves between devices by JAX's collectives and lax.ppermute only.
A program may use at most 64 MiB of HBM per device.

v0:
```python
import jax
import jax.numpy as jnp
from jax import lax
from jax.sharding import PartitionSpec as P

BANDS = 8192
CHEB = 6


def apply_operator(current, hamiltonian, neighbours):
    everyone = lax.all_gather(current, "elem", axis=0, tiled=True)
    near = everyone[neighbours]
    return jnp.einsum("ekij,ekjb->eib", hamiltonian, near, preferred_element_type=jnp.float32)


def local(coefficients, hamiltonian, neighbours, basis_values):
    previous = coefficients.astype(jnp.float32)
    current = apply_operator(coefficients, hamiltonian, neighbours)
    for step in range(CHEB - 1):
        following = (
            2.0 * apply_operator(current.astype(jnp.bfloat16), hamiltonian, neighbours) - previous
        )
        previous = current
        current = following
    filtered = current.astype(jnp.bfloat16)
    points_dev = basis_values.shape[1] // lax.axis_size("band")
    first_point = lax.axis_index("band") * points_dev
    own_values = lax.dynamic_slice_in_dim(basis_values, first_point, points_dev, 1)
    orbital = jnp.einsum(
        "epj,ejb->epb",
        own_values,
        lax.all_gather(filtered, "band", axis=2, tiled=True),
        preferred_element_type=jnp.float32,
    )
    summed = jnp.sum(orbital * orbital, axis=2)
    density = summed / BANDS
    return (filtered, density)


def solution(mesh):
    return jax.shard_map(
        local,
        mesh=mesh,
        in_specs=(
            P("elem", None, "band"),
            P("elem", None, None, None),
            P("elem", None),
            P("elem", None, None),
        ),
        out_specs=(P("elem", None, "band"), P("elem", "band")),
        check_vma=False,
    )
```

profile of v0, /device:TPU:1, one launch (start us, length us, event | category | flops | bytes accessed | tf_op | source)
XLA Modules:
  0.0 522.5 jit_solution(13673761945022086740)
XLA Ops:
  7.2 0.0 copy-start
  7.2 0.0 all-gather.8.cloned.1.call-start
  7.2 0.7 all-gather.8.cloned.1.call-update
  7.9 0.0 all-gather.10.cloned.1.call-start
  8.0 1.0 compare_select_fusion
  8.9 0.1 reshape.6
  9.0 44.5 %all-gather.8.cloned.1.call-done = bf16[32,128,128]{2,1,0:T(8,128)(2,1)} async-done(((bf16[4,128,128]{2,1,0:T(8,128)(2,1)}), bf16[32,128,128]{2,1,0:T(8,128)(2,1)}) %all-gather.8.cloned.1.call-update) | async-done | bytes 1048592 | tf_op jit(solution)/shard_map/all_gather | solution.py:11
  53.5 4.0 gather_fusion
  57.5 0.0 copy-done
  57.5 3.3 convolution_bitcast_fusion.5
  60.9 0.0 copy-start.2
  60.9 0.7 copy-done.2
  61.6 0.7 convert_bitcast_fusion.1
  62.2 1.7 copy.11
  63.9 0.0 all-gather.10.cloned.1.call-update
  63.9 0.0 all-gather.12.cloned.1.call-start
  64.0 1.7 copy.13
  65.6 37.3 %all-gather.10.cloned.1.call-done = bf16[32,128,128]{2,1,0:T(8,128)(2,1)} async-done(((bf16[4,128,128]{2,1,0:T(8,128)(2,1)}), bf16[32,128,128]{2,1,0:T(8,128)(2,1)}) %all-gather.10.cloned.1.call-update) | async-done | bytes 1048592 | tf_op jit(solution)/shard_map/all_gather | solution.py:11
  103.0 4.0 gather_fusion.1
  107.0 4.1 fusion.19
  111.1 1.7 copy.14
  112.8 0.0 all-gather.12.cloned.1.call-update
  112.8 0.0 all-gather.14.cloned.1.call-start
  112.8 39.2 %all-gather.12.cloned.1.call-done = bf16[32,128,128]{2,1,0:T(8,128)(2,1)} async-done(((bf16[4,128,128]{2,1,0:T(8,128)(2,1)}), bf16[32,128,128]{2,1,0:T(8,128)(2,1)}) %all-gather.12.cloned.1.call-update) | async-done | bytes 1048592 | tf_op jit(solution)/shard_map/all_gather | solution.py:11
  152.0 4.0 gather_fusion.2
  156.1 3.3 fusion.3
  159.4 0.0 copy-start.1
  159.4 0.7 copy-done.1
  160.2 0.7 convert_bitcast_fusion
  160.8 1.6 copy.16
  162.5 0.0 all-gather.14.cloned.1.call-update
  162.5 0.0 all-gather.16.cloned.1.call-start
  162.6 39.2 %all-gather.14.cloned.1.call-done = bf16[32,128,128]{2,1,0:T(8,128)(2,1)} async-done(((bf16[4,128,128]{2,1,0:T(8,128)(2,1)}), bf16[32,128,128]{2,1,0:T(8,128)(2,1)}) %all-gather.14.cloned.1.call-update) | async-done | bytes 1048592 | tf_op jit(solution)/shard_map/all_gather | solution.py:11
  201.8 4.0 gather_fusion.3
  205.8 4.1 fusion.20
  209.9 1.7 copy.18
  211.6 0.0 all-gather.16.cloned.1.call-update
  211.6 0.0 all-gather.18.cloned.1.call-start
  211.6 39.2 %all-gather.16.cloned.1.call-done = bf16[32,128,128]{2,1,0:T(8,128)(2,1)} async-done(((bf16[4,128,128]{2,1,0:T(8,128)(2,1)}), bf16[32,128,128]{2,1,0:T(8,128)(2,1)}) %all-gather.16.cloned.1.call-update) | async-done | bytes 1048592 | tf_op jit(solution)/shard_map/all_gather | solution.py:11
  250.9 4.0 gather_fusion.4
  254.9 4.0 fusion.16
  258.9 1.7 copy.20
  260.6 0.0 all-gather.18.cloned.1.call-update
  260.6 0.2 all-gather.20.cloned.1.call-start
  260.8 39.0 %all-gather.18.cloned.1.call-done = bf16[32,128,128]{2,1,0:T(8,128)(2,1)} async-done(((bf16[4,128,128]{2,1,0:T(8,128)(2,1)}), bf16[32,128,128]{2,1,0:T(8,128)(2,1)}) %all-gather.18.cloned.1.call-update) | async-done | bytes 1048592 | tf_op jit(solution)/shard_map/all_gather | solution.py:11
  299.9 4.0 gather_fusion.5
  303.9 4.0 fusion.14
  307.9 0.0 all-gather.20.cloned.1.call-update
  307.9 1.7 copy.23
  309.6 199.0 %all-gather.20.cloned.1.call-done = bf16[4,128,8192]{1,2,0:T(8,128)(2,1)} async-done(((bf16[4,128,128]{1,2,0:T(8,128)(2,1)}), bf16[4,128,8192]{1,2,0:T(8,128)(2,1)}) %all-gather.20.cloned.1.call-update) | async-done | bytes 8388624 | tf_op jit(solution)/shard_map/all_gather | solution.py:32
  508.6 6.5 %fusion = f32[4,64]{1,0:T(4,128)S(1)} fusion(bf16[4,128,8192]{1,2,0:T(8,128)(2,1)} %all-gather.20.cloned.1.call-done, bf16[4,4096,128]{2,1,0:T(8,128)(2,1)} %param.7, s32[]{:T(128)S(6)} %select_n.5), kind=kOutput, calls=%fused_computation.7 | convolution fusion | flops 541064960 | bytes 8455172 | tf_op jit(solution)/shard_map/epj,ejb->epb/dot_general | solution.py:29
  515.1 0.6 broadcast_multiply_fusion
  (1 shorter events, 0.0 us)
Async XLA Ops:
  7.2 50.4 %copy-start = (bf16[4,27,128,128]{3,2,1,0:T(8,128)(2,1)S(1)}, bf16[4,27,128,128]{3,2,1,0:T(8,128)(2,1)}, u32[]{:S(2)}) copy-start(bf16[4,27,128,128]{3,2,1,0:T(8,128)(2,1)} %param.5) | copy-start | bytes 10616836
  7.2 46.3 %all-gather.8.cloned.1.call-start = ((), (), s32[]{:S(2)}) async-start(), calls=%async_computation | async-start | bytes 1179648 | tf_op jit(solution)/shard_map/all_gather | solution.py:11
  7.9 95.0 %all-gather.10.cloned.1.call-start = ((), (), s32[]{:S(2)}) async-start(), calls=%async_computation.1 | async-start | bytes 1179648 | tf_op jit(solution)/shard_map/all_gather | solution.py:11
  60.9 0.7 copy-start.2
  63.9 88.1 %all-gather.12.cloned.1.call-start = ((), (), s32[]{:S(2)}) async-start(), calls=%async_computation.2 | async-start | bytes 1179648 | tf_op jit(solution)/shard_map/all_gather | solution.py:11
  112.8 89.0 %all-gather.14.cloned.1.call-start = ((), (), s32[]{:S(2)}) async-start(), calls=%async_computation.3 | async-start | bytes 1179648 | tf_op jit(solution)/shard_map/all_gather | solution.py:11
  159.4 0.7 copy-start.1
  162.5 88.3 %all-gather.16.cloned.1.call-start = ((), (), s32[]{:S(2)}) async-start(), calls=%async_computation.4 | async-start | bytes 1179648 | tf_op jit(solution)/shard_map/all_gather | solution.py:11
  211.6 88.3 %all-gather.18.cloned.1.call-start = ((), (), s32[]{:S(2)}) async-start(), calls=%async_computation.5 | async-start | bytes 1179648 | tf_op jit(solution)/shard_map/all_gather | solution.py:11
  260.6 248.0 %all-gather.20.cloned.1.call-start = ((), (), s32[]{:S(2)}) async-start(), calls=%async_computation.6 | async-start | bytes 8519680 | tf_op jit(solution)/shard_map/all_gather | solution.py:32
Sparse Core Ops, SparseCore 0:
  10.1 43.3 all-gather.7
  64.0 38.8 all-gather.9
  112.9 39.0 all-gather.11
  162.6 39.0 all-gather.13
  211.7 39.0 all-gather.15
  260.7 39.0 all-gather.17
  308.0 200.4 all-gather.19
where the time goes:
time: 525 us; the launch traced here: 523 us
  waiting for transfers between devices  438 us (83%)
  local copies, waits for them, and re-layouts  37.4 us (7%)
  matrix products  29.4 us (6%)
  between operations  14.2 us (3%)
    all_gather x6, waiting for transfers between devices, apply_operator(): everyone = lax.all_gather(current, 'elem', axis=0, tiled=True)  238 us
    all_gather x1, waiting for transfers between devices, local(): lax.all_gather(filtered, 'band', axis=2, tiled=True)  199 us
    gather x6, local copies, waits for them, and re-layouts, apply_operator(): near = everyone[neighbours]  24.3 us
    dot_general x6, matrix products, apply_operator(): jnp.einsum('ekij,ekjb->eib', hamiltonian, near, preferred_element_type=jn...  22.9 us
  transfers between devices with their start and end apart: 7, of which 7 were waited for; matrix products, arithmetic and copies ran while one was open for 1% of the time, Pallas kernels for 0%

commit v1 on v0

v1 whole, which is shorter than its diff:
```python
import functools

import jax
import jax.numpy as jnp
from jax import lax
from jax.experimental import pallas as pl
from jax.experimental.pallas import tpu as pltpu
from jax.sharding import PartitionSpec as P

BANDS = 8192
NB = 128
POINTS = 4096
PLANES = 8
KDIM = 12 * NB
WIDE = 4 * NB
NX = 4
EDGE = 16
BF = jnp.bfloat16
F32 = jnp.float32
NT = (((1,), (1,)), ((), ()))


def fold_kernel(pair_ref, near_ref, h_ref, out_ref):
    e = 2 * pair_ref[0] + pl.program_id(0)
    rows = lax.broadcasted_iota(jnp.int32, (NB, NB), 0)
    cols = lax.broadcasted_iota(jnp.int32, (NB, NB), 1)
    eye = (rows == cols).astype(F32).astype(BF)
    choices = ((1,), (0, 2))
    for dx in range(3):
        ids = [
            near_ref[e, 9 * dx + 3 * b[0] + c[0]] for b in choices for c in choices
        ]
        spot = 0
        for b in choices:
            for c in choices:
                total = None
                for i in b:
                    for j in c:
                        part = lax.dot_general(
                            eye, h_ref[0, 9 * dx + 3 * i + j], NT, preferred_element_type=F32
                        )
                        total = part if total is None else total + part
                rank = jnp.int32(0)
                for other in range(4):
                    if other != spot:
                        rank = rank + (ids[other] < ids[spot]).astype(jnp.int32)
                row = pl.multiple_of((4 * dx + rank) * NB, NB)
                out_ref[0, pl.ds(row, NB), :] = total.astype(BF)
                spot += 1


def fold(hamiltonian, neighbours, pair):
    return pl.pallas_call(
        fold_kernel,
        out_shape=jax.ShapeDtypeStruct((2, KDIM, NB), BF),
        grid_spec=pltpu.PrefetchScalarGridSpec(
            num_scalar_prefetch=2,
            grid=(2,),
            in_specs=[
                pl.BlockSpec((1, 27, NB, NB), lambda t, pair, near: (2 * pair[0] + t, 0, 0, 0))
            ],
            out_specs=pl.BlockSpec((1, KDIM, NB), lambda t, pair, near: (t, 0, 0)),
        ),
        compiler_params=pltpu.CompilerParams(vmem_limit_bytes=16 * 2**20),
        cost_estimate=pl.CostEstimate(flops=2 * 27 * 2 * NB**3, bytes_accessed=2600000, transcendentals=0),
    )(pair, neighbours, hamiltonian)


def turn_kernel(y_ref, near_ref, out_ref):
    for e in range(4):
        block = y_ref[e].astype(F32).T.astype(BF)
        for copy in range(4):
            out_ref[copy, pl.ds(e * NB, NB), :] = block
    for copy in range(4):
        out_ref[copy, pl.ds(4 * NB, EDGE), :] = near_ref[...]


def turn(coefficients, near):
    return pl.pallas_call(
        turn_kernel,
        out_shape=jax.ShapeDtypeStruct((4, 4 * NB + EDGE, NB), BF),
        compiler_params=pltpu.CompilerParams(vmem_limit_bytes=16 * 2**20),
    )(coefficients, near)


def filter_kernel(near_ref, base_ref, *refs):
    h_refs = refs[:16]
    y_own, y_other, b_ref, filt_ref, dens_ref = refs[16:21]
    hbuf, ybuf, za, zb, bbuf, pid, slot, h_sems, b_sem = refs[21:]
    core = base_ref[16]

    rep = jnp.int32(0)
    for x in range(PLANES):
        ids = [near_ref[rep, 9 + 3 * b + c] for b in (1, 0) for c in (1, 0)]
        following = near_ref[rep, 18 + 4]
        for a, b in ((0, 1), (2, 3), (0, 2), (1, 3), (1, 2)):
            ids[a], ids[b] = jnp.minimum(ids[a], ids[b]), jnp.maximum(ids[a], ids[b])
        for r in range(4):
            slot[ids[r]] = 4 * x + r
        rep = following

    def place(g):
        s = slot[g]
        return s // 4, pl.multiple_of((s % 4) * NB, NB), s

    def h_copy(ref, k, g):
        x, lane, s = place(g)
        return pltpu.make_async_copy(
            ref.at[k], hbuf.at[x, :, pl.ds(lane, NB)], h_sems.at[s]
        )

    for i, ref in enumerate(h_refs):
        for k in range(2):
            h_copy(ref, k, base_ref[i] + k).start()
    b_copy = pltpu.make_async_copy(b_ref, bbuf, b_sem)
    b_copy.start()

    for source, side in ((y_own, core), (y_other, 1 - core)):
        for z in range(4):
            for e in range(4):
                x, lane, _ = place((2 * z + side) * 4 + e)
                block = source[z, pl.ds(e * NB, NB), :]
                ybuf[0, x, :, pl.ds(lane, NB)] = block
                za[x, :, pl.ds(lane, NB)] = block.astype(F32)

    def around(src, x):
        return jnp.concatenate(
            [ybuf[src, (x + 7) % 8], ybuf[src, x], ybuf[src, (x + 1) % 8]], axis=1
        )

    for step in range(5):
        src, dst = step % 2, 1 - step % 2
        past = zb if step % 2 == 0 else za
        for x in range(PLANES):
            if step == 0:
                for r in range(4):
                    pltpu.make_async_copy(
                        h_refs[0].at[0], hbuf.at[x, :, pl.ds(r * NB, NB)], h_sems.at[4 * x + r]
                    ).wait()
            acc = jnp.dot(around(src, x), hbuf[x], preferred_element_type=F32)
            new = acc if step == 0 else 2.0 * acc - past[x]
            past[x] = new
            ybuf[dst, x] = new.astype(BF)

    b_copy.wait()
    mine = base_ref[17]
    for e in range(4):
        x, lane, _ = place(mine + e)
        left = lax.rem(x + 7, 8)
        right = lax.rem(x + 1, 8)
        near = jnp.concatenate([ybuf[1, left], ybuf[1, x], ybuf[1, right]], axis=1)
        acc = jnp.dot(near, hbuf[x, :, pl.ds(lane, NB)], preferred_element_type=F32)
        last = (2.0 * acc - za[x, :, pl.ds(lane, NB)]).astype(BF)
        filt_ref[e] = last.astype(F32).T.astype(BF)
        for p in range(0, POINTS, 512):
            phi = lax.dot_general(
                last, bbuf[e, pl.ds(p, 512), :], NT, preferred_element_type=F32
            )
            dens_ref[e : e + 1, p : p + 512] = jnp.sum(phi * phi, axis=0, keepdims=True)


def filtering(near, base, pieces, y_own, y_other, basis_values):
    anywhere = pl.BlockSpec(memory_space=pl.ANY)
    smem = pl.BlockSpec(memory_space=pltpu.SMEM)
    vmem = pl.BlockSpec(memory_space=pltpu.VMEM)
    return pl.pallas_call(
        filter_kernel,
        out_shape=(
            jax.ShapeDtypeStruct((4, NB, NB), BF),
            jax.ShapeDtypeStruct((4, POINTS), F32),
        ),
        in_specs=[smem, smem] + [anywhere] * 16 + [vmem, vmem, anywhere],
        out_specs=(vmem, vmem),
        scratch_shapes=[
            pltpu.VMEM((PLANES, KDIM, WIDE), BF),
            pltpu.VMEM((2, PLANES, NB, WIDE), BF),
            pltpu.VMEM((PLANES, NB, WIDE), F32),
            pltpu.VMEM((PLANES, NB, WIDE), F32),
            pltpu.VMEM((4, POINTS, NB), BF),
            pltpu.SMEM((32,), jnp.int32),
            pltpu.SMEM((32,), jnp.int32),
            pltpu.SemaphoreType.DMA((32,)),
            pltpu.SemaphoreType.DMA,
        ],
        compiler_params=pltpu.CompilerParams(vmem_limit_bytes=48 * 2**20),
    )(near, base, *pieces, y_own, y_other, basis_values)


def routes(nbands):
    def index(y, h, x, lo, core):
        return (lo * 2 + core) * nbands + (y * 2 + h) * NX + x

    ny = nbands // (2 * NX)
    every = [
        (y, h, x, lo, core)
        for y in range(ny)
        for h in range(2)
        for x in range(NX)
        for lo in range(4)
        for core in range(2)
    ]

    def along_z(d):
        pairs = []
        for y, h, x, lo, core in every:
            z = (4 * h + lo + d) % 8
            pairs.append((index(y, h, x, lo, core), index(y, z // 4, x, z % 4, core)))
        return pairs

    return (
        along_z(1),
        along_z(-1),
        [(index(*q), index(q[0], q[1], q[2] ^ 1, q[3], q[4])) for q in every],
        [(index(*q), index(q[0] ^ 1, q[1], q[2], q[3], q[4])) for q in every],
        [(index(*q), index(q[0], q[1], q[2], q[3], q[4] ^ 1)) for q in every],
    )


def local(nbands, coefficients, hamiltonian, neighbours, basis_values):
    both = ("elem", "band")
    up, down, over_x, over_y, over_core = routes(nbands)
    elem = lax.axis_index("elem")
    band = lax.axis_index("band")
    lo, core = elem // 2, elem % 2
    pa = (band % NX + band // (2 * NX)) % 2
    pb = 1 - pa

    def move(value, pairs):
        return lax.ppermute(value, both, pairs)

    own_a = fold(hamiltonian, neighbours, pa[None])
    own_b = fold(hamiltonian, neighbours, pb[None])
    from_below = move(own_a, up)
    from_above = move(own_b, down)

    near = jnp.pad(neighbours.astype(BF), ((0, EDGE - 4), (0, NB - 27)))
    turned = turn(coefficients, near)
    groups = [[2 * z + c for z in range(4)] for c in range(2)]
    y_own = lax.all_to_all(turned, "elem", 0, 0, axis_index_groups=groups)
    y_other = move(y_own, over_core)

    far_a = move(from_below, up)
    far_b = move(from_above, down)
    below_b = move(from_below, over_x)
    above_a = move(from_above, over_y)

    pieces = [own_a, own_b, from_below, from_above, far_a, far_b, below_b, above_a]
    swapped = [move(piece, over_core) for piece in pieces]

    def first(z, c, pair):
        return (((lo + z) % 4) * 2 + c) * 4 + 2 * pair

    order = [(0, pa), (0, pb), (3, pa), (1, pb), (2, pa), (2, pb), (3, pb), (1, pa)]
    base = jnp.stack(
        [first(z, core, pair) for z, pair in order]
        + [first(z, 1 - core, pair) for z, pair in order]
        + [core, elem * 4]
    ).astype(jnp.int32)

    def table(y):
        return y[:, 4 * NB : 4 * NB + 4, :27].astype(jnp.int32)

    ids = jnp.stack([table(y_own), table(y_other)], axis=1)
    ids = jnp.where(core == 0, ids, ids[:, ::-1]).reshape(32, 27)

    filtered, partial = filtering(ids, base, pieces + swapped, y_own, y_other, basis_values)
    parts = partial.reshape(4, nbands, POINTS // nbands).swapaxes(0, 1)
    density = jnp.sum(lax.all_to_all(parts, "band", 0, 0), axis=0) / BANDS
    return filtered, density


def solution(mesh):
    return jax.shard_map(
        functools.partial(local, mesh.shape["band"]),
        mesh=mesh,
        in_specs=(
            P("elem", None, "band"),
            P("elem", None, None, None),
            P("elem", None),
            P("elem", None, None),
        ),
        out_specs=(P("elem", None, "band"), P("elem", "band")),
        check_vma=False,
    )
```

time: 525 us -> 129 us (0.25)
  waiting for transfers between devices: 438 us -> 8.43 us
  starting transfers between devices: 0.47 us -> 62.9 us
  local copies, waits for them, and re-layouts: 37.4 us -> 4.69 us
  matrix products: 29.4 us -> 0 us
  blocking collectives: 0 us -> 24.7 us
  Pallas kernels: 0 us -> 23.2 us
  between operations: 14.2 us -> 1.07 us
    all_gather x7 -> x0, waiting for transfers between devices: 437 us -> none  [the longest x6 238 us: apply_operator(): everyone = lax.all_gather(current, 'elem', axis=0, tiled=True)]
    ppermute x0 -> x15, starting transfers between devices: none -> 55.1 us  [move(): return lax.ppermute(value, both, pairs)]
    dot_general x7 -> x0, matrix products: 29.4 us -> none  [the longest x6 22.9 us: apply_operator(): jnp.einsum('ekij,ekjb->eib', hamiltonian, near, preferred_element_type=jn...]
    all_to_all x0 -> x1, blocking collectives: none -> 24.7 us  [local(): density = jnp.sum(lax.all_to_all(parts, 'band', 0, 0), axis=0) / BANDS]
    gather x6 -> x0, local copies, waits for them, and re-layouts: 24.3 us -> none  [apply_operator(): near = everyone[neighbours]]
    pallas_call x0 -> x4, Pallas kernels: none -> 23.2 us  [the longest x1 18.1 us: filtering(): pl.pallas_call(filter_kernel, out_shape=(jax.ShapeDtypeStruct((4, NB, NB)...]
    ppermute x0 -> x15, waiting for transfers between devices: none -> 8.43 us  [move(): return lax.ppermute(value, both, pairs)]
    convert_element_type x5 -> x0, local copies, waits for them, and re-layouts: 8.28 us -> none  [local(): current.astype(jnp.bfloat16)]
  transfers between devices with their start and end apart: 7 -> 16, of which waited for: 7 -> 4; matrix products, arithmetic and copies ran while one was open for 1% -> 0% of each run, Pallas kernels for 0% -> 3%
where the time goes in v1:
time: 129 us; the launch traced here: 127 us
  starting transfers between devices  62.9 us (49%)
  blocking collectives  24.7 us (19%)
  Pallas kernels  23.2 us (18%)
  waiting for transfers between devices  8.43 us (7%)
  local copies, waits for them, and re-layouts  4.69 us (4%)
  other arithmetic  2.23 us (2%)
    ppermute x15, starting transfers between devices, move(): return lax.ppermute(value, both, pairs)  55.1 us
    all_to_all x1, blocking collectives, local(): density = jnp.sum(lax.all_to_all(parts, 'band', 0, 0), axis=0) / BANDS  24.7 us
    pallas_call x1, Pallas kernels, filtering(): pl.pallas_call(filter_kernel, out_shape=(jax.ShapeDtypeStruct((4, NB, NB)...  18.1 us
    ppermute x15, waiting for transfers between devices, move(): return lax.ppermute(value, both, pairs)  8.43 us
    all_to_all x1, starting transfers between devices, local(): y_own = lax.all_to_all(turned, 'elem', 0, 0, axis_index_groups=groups)  7.81 us
    pallas_call x2, Pallas kernels, fold(): pl.pallas_call(fold_kernel, out_shape=jax.ShapeDtypeStruct((2, KDIM, NB),...  4.14 us
    unnamed x12, local copies, waits for them, and re-layouts  3.84 us
  transfers between devices with their start and end apart: 16, of which 4 were waited for; matrix products, arithmetic and copies ran while one was open for 0% of the time, Pallas kernels for 3%

profile of v1, /device:TPU:1, one launch (start us, length us, event | category | flops | bytes accessed | tf_op | source)
XLA Modules:
  0.0 127.2 jit_solution(7253260575912039763)
XLA Ops:
  0.6 0.0 copy-start.4
  0.6 0.7 convert_element_type.4
  1.4 0.0 copy-start.2
  1.4 0.9 copy-done.2
  2.3 0.9 shard_map.59
  3.2 7.8 %all-to-all-start = ((bf16[4,528,128]{2,1,0:T(8,128)(2,1)}), bf16[4,528,128]{2,1,0:T(8,128)(2,1)S(1)}, u32[]{:S(2)}, u32[]{:S(2)}) async-start(bf16[4,528,128]{2,1,0:T(8,128)(2,1)} %shard_map.59), calls=%async_computation | async-start | bytes 1081344 | tf_op jit(solution)/shard_map/all_to_all | solution.py:239
  11.0 0.0 copy-start
  11.0 2.0 %copy-done = bf16[4,27,128,128]{3,2,1,0:T(8,128)(2,1)S(1)} copy-done((bf16[4,27,128,128]{3,2,1,0:T(8,128)(2,1)S(1)}, bf16[4,27,128,128]{3,2,1,0:T(8,128)(2,1)}, u32[]{:S(2)}) %copy-start) | copy-done | bytes 3538968
  13.0 0.0 copy-start.3
  13.0 0.7 copy-done.3
  13.7 0.0 copy-start.1
  13.7 2.1 %shard_map.61.refs_1_ = bf16[2,1536,128]{2,1,0:T(8,128)(2,1)S(1)} custom-call(s32[1]{0:T(128)} %bitcast.22.pair_ref, s32[4,27]{1,0:T(4,128)S(1)} %copy-done.3, bf16[4,27,128,128]{3,2,1,0:T(8,128)(2,1)S(1)} %copy-done), custom_call_target="tpu_custom_call" | custom-call | flops 226492416 | bytes 2600000 | tf_op jit(solution)/shard_map/pallas_call | solution.py:53
  15.8 8.2 %collective-permute-start.2 = (bf16[2,1536,128]{2,1,0:T(8,128)(2,1)S(1)}, bf16[2,1536,128]{2,1,0:T(8,128)(2,1)S(1)}, u32[]{:S(2)}, u32[]{:S(2)}) collective-permute-start(bf16[2,1536,128]{2,1,0:T(8,128)(2,1)S(1)} %shard_map.61.refs_1_), channel_id=1, source_target_pairs={{0,388},{64,452},{128,0},{192,64},{256,128},{320,192},{384,256},{4... | collective-permute-start | bytes 2359304 | tf_op jit(solution)/shard_map/ppermute | solution.py:229
  24.0 0.0 copy-done.4
  24.0 0.0 copy-done.1
  24.0 2.1 %shard_map.60.refs_0_ = bf16[2,1536,128]{2,1,0:T(8,128)(2,1)S(1)} custom-call(s32[1]{0:T(128)} %bitcast.21.pair_ref, s32[4,27]{1,0:T(4,128)S(1)} %copy-done.4, bf16[4,27,128,128]{3,2,1,0:T(8,128)(2,1)S(1)} %copy-done.1), custom_call_target="tpu_custom_call" | custom-call | flops 226492416 | bytes 2600000 | tf_op jit(solution)/shard_map/pallas_call | solution.py:53
  26.1 1.9 %collective-permute-start.1 = (bf16[2,1536,128]{2,1,0:T(8,128)(2,1)S(1)}, bf16[2,1536,128]{2,1,0:T(8,128)(2,1)}, u32[]{:S(2)}, u32[]{:S(2)}) collective-permute-start(bf16[2,1536,128]{2,1,0:T(8,128)(2,1)S(1)} %shard_map.60.refs_0_), channel_id=1, source_target_pairs={{0,128},{64,192},{128,256},{192,320},{256,384},{320,448},{384,4},{... | collective-permute-start | bytes 2359304 | tf_op jit(solution)/shard_map/ppermute | solution.py:229
  28.0 3.4 %collective-permute-start.8 = (bf16[2,1536,128]{2,1,0:T(8,128)(2,1)S(1)}, bf16[2,1536,128]{2,1,0:T(8,128)(2,1)}, u32[]{:S(2)}, u32[]{:S(2)}) collective-permute-start(bf16[2,1536,128]{2,1,0:T(8,128)(2,1)S(1)} %shard_map.61.refs_1_), channel_id=1, source_target_pairs={{0,64},{64,0},{128,192},{192,128},{256,320},{320,256},{384,448},{4... | collective-permute-start | bytes 2359304 | tf_op jit(solution)/shard_map/ppermute | solution.py:229
  31.5 1.9 %collective-permute-start.7 = (bf16[2,1536,128]{2,1,0:T(8,128)(2,1)S(1)}, bf16[2,1536,128]{2,1,0:T(8,128)(2,1)}, u32[]{:S(2)}, u32[]{:S(2)}) collective-permute-start(bf16[2,1536,128]{2,1,0:T(8,128)(2,1)S(1)} %shard_map.60.refs_0_), channel_id=1, source_target_pairs={{0,64},{64,0},{128,192},{192,128},{256,320},{320,256},{384,448},{4... | collective-permute-start | bytes 2359304 | tf_op jit(solution)/shard_map/ppermute | solution.py:229
  33.4 0.0 all-to-all-done.refs_16_
  33.4 2.4 %collective-permute-start = (bf16[4,528,128]{2,1,0:T(8,128)(2,1)S(1)}, bf16[4,528,128]{2,1,0:T(8,128)(2,1)S(1)}, u32[]{:S(2)}, u32[]{:S(2)}) collective-permute-start(bf16[4,528,128]{2,1,0:T(8,128)(2,1)S(1)} %all-to-all-done.refs_16_), channel_id=1, source_target_pairs={{0,64},{64,0},{128,192},{192,128},{256,320},{320,256},{384,448},{4... | collective-permute-start | bytes 1622024 | tf_op jit(solution)/shard_map/ppermute | solution.py:229
  35.8 3.8 %collective-permute-done.2.refs_3_ = bf16[2,1536,128]{2,1,0:T(8,128)(2,1)S(1)} collective-permute-done((bf16[2,1536,128]{2,1,0:T(8,128)(2,1)S(1)}, bf16[2,1536,128]{2,1,0:T(8,128)(2,1)S(1)}, u32[]{:S(2)}, u32[]{:S(2)}) %collective-permute-start.2) | collective-permute-done | bytes 786464 | tf_op jit(solution)/shard_map/ppermute | solution.py:229
  39.6 5.3 %collective-permute-start.4 = (bf16[2,1536,128]{2,1,0:T(8,128)(2,1)S(1)}, bf16[2,1536,128]{2,1,0:T(8,128)(2,1)}, u32[]{:S(2)}, u32[]{:S(2)}) collective-permute-start(bf16[2,1536,128]{2,1,0:T(8,128)(2,1)S(1)} %collective-permute-done.2.refs_3_), channel_id=1, source_target_pairs={{0,388},{64,452},{128,0},{192,64},{256,128},{320,192},{384,256},{4... | collective-permute-start | bytes 2359304 | tf_op jit(solution)/shard_map/ppermute | solution.py:229
  44.9 1.9 %collective-permute-done.1.refs_2_ = bf16[2,1536,128]{2,1,0:T(8,128)(2,1)} collective-permute-done((bf16[2,1536,128]{2,1,0:T(8,128)(2,1)S(1)}, bf16[2,1536,128]{2,1,0:T(8,128)(2,1)}, u32[]{:S(2)}, u32[]{:S(2)}) %collective-permute-start.1) | collective-permute-done | bytes 786464 | tf_op jit(solution)/shard_map/ppermute | solution.py:229
  46.8 3.2 %collective-permute-start.6 = (bf16[2,1536,128]{2,1,0:T(8,128)(2,1)S(1)}, bf16[2,1536,128]{2,1,0:T(8,128)(2,1)}, u32[]{:S(2)}, u32[]{:S(2)}) collective-permute-start(bf16[2,1536,128]{2,1,0:T(8,128)(2,1)S(1)} %collective-permute-done.2.refs_3_), channel_id=1, source_target_pairs={{0,8},{64,72},{128,136},{192,200},{256,264},{320,328},{384,392},{4... | collective-permute-start | bytes 2359304 | tf_op jit(solution)/shard_map/ppermute | solution.py:229
  50.0 0.0 collective-permute-done.8.refs_9_
  50.0 1.9 %collective-permute-start.3 = (bf16[2,1536,128]{2,1,0:T(8,128)(2,1)}, bf16[2,1536,128]{2,1,0:T(8,128)(2,1)}, u32[]{:S(2)}, u32[]{:S(2)}) collective-permute-start(bf16[2,1536,128]{2,1,0:T(8,128)(2,1)} %collective-permute-done.1.refs_2_), channel_id=1, source_target_pairs={{0,128},{64,192},{128,256},{192,320},{256,384},{320,448},{384,4},{... | collective-permute-start | bytes 2359304 | tf_op jit(solution)/shard_map/ppermute | solution.py:229
  52.0 0.0 collective-permute-done.7.refs_8_
  52.0 3.1 %collective-permute-start.5 = (bf16[2,1536,128]{2,1,0:T(8,128)(2,1)}, bf16[2,1536,128]{2,1,0:T(8,128)(2,1)}, u32[]{:S(2)}, u32[]{:S(2)}) collective-permute-start(bf16[2,1536,128]{2,1,0:T(8,128)(2,1)} %collective-permute-done.1.refs_2_), channel_id=1, source_target_pairs={{0,1},{64,65},{128,129},{192,193},{256,257},{320,321},{384,385},{4... | collective-permute-start | bytes 2359304 | tf_op jit(solution)/shard_map/ppermute | solution.py:229
  55.1 0.0 collective-permute-done.refs_17_
  55.1 4.9 %collective-permute-start.10 = (bf16[2,1536,128]{2,1,0:T(8,128)(2,1)S(1)}, bf16[2,1536,128]{2,1,0:T(8,128)(2,1)}, u32[]{:S(2)}, u32[]{:S(2)}) collective-permute-start(bf16[2,1536,128]{2,1,0:T(8,128)(2,1)S(1)} %collective-permute-done.2.refs_3_), channel_id=1, source_target_pairs={{0,64},{64,0},{128,192},{192,128},{256,320},{320,256},{384,448},{4... | collective-permute-start | bytes 2359304 | tf_op jit(solution)/shard_map/ppermute | solution.py:229
  60.2 0.0 collective-permute-done.4.refs_5_
  60.2 4.4 %collective-permute-start.9 = (bf16[2,1536,128]{2,1,0:T(8,128)(2,1)}, bf16[2,1536,128]{2,1,0:T(8,128)(2,1)}, u32[]{:S(2)}, u32[]{:S(2)}) collective-permute-start(bf16[2,1536,128]{2,1,0:T(8,128)(2,1)} %collective-permute-done.1.refs_2_), channel_id=1, source_target_pairs={{0,64},{64,0},{128,192},{192,128},{256,320},{320,256},{384,448},{4... | collective-permute-start | bytes 2359304 | tf_op jit(solution)/shard_map/ppermute | solution.py:229
  64.5 0.9 collective-permute-done.6.refs_7_
  65.4 5.3 %collective-permute-start.12 = (bf16[2,1536,128]{2,1,0:T(8,128)(2,1)}, bf16[2,1536,128]{2,1,0:T(8,128)(2,1)}, u32[]{:S(2)}, u32[]{:S(2)}) collective-permute-start(bf16[2,1536,128]{2,1,0:T(8,128)(2,1)} %collective-permute-done.4.refs_5_), channel_id=1, source_target_pairs={{0,64},{64,0},{128,192},{192,128},{256,320},{320,256},{384,448},{4... | collective-permute-start | bytes 2359304 | tf_op jit(solution)/shard_map/ppermute | solution.py:229
  70.7 0.0 collective-permute-done.3.refs_4_
  70.7 4.6 %collective-permute-start.14 = (bf16[2,1536,128]{2,1,0:T(8,128)(2,1)}, bf16[2,1536,128]{2,1,0:T(8,128)(2,1)}, u32[]{:S(2)}, u32[]{:S(2)}) collective-permute-start(bf16[2,1536,128]{2,1,0:T(8,128)(2,1)} %collective-permute-done.6.refs_7_), channel_id=1, source_target_pairs={{0,64},{64,0},{128,192},{192,128},{256,320},{320,256},{384,448},{4... | collective-permute-start | bytes 2359304 | tf_op jit(solution)/shard_map/ppermute | solution.py:229
  75.3 0.0 collective-permute-done.5.refs_6_
  75.3 1.9 %collective-permute-start.11 = (bf16[2,1536,128]{2,1,0:T(8,128)(2,1)}, bf16[2,1536,128]{2,1,0:T(8,128)(2,1)}, u32[]{:S(2)}, u32[]{:S(2)}) collective-permute-start(bf16[2,1536,128]{2,1,0:T(8,128)(2,1)} %collective-permute-done.3.refs_4_), channel_id=1, source_target_pairs={{0,64},{64,0},{128,192},{192,128},{256,320},{320,256},{384,448},{4... | collective-permute-start | bytes 2359304 | tf_op jit(solution)/shard_map/ppermute | solution.py:229
  77.3 0.0 collective-permute-done.10.refs_11_
  77.3 2.6 %collective-permute-start.13 = (bf16[2,1536,128]{2,1,0:T(8,128)(2,1)}, bf16[2,1536,128]{2,1,0:T(8,128)(2,1)}, u32[]{:S(2)}, u32[]{:S(2)}) collective-permute-start(bf16[2,1536,128]{2,1,0:T(8,128)(2,1)} %collective-permute-done.5.refs_6_), channel_id=1, source_target_pairs={{0,64},{64,0},{128,192},{192,128},{256,320},{320,256},{384,448},{4... | collective-permute-start | bytes 2359304 | tf_op jit(solution)/shard_map/ppermute | solution.py:229
  79.9 0.1 stack.93.base_ref
  80.1 0.0 collective-permute-done.9.refs_10_
  80.1 0.0 collective-permute-done.12.refs_13_
  80.1 0.0 collective-permute-done.14.refs_15_
  80.1 0.0 collective-permute-done.11.refs_12_
  80.1 1.8 %collective-permute-done.13.refs_14_ = bf16[2,1536,128]{2,1,0:T(8,128)(2,1)} collective-permute-done((bf16[2,1536,128]{2,1,0:T(8,128)(2,1)}, bf16[2,1536,128]{2,1,0:T(8,128)(2,1)}, u32[]{:S(2)}, u32[]{:S(2)}) %collective-permute-start.13) | collective-permute-done | bytes 786464 | tf_op jit(solution)/shard_map/ppermute | solution.py:229
  81.9 18.1 %shard_map.62 = (bf16[4,128,128]{2,1,0:T(8,128)(2,1)}, f32[4,4096]{1,0:T(4,128)S(1)}) custom-call(s32[32,27]{1,0:T(8,128)S(1)} %bitcast.28, s32[18]{0:T(128)S(1)} %stack.93.base_ref, bf16[2,1536,128]{2,1,0:T(8,128)(2,1)S(1)} %shard_map.60.refs_0_, bf16[2,1536,128]{2,1,0:T(8,128)(2,1)S(1)} %shard_map.61.refs_1_, ...), custom_call_target="tpu_custom_call" | custom-call | tf_op jit(solution)/shard_map/pallas_call | solution.py:166
  100.1 0.1 reshape.11
  100.2 0.1 copy.10
  100.3 0.1 reshape.12
  100.4 24.7 %all_to_all.10 = f32[64,1,256]{2,1,0:T(1,128)S(1)} all-to-all(f32[64,1,256]{2,1,0:T(1,128)S(1)} %reshape.12), channel_id=1, replica_groups=mesh['elem'=8,'band'=64] {'band'}, dimensions={0} | all-to-all | bytes 131072 | tf_op jit(solution)/shard_map/all_to_all | solution.py:268
  125.1 0.5 broadcast.12
  125.6 0.8 reduce
  126.4 0.1 reshape.13
  126.5 0.1 reduce_sum.9
  126.6 0.6 broadcast_multiply_fusion
  (6 shorter events, 0.0 us)
Async XLA Ops:
  0.6 23.4 %copy-start.4 = (s32[4,27]{1,0:T(4,128)S(1)}, s32[4,27]{1,0:T(4,128)}, u32[]{:S(2)}) copy-start(s32[4,27]{1,0:T(4,128)} %near_ref.3) | copy-start | bytes 1300
  1.4 0.9 copy-start.2
  3.2 30.2 %all-to-all-start = ((bf16[4,528,128]{2,1,0:T(8,128)(2,1)}), bf16[4,528,128]{2,1,0:T(8,128)(2,1)S(1)}, u32[]{:S(2)}, u32[]{:S(2)}) async-start(bf16[4,528,128]{2,1,0:T(8,128)(2,1)} %shard_map.59), calls=%async_computation | async-start | bytes 1081344 | tf_op jit(solution)/shard_map/all_to_all | solution.py:239
  11.0 2.0 %copy-start = (bf16[4,27,128,128]{3,2,1,0:T(8,128)(2,1)S(1)}, bf16[4,27,128,128]{3,2,1,0:T(8,128)(2,1)}, u32[]{:S(2)}) copy-start(bf16[4,27,128,128]{3,2,1,0:T(8,128)(2,1)} %h_ref.3) | copy-start | bytes 10616836
  13.0 0.7 copy-start.3
  13.7 10.3 %copy-start.1 = (bf16[4,27,128,128]{3,2,1,0:T(8,128)(2,1)S(1)}, bf16[4,27,128,128]{3,2,1,0:T(8,128)(2,1)}, u32[]{:S(2)}) copy-start(bf16[4,27,128,128]{3,2,1,0:T(8,128)(2,1)} %h_ref.3) | copy-start | bytes 10616836
  15.8 23.8 %collective-permute-start.2 = (bf16[2,1536,128]{2,1,0:T(8,128)(2,1)S(1)}, bf16[2,1536,128]{2,1,0:T(8,128)(2,1)S(1)}, u32[]{:S(2)}, u32[]{:S(2)}) collective-permute-start(bf16[2,1536,128]{2,1,0:T(8,128)(2,1)S(1)} %shard_map.61.refs_1_), channel_id=1, source_target_pairs={{0,388},{64,452},{128,0},{192,64},{256,128},{320,192},{384,256},{4... | collective-permute-start | bytes 2359304 | tf_op jit(solution)/shard_map/ppermute | solution.py:229
  26.1 20.7 %collective-permute-start.1 = (bf16[2,1536,128]{2,1,0:T(8,128)(2,1)S(1)}, bf16[2,1536,128]{2,1,0:T(8,128)(2,1)}, u32[]{:S(2)}, u32[]{:S(2)}) collective-permute-start(bf16[2,1536,128]{2,1,0:T(8,128)(2,1)S(1)} %shard_map.60.refs_0_), channel_id=1, source_target_pairs={{0,128},{64,192},{128,256},{192,320},{256,384},{320,448},{384,4},{... | collective-permute-start | bytes 2359304 | tf_op jit(solution)/shard_map/ppermute | solution.py:229
  28.0 22.0 %collective-permute-start.8 = (bf16[2,1536,128]{2,1,0:T(8,128)(2,1)S(1)}, bf16[2,1536,128]{2,1,0:T(8,128)(2,1)}, u32[]{:S(2)}, u32[]{:S(2)}) collective-permute-start(bf16[2,1536,128]{2,1,0:T(8,128)(2,1)S(1)} %shard_map.61.refs_1_), channel_id=1, source_target_pairs={{0,64},{64,0},{128,192},{192,128},{256,320},{320,256},{384,448},{4... | collective-permute-start | bytes 2359304 | tf_op jit(solution)/shard_map/ppermute | solution.py:229
  31.5 20.5 %collective-permute-start.7 = (bf16[2,1536,128]{2,1,0:T(8,128)(2,1)S(1)}, bf16[2,1536,128]{2,1,0:T(8,128)(2,1)}, u32[]{:S(2)}, u32[]{:S(2)}) collective-permute-start(bf16[2,1536,128]{2,1,0:T(8,128)(2,1)S(1)} %shard_map.60.refs_0_), channel_id=1, source_target_pairs={{0,64},{64,0},{128,192},{192,128},{256,320},{320,256},{384,448},{4... | collective-permute-start | bytes 2359304 | tf_op jit(solution)/shard_map/ppermute | solution.py:229
  33.4 21.7 %collective-permute-start = (bf16[4,528,128]{2,1,0:T(8,128)(2,1)S(1)}, bf16[4,528,128]{2,1,0:T(8,128)(2,1)S(1)}, u32[]{:S(2)}, u32[]{:S(2)}) collective-permute-start(bf16[4,528,128]{2,1,0:T(8,128)(2,1)S(1)} %all-to-all-done.refs_16_), channel_id=1, source_target_pairs={{0,64},{64,0},{128,192},{192,128},{256,320},{320,256},{384,448},{4... | collective-permute-start | bytes 1622024 | tf_op jit(solution)/shard_map/ppermute | solution.py:229
  39.6 20.6 %collective-permute-start.4 = (bf16[2,1536,128]{2,1,0:T(8,128)(2,1)S(1)}, bf16[2,1536,128]{2,1,0:T(8,128)(2,1)}, u32[]{:S(2)}, u32[]{:S(2)}) collective-permute-start(bf16[2,1536,128]{2,1,0:T(8,128)(2,1)S(1)} %collective-permute-done.2.refs_3_), channel_id=1, source_target_pairs={{0,388},{64,452},{128,0},{192,64},{256,128},{320,192},{384,256},{4... | collective-permute-start | bytes 2359304 | tf_op jit(solution)/shard_map/ppermute | solution.py:229
  46.8 18.6 %collective-permute-start.6 = (bf16[2,1536,128]{2,1,0:T(8,128)(2,1)S(1)}, bf16[2,1536,128]{2,1,0:T(8,128)(2,1)}, u32[]{:S(2)}, u32[]{:S(2)}) collective-permute-start(bf16[2,1536,128]{2,1,0:T(8,128)(2,1)S(1)} %collective-permute-done.2.refs_3_), channel_id=1, source_target_pairs={{0,8},{64,72},{128,136},{192,200},{256,264},{320,328},{384,392},{4... | collective-permute-start | bytes 2359304 | tf_op jit(solution)/shard_map/ppermute | solution.py:229
  50.0 20.6 %collective-permute-start.3 = (bf16[2,1536,128]{2,1,0:T(8,128)(2,1)}, bf16[2,1536,128]{2,1,0:T(8,128)(2,1)}, u32[]{:S(2)}, u32[]{:S(2)}) collective-permute-start(bf16[2,1536,128]{2,1,0:T(8,128)(2,1)} %collective-permute-done.1.refs_2_), channel_id=1, source_target_pairs={{0,128},{64,192},{128,256},{192,320},{256,384},{320,448},{384,4},{... | collective-permute-start | bytes 2359304 | tf_op jit(solution)/shard_map/ppermute | solution.py:229
  52.0 23.3 %collective-permute-start.5 = (bf16[2,1536,128]{2,1,0:T(8,128)(2,1)}, bf16[2,1536,128]{2,1,0:T(8,128)(2,1)}, u32[]{:S(2)}, u32[]{:S(2)}) collective-permute-start(bf16[2,1536,128]{2,1,0:T(8,128)(2,1)} %collective-permute-done.1.refs_2_), channel_id=1, source_target_pairs={{0,1},{64,65},{128,129},{192,193},{256,257},{320,321},{384,385},{4... | collective-permute-start | bytes 2359304 | tf_op jit(solution)/shard_map/ppermute | solution.py:229
  55.1 22.2 %collective-permute-start.10 = (bf16[2,1536,128]{2,1,0:T(8,128)(2,1)S(1)}, bf16[2,1536,128]{2,1,0:T(8,128)(2,1)}, u32[]{:S(2)}, u32[]{:S(2)}) collective-permute-start(bf16[2,1536,128]{2,1,0:T(8,128)(2,1)S(1)} %collective-permute-done.2.refs_3_), channel_id=1, source_target_pairs={{0,64},{64,0},{128,192},{192,128},{256,320},{320,256},{384,448},{4... | collective-permute-start | bytes 2359304 | tf_op jit(solution)/shard_map/ppermute | solution.py:229
  60.2 19.9 %collective-permute-start.9 = (bf16[2,1536,128]{2,1,0:T(8,128)(2,1)}, bf16[2,1536,128]{2,1,0:T(8,128)(2,1)}, u32[]{:S(2)}, u32[]{:S(2)}) collective-permute-start(bf16[2,1536,128]{2,1,0:T(8,128)(2,1)} %collective-permute-done.1.refs_2_), channel_id=1, source_target_pairs={{0,64},{64,0},{128,192},{192,128},{256,320},{320,256},{384,448},{4... | collective-permute-start | bytes 2359304 | tf_op jit(solution)/shard_map/ppermute | solution.py:229
  65.4 14.6 %collective-permute-start.12 = (bf16[2,1536,128]{2,1,0:T(8,128)(2,1)}, bf16[2,1536,128]{2,1,0:T(8,128)(2,1)}, u32[]{:S(2)}, u32[]{:S(2)}) collective-permute-start(bf16[2,1536,128]{2,1,0:T(8,128)(2,1)} %collective-permute-done.4.refs_5_), channel_id=1, source_target_pairs={{0,64},{64,0},{128,192},{192,128},{256,320},{320,256},{384,448},{4... | collective-permute-start | bytes 2359304 | tf_op jit(solution)/shard_map/ppermute | solution.py:229
  70.7 9.4 %collective-permute-start.14 = (bf16[2,1536,128]{2,1,0:T(8,128)(2,1)}, bf16[2,1536,128]{2,1,0:T(8,128)(2,1)}, u32[]{:S(2)}, u32[]{:S(2)}) collective-permute-start(bf16[2,1536,128]{2,1,0:T(8,128)(2,1)} %collective-permute-done.6.refs_7_), channel_id=1, source_target_pairs={{0,64},{64,0},{128,192},{192,128},{256,320},{320,256},{384,448},{4... | collective-permute-start | bytes 2359304 | tf_op jit(solution)/shard_map/ppermute | solution.py:229
  75.3 4.7 %collective-permute-start.11 = (bf16[2,1536,128]{2,1,0:T(8,128)(2,1)}, bf16[2,1536,128]{2,1,0:T(8,128)(2,1)}, u32[]{:S(2)}, u32[]{:S(2)}) collective-permute-start(bf16[2,1536,128]{2,1,0:T(8,128)(2,1)} %collective-permute-done.3.refs_4_), channel_id=1, source_target_pairs={{0,64},{64,0},{128,192},{192,128},{256,320},{320,256},{384,448},{4... | collective-permute-start | bytes 2359304 | tf_op jit(solution)/shard_map/ppermute | solution.py:229
  77.3 4.6 %collective-permute-start.13 = (bf16[2,1536,128]{2,1,0:T(8,128)(2,1)}, bf16[2,1536,128]{2,1,0:T(8,128)(2,1)}, u32[]{:S(2)}, u32[]{:S(2)}) collective-permute-start(bf16[2,1536,128]{2,1,0:T(8,128)(2,1)} %collective-permute-done.5.refs_6_), channel_id=1, source_target_pairs={{0,64},{64,0},{128,192},{192,128},{256,320},{320,256},{384,448},{4... | collective-permute-start | bytes 2359304 | tf_op jit(solution)/shard_map/ppermute | solution.py:229

commit v2 on v1

--- a/solution.py
+++ b/solution.py
@@ -20,50 +20,72 @@
 NT = (((1,), (1,)), ((), ()))
 
 
-def fold_kernel(pair_ref, near_ref, h_ref, out_ref):
-    e = 2 * pair_ref[0] + pl.program_id(0)
+def fold_kernel(pair_ref, near_ref, h0_ref, h1_ref, h2_ref, a_ref, b_ref):
+    step = pl.program_id(0)
+    e = lax.rem(2 * pair_ref[0] + step, 4)
     rows = lax.broadcasted_iota(jnp.int32, (NB, NB), 0)
     cols = lax.broadcasted_iota(jnp.int32, (NB, NB), 1)
     eye = (rows == cols).astype(F32).astype(BF)
     choices = ((1,), (0, 2))
-    for dx in range(3):
-        ids = [
-            near_ref[e, 9 * dx + 3 * b[0] + c[0]] for b in choices for c in choices
-        ]
-        spot = 0
-        for b in choices:
-            for c in choices:
-                total = None
-                for i in b:
-                    for j in c:
-                        part = lax.dot_general(
-                            eye, h_ref[0, 9 * dx + 3 * i + j], NT, preferred_element_type=F32
-                        )
-                        total = part if total is None else total + part
-                rank = jnp.int32(0)
-                for other in range(4):
-                    if other != spot:
-                        rank = rank + (ids[other] < ids[spot]).astype(jnp.int32)
-                row = pl.multiple_of((4 * dx + rank) * NB, NB)
-                out_ref[0, pl.ds(row, NB), :] = total.astype(BF)
-                spot += 1
+
+    def write(out_ref):
+        for dx, h_ref in enumerate((h0_ref, h1_ref, h2_ref)):
+            ids = [
+                near_ref[e, 9 * dx + 3 * b[0] + c[0]] for b in choices for c in choices
+            ]
+            spot = 0
+            for b in choices:
+                for c in choices:
+                    total = None
+                    for i in b:
+                        for j in c:
+                            part = h_ref[0, 3 * i + j].astype(F32)
+                            total = part if total is None else total + part
+                    turned = lax.dot_general(
+                        eye, total.astype(BF), NT, preferred_element_type=F32
+                    )
+                    rank = jnp.int32(0)
+                    for other in range(4):
+                        if other != spot:
+                            rank = rank + (ids[other] < ids[spot]).astype(jnp.int32)
+                    row = pl.multiple_of((4 * dx + rank) * NB, NB)
+                    out_ref[0, pl.ds(row, NB), :] = turned.astype(BF)
+                    spot += 1
+
+    @pl.when(step < 2)
+    def _():
+        write(a_ref)
+
+    @pl.when(step >= 2)
+    def _():
+        write(b_ref)
 
 
 def fold(hamiltonian, neighbours, pair):
+    shape = jax.ShapeDtypeStruct((2, KDIM, NB), BF)
     return pl.pallas_call(
         fold_kernel,
-        out_shape=jax.ShapeDtypeStruct((2, KDIM, NB), BF),
+        out_shape=(shape, shape),
         grid_spec=pltpu.PrefetchScalarGridSpec(
             num_scalar_prefetch=2,
-            grid=(2,),
+            grid=(4,),
             in_specs=[
-                pl.BlockSpec((1, 27, NB, NB), lambda t, pair, near: (2 * pair[0] + t, 0, 0, 0))
+                pl.BlockSpec(
+                    (1, 9, NB, NB),
+                    lambda t, pair, near, dx=dx: (lax.rem(2 * pair[0] + t, 4), dx, 0, 0),
+                )
+                for dx in range(3)
             ],
-            out_specs=pl.BlockSpec((1, KDIM, NB), lambda t, pair, near: (t, 0, 0)),
+            out_specs=(
+                pl.BlockSpec((1, KDIM, NB), lambda t, pair, near: (jnp.minimum(t, 1), 0, 0)),
+                pl.BlockSpec((1, KDIM, NB), lambda t, pair, near: (jnp.maximum(t - 2, 0), 0, 0)),
+            ),
         ),
-        compiler_params=pltpu.CompilerParams(vmem_limit_bytes=16 * 2**20),
-        cost_estimate=pl.CostEstimate(flops=2 * 27 * 2 * NB**3, bytes_accessed=2600000, transcendentals=0),
-    )(pair, neighbours, hamiltonian)
+        compiler_params=pltpu.CompilerParams(vmem_limit_bytes=60 * 2**20),
+        cost_estimate=pl.CostEstimate(
+            flops=4 * 27 * 2 * NB**3, bytes_accessed=5200000, transcendentals=0
+        ),
+    )(pair, neighbours, hamiltonian, hamiltonian, hamiltonian)
 
 
 def turn_kernel(y_ref, near_ref, out_ref):
@@ -83,11 +105,24 @@
     )(coefficients, near)
 
 
-def filter_kernel(near_ref, base_ref, *refs):
+def parity(band):
+    return (band % NX + band // (2 * NX)) % 2
+
+
+def piece_bases(lo, core, pa):
+    pb = 1 - pa
+    order = [(0, pa), (0, pb), (3, pa), (1, pb), (2, pa), (2, pb), (3, pb), (1, pa)]
+    return [(((lo + z) % 4) * 2 + core) * 4 + 2 * pair for z, pair in order]
+
+
+def filter_kernel(near_ref, *refs):
     h_refs = refs[:16]
     y_own, y_other, b_ref, filt_ref, dens_ref = refs[16:21]
     hbuf, ybuf, za, zb, bbuf, pid, slot, h_sems, b_sem = refs[21:]
-    core = base_ref[16]
+    elem, band = lax.axis_index("elem"), lax.axis_index("band")
+    lo, core = elem // 2, elem % 2
+    pa = parity(band)
+    bases = piece_bases(lo, core, pa) + piece_bases(lo, 1 - core, pa)
 
     rep = jnp.int32(0)
     for x in range(PLANES):
@@ -111,9 +146,7 @@
 
     for i, ref in enumerate(h_refs):
         for k in range(2):
-            h_copy(ref, k, base_ref[i] + k).start()
-    b_copy = pltpu.make_async_copy(b_ref, bbuf, b_sem)
-    b_copy.start()
+            h_copy(ref, k, bases[i] + k).start()
 
     for source, side in ((y_own, core), (y_other, 1 - core)):
         for z in range(4):
@@ -128,7 +161,10 @@
             [ybuf[src, (x + 7) % 8], ybuf[src, x], ybuf[src, (x + 1) % 8]], axis=1
         )
 
+    b_copy = pltpu.make_async_copy(b_ref, bbuf, b_sem)
     for step in range(5):
+        if step == 1:
+            b_copy.start()
         src, dst = step % 2, 1 - step % 2
         past = zb if step % 2 == 0 else za
         for x in range(PLANES):
@@ -143,7 +179,7 @@
             ybuf[dst, x] = new.astype(BF)
 
     b_copy.wait()
-    mine = base_ref[17]
+    mine = elem * 4
     for e in range(4):
         x, lane, _ = place(mine + e)
         left = lax.rem(x + 7, 8)
@@ -159,8 +195,9 @@
             dens_ref[e : e + 1, p : p + 512] = jnp.sum(phi * phi, axis=0, keepdims=True)
 
 
-def filtering(near, base, pieces, y_own, y_other, basis_values):
+def filtering(near, pieces, y_own, y_other, basis_values):
     anywhere = pl.BlockSpec(memory_space=pl.ANY)
+    hbm = pl.BlockSpec(memory_space=pltpu.HBM)
     smem = pl.BlockSpec(memory_space=pltpu.SMEM)
     vmem = pl.BlockSpec(memory_space=pltpu.VMEM)
     return pl.pallas_call(
@@ -169,7 +206,7 @@
             jax.ShapeDtypeStruct((4, NB, NB), BF),
             jax.ShapeDtypeStruct((4, POINTS), F32),
         ),
-        in_specs=[smem, smem] + [anywhere] * 16 + [vmem, vmem, anywhere],
+        in_specs=[smem, hbm, hbm] + [anywhere] * 14 + [vmem, vmem, anywhere],
         out_specs=(vmem, vmem),
         scratch_shapes=[
             pltpu.VMEM((PLANES, KDIM, WIDE), BF),
@@ -182,8 +219,8 @@
             pltpu.SemaphoreType.DMA((32,)),
             pltpu.SemaphoreType.DMA,
         ],
-        compiler_params=pltpu.CompilerParams(vmem_limit_bytes=48 * 2**20),
-    )(near, base, *pieces, y_own, y_other, basis_values)
+        compiler_params=pltpu.CompilerParams(vmem_limit_bytes=40 * 2**20),
+    )(near, *pieces, y_own, y_other, basis_values)
 
 
 def routes(nbands):
@@ -219,43 +256,38 @@
 def local(nbands, coefficients, hamiltonian, neighbours, basis_values):
     both = ("elem", "band")
     up, down, over_x, over_y, over_core = routes(nbands)
-    elem = lax.axis_index("elem")
-    band = lax.axis_index("band")
-    lo, core = elem // 2, elem % 2
-    pa = (band % NX + band // (2 * NX)) % 2
-    pb = 1 - pa
+    core = lax.axis_index("elem") % 2
+    pa = parity(lax.axis_index("band"))
 
     def move(value, pairs):
         return lax.ppermute(value, both, pairs)
 
-    own_a = fold(hamiltonian, neighbours, pa[None])
-    own_b = fold(hamiltonian, neighbours, pb[None])
+    own_a, own_b = fold(hamiltonian, neighbours, pa[None])
     from_below = move(own_a, up)
     from_above = move(own_b, down)
 
+    coefficients, neighbours, own_b = lax.optimization_barrier(
+        (coefficients, neighbours, own_b)
+    )
     near = jnp.pad(neighbours.astype(BF), ((0, EDGE - 4), (0, NB - 27)))
     turned = turn(coefficients, near)
     groups = [[2 * z + c for z in range(4)] for c in range(2)]
     y_own = lax.all_to_all(turned, "elem", 0, 0, axis_index_groups=groups)
     y_other = move(y_own, over_core)
 
+    own_swapped = [move(own_a, over_core), move(own_b, over_core)]
+    from_below, from_above, y_other, own_swapped = lax.optimization_barrier(
+        (from_below, from_above, y_other, own_swapped)
+    )
     far_a = move(from_below, up)
     far_b = move(from_above, down)
-    below_b = move(from_below, over_x)
-    above_a = move(from_above, over_y)
-
-    pieces = [own_a, own_b, from_below, from_above, far_a, far_b, below_b, above_a]
-    swapped = [move(piece, over_core) for piece in pieces]
-
-    def first(z, c, pair):
-        return (((lo + z) % 4) * 2 + c) * 4 + 2 * pair
-
-    order = [(0, pa), (0, pb), (3, pa), (1, pb), (2, pa), (2, pb), (3, pb), (1, pa)]
-    base = jnp.stack(
-        [first(z, core, pair) for z, pair in order]
-        + [first(z, 1 - core, pair) for z, pair in order]
-        + [core, elem * 4]
-    ).astype(jnp.int32)
+    next_swapped = [move(from_below, over_core), move(from_above, over_core)]
+    for_x, for_y, next_swapped = lax.optimization_barrier(
+        (from_below, from_above, next_swapped)
+    )
+    below_b = move(for_x, over_x)
+    above_a = move(for_y, over_y)
+
 
     def table(y):
         return y[:, 4 * NB : 4 * NB + 4, :27].astype(jnp.int32)
@@ -263,7 +295,11 @@
     ids = jnp.stack([table(y_own), table(y_other)], axis=1)
     ids = jnp.where(core == 0, ids, ids[:, ::-1]).reshape(32, 27)
 
-    filtered, partial = filtering(ids, base, pieces + swapped, y_own, y_other, basis_values)
+    ids, below_b = lax.optimization_barrier((ids, below_b))
+    pieces = [own_a, own_b, from_below, from_above, far_a, far_b, below_b, above_a]
+    swapped = own_swapped + next_swapped + [move(piece, over_core) for piece in pieces[4:]]
+
+    filtered, partial = filtering(ids, pieces + swapped, y_own, y_other, basis_values)
     parts = partial.reshape(4, nbands, POINTS // nbands).swapaxes(0, 1)
     density = jnp.sum(lax.all_to_all(parts, "band", 0, 0), axis=0) / BANDS
     return filtered, density

time: 129 us -> 136 us (1.054)
  waiting for transfers between devices: 8.43 us -> 22.1 us
  starting transfers between devices: 62.9 us -> 56.6 us
  blocking collectives: 24.7 us -> 27.6 us
  local copies, waits for them, and re-layouts: 4.69 us -> 3.27 us
    ppermute x15, waiting for transfers between devices: 8.43 us -> 22.1 us  [move(): return lax.ppermute(value, both, pairs)]
    ppermute x15, starting transfers between devices: 55.1 us -> 48.8 us  [move(): return lax.ppermute(value, both, pairs)]
    all_to_all x1, blocking collectives: 24.7 us -> 27.6 us  [local(): density = jnp.sum(lax.all_to_all(parts, 'band', 0, 0), axis=0) / BANDS]
    pallas_call x2 -> x1, Pallas kernels: 4.14 us -> 5.66 us  [fold(): pl.pallas_call(fold_kernel, out_shape=(shape, shape), grid_spec=pltpu.Pre...]
    pallas_call x1, Pallas kernels: 18.1 us -> 16.6 us  [filtering(): pl.pallas_call(filter_kernel, out_shape=(jax.ShapeDtypeStruct((4, NB, NB)...]
    unnamed x12 -> x10, local copies, waits for them, and re-layouts: 3.84 us -> 2.52 us
  transfers between devices with their start and end apart: 16 -> 16, of which waited for: 4 -> 4; matrix products, arithmetic and copies ran while one was open for 0% -> 0% of each run, Pallas kernels for 3% -> 0%
where the time goes in v2:
time: 136 us; the launch traced here: 135 us
  starting transfers between devices  56.6 us (42%)
  blocking collectives  27.6 us (20%)
  Pallas kernels  23.2 us (17%)
  waiting for transfers between devices  22.1 us (16%)
  local copies, waits for them, and re-layouts  3.27 us (2%)
  other arithmetic  1.49 us (1%)
    ppermute x15, starting transfers between devices, move(): return lax.ppermute(value, both, pairs)  48.8 us
    all_to_all x1, blocking collectives, local(): density = jnp.sum(lax.all_to_all(parts, 'band', 0, 0), axis=0) / BANDS  27.6 us
    ppermute x15, waiting for transfers between devices, move(): return lax.ppermute(value, both, pairs)  22.1 us
    pallas_call x1, Pallas kernels, filtering(): pl.pallas_call(filter_kernel, out_shape=(jax.ShapeDtypeStruct((4, NB, NB)...  16.6 us
    all_to_all x1, starting transfers between devices, local(): y_own = lax.all_to_all(turned, 'elem', 0, 0, axis_index_groups=groups)  7.81 us
    pallas_call x1, Pallas kernels, fold(): pl.pallas_call(fold_kernel, out_shape=(shape, shape), grid_spec=pltpu.Pre...  5.66 us
  transfers between devices with their start and end apart: 16, of which 4 were waited for; matrix products, arithmetic and copies ran while one was open for 0% of the time, Pallas kernels for 0%

profile of v2, /device:TPU:1, one launch (start us, length us, event | category | flops | bytes accessed | tf_op | source)
XLA Modules:
  0.0 135.1 jit_solution(3426207574296130464)
XLA Ops:
  0.7 0.0 copy-start.3
  0.7 0.0 copy-start.2
  0.7 5.7 %shard_map.59 = (bf16[2,1536,128]{2,1,0:T(8,128)(2,1)}, bf16[2,1536,128]{2,1,0:T(8,128)(2,1)}) custom-call(s32[1]{0:T(128)} %bitcast.pair_ref, s32[4,27]{1,0:T(4,128)} %near_ref.1, bf16[4,27,128,128]{3,2,1,0:T(8,128)(2,1)} %h2_ref.1, bf16[4,27,128,128]{3,2,1,0:T(8,128)(2,1)} %h2_ref.1, bf16[4,27,128,128]{3,2,1,0:T(8,128)(2,1)} %h2_ref.1), custom_call_target="tpu_custom_call" | custom-call | flops 452984832 | bytes 5200000 | tf_op jit(solution)/shard_map/pallas_call | solution.py:66
  6.4 0.0 copy-done.3
  6.4 0.0 copy-done.2
  6.4 0.9 shard_map.60
  7.3 7.8 %all-to-all-start = ((bf16[4,528,128]{2,1,0:T(8,128)(2,1)}), bf16[4,528,128]{2,1,0:T(8,128)(2,1)S(1)}, u32[]{:S(2)}, u32[]{:S(2)}) async-start(bf16[4,528,128]{2,1,0:T(8,128)(2,1)} %shard_map.60), calls=%async_computation | async-start | bytes 1081344 | tf_op jit(solution)/shard_map/all_to_all | solution.py:275
  15.1 4.5 %collective-permute-start.4 = (bf16[2,1536,128]{2,1,0:T(8,128)(2,1)}, bf16[2,1536,128]{2,1,0:T(8,128)(2,1)S(1)}, u32[]{:S(2)}, u32[]{:S(2)}) collective-permute-start(bf16[2,1536,128]{2,1,0:T(8,128)(2,1)} %get-tuple-element.24.refs_1_), channel_id=1, source_target_pairs={{0,64},{64,0},{128,192},{192,128},{256,320},{320,256},{384,448},{4... | collective-permute-start | bytes 2359304 | tf_op jit(solution)/shard_map/ppermute | solution.py:263
  19.6 3.6 %collective-permute-start = (bf16[2,1536,128]{2,1,0:T(8,128)(2,1)}, bf16[2,1536,128]{2,1,0:T(8,128)(2,1)S(1)}, u32[]{:S(2)}, u32[]{:S(2)}) collective-permute-start(bf16[2,1536,128]{2,1,0:T(8,128)(2,1)} %get-tuple-element.23.refs_0_), channel_id=1, source_target_pairs={{0,128},{64,192},{128,256},{192,320},{256,384},{320,448},{384,4},{... | collective-permute-start | bytes 2359304 | tf_op jit(solution)/shard_map/ppermute | solution.py:263
  23.2 5.2 %collective-permute-start.1 = (bf16[2,1536,128]{2,1,0:T(8,128)(2,1)}, bf16[2,1536,128]{2,1,0:T(8,128)(2,1)S(1)}, u32[]{:S(2)}, u32[]{:S(2)}) collective-permute-start(bf16[2,1536,128]{2,1,0:T(8,128)(2,1)} %get-tuple-element.24.refs_1_), channel_id=1, source_target_pairs={{0,388},{64,452},{128,0},{192,64},{256,128},{320,192},{384,256},{4... | collective-permute-start | bytes 2359304 | tf_op jit(solution)/shard_map/ppermute | solution.py:263
  28.4 2.2 %collective-permute-start.3 = (bf16[2,1536,128]{2,1,0:T(8,128)(2,1)}, bf16[2,1536,128]{2,1,0:T(8,128)(2,1)}, u32[]{:S(2)}, u32[]{:S(2)}) collective-permute-start(bf16[2,1536,128]{2,1,0:T(8,128)(2,1)} %get-tuple-element.23.refs_0_), channel_id=1, source_target_pairs={{0,64},{64,0},{128,192},{192,128},{256,320},{320,256},{384,448},{4... | collective-permute-start | bytes 2359304 | tf_op jit(solution)/shard_map/ppermute | solution.py:263
  30.6 0.0 all-to-all-done.refs_16_
  30.6 3.8 %collective-permute-start.2 = (bf16[4,528,128]{2,1,0:T(8,128)(2,1)S(1)}, bf16[4,528,128]{2,1,0:T(8,128)(2,1)S(1)}, u32[]{:S(2)}, u32[]{:S(2)}) collective-permute-start(bf16[4,528,128]{2,1,0:T(8,128)(2,1)S(1)} %all-to-all-done.refs_16_), channel_id=1, source_target_pairs={{0,64},{64,0},{128,192},{192,128},{256,320},{320,256},{384,448},{4... | collective-permute-start | bytes 1622024 | tf_op jit(solution)/shard_map/ppermute | solution.py:263
  34.4 0.0 collective-permute-done.4.refs_9_
  34.4 10.2 %collective-permute-done.refs_2_ = bf16[2,1536,128]{2,1,0:T(8,128)(2,1)S(1)} collective-permute-done((bf16[2,1536,128]{2,1,0:T(8,128)(2,1)}, bf16[2,1536,128]{2,1,0:T(8,128)(2,1)S(1)}, u32[]{:S(2)}, u32[]{:S(2)}) %collective-permute-start) | collective-permute-done | bytes 786464 | tf_op jit(solution)/shard_map/ppermute | solution.py:263
  44.6 1.1 collective-permute-done.1.refs_3_
  45.7 0.0 collective-permute-done.3.refs_8_
  45.7 0.0 collective-permute-done.2.refs_17_
  45.7 3.0 %collective-permute-start.5 = (bf16[2,1536,128]{2,1,0:T(8,128)(2,1)S(1)}, bf16[2,1536,128]{2,1,0:T(8,128)(2,1)}, u32[]{:S(2)}, u32[]{:S(2)}) collective-permute-start(bf16[2,1536,128]{2,1,0:T(8,128)(2,1)S(1)} %collective-permute-done.refs_2_), channel_id=1, source_target_pairs={{0,64},{64,0},{128,192},{192,128},{256,320},{320,256},{384,448},{4... | collective-permute-start | bytes 2359304 | tf_op jit(solution)/shard_map/ppermute | solution.py:263
  48.7 1.9 %collective-permute-start.6 = (bf16[2,1536,128]{2,1,0:T(8,128)(2,1)S(1)}, bf16[2,1536,128]{2,1,0:T(8,128)(2,1)}, u32[]{:S(2)}, u32[]{:S(2)}) collective-permute-start(bf16[2,1536,128]{2,1,0:T(8,128)(2,1)S(1)} %collective-permute-done.1.refs_3_), channel_id=1, source_target_pairs={{0,64},{64,0},{128,192},{192,128},{256,320},{320,256},{384,448},{4... | collective-permute-start | bytes 2359304 | tf_op jit(solution)/shard_map/ppermute | solution.py:263
  50.7 3.1 %collective-permute-start.8 = (bf16[2,1536,128]{2,1,0:T(8,128)(2,1)S(1)}, bf16[2,1536,128]{2,1,0:T(8,128)(2,1)S(1)}, u32[]{:S(2)}, u32[]{:S(2)}) collective-permute-start(bf16[2,1536,128]{2,1,0:T(8,128)(2,1)S(1)} %collective-permute-done.refs_2_), channel_id=1, source_target_pairs={{0,128},{64,192},{128,256},{192,320},{256,384},{320,448},{384,4},{... | collective-permute-start | bytes 2359304 | tf_op jit(solution)/shard_map/ppermute | solution.py:263
  53.8 3.6 %collective-permute-start.9 = (bf16[2,1536,128]{2,1,0:T(8,128)(2,1)S(1)}, bf16[2,1536,128]{2,1,0:T(8,128)(2,1)S(1)}, u32[]{:S(2)}, u32[]{:S(2)}) collective-permute-start(bf16[2,1536,128]{2,1,0:T(8,128)(2,1)S(1)} %collective-permute-done.1.refs_3_), channel_id=1, source_target_pairs={{0,388},{64,452},{128,0},{192,64},{256,128},{320,192},{384,256},{4... | collective-permute-start | bytes 2359304 | tf_op jit(solution)/shard_map/ppermute | solution.py:263
  57.5 0.0 collective-permute-done.5.refs_10_
  57.5 0.0 collective-permute-done.6.refs_11_
  57.5 3.1 %collective-permute-start.7 = (bf16[2,1536,128]{2,1,0:T(8,128)(2,1)S(1)}, bf16[2,1536,128]{2,1,0:T(8,128)(2,1)S(1)}, u32[]{:S(2)}, u32[]{:S(2)}) collective-permute-start(bf16[2,1536,128]{2,1,0:T(8,128)(2,1)S(1)} %collective-permute-done.refs_2_), channel_id=1, source_target_pairs={{0,1},{64,65},{128,129},{192,193},{256,257},{320,321},{384,385},{4... | collective-permute-start | bytes 2359304 | tf_op jit(solution)/shard_map/ppermute | solution.py:263
  60.6 3.2 %collective-permute-start.10 = (bf16[2,1536,128]{2,1,0:T(8,128)(2,1)S(1)}, bf16[2,1536,128]{2,1,0:T(8,128)(2,1)S(1)}, u32[]{:S(2)}, u32[]{:S(2)}) collective-permute-start(bf16[2,1536,128]{2,1,0:T(8,128)(2,1)S(1)} %collective-permute-done.1.refs_3_), channel_id=1, source_target_pairs={{0,8},{64,72},{128,136},{192,200},{256,264},{320,328},{384,392},{4... | collective-permute-start | bytes 2359304 | tf_op jit(solution)/shard_map/ppermute | solution.py:263
  63.9 9.1 %collective-permute-done.8.refs_4_ = bf16[2,1536,128]{2,1,0:T(8,128)(2,1)S(1)} collective-permute-done((bf16[2,1536,128]{2,1,0:T(8,128)(2,1)S(1)}, bf16[2,1536,128]{2,1,0:T(8,128)(2,1)S(1)}, u32[]{:S(2)}, u32[]{:S(2)}) %collective-permute-start.8) | collective-permute-done | bytes 786464 | tf_op jit(solution)/shard_map/ppermute | solution.py:263
  73.0 2.9 %collective-permute-start.11 = (bf16[2,1536,128]{2,1,0:T(8,128)(2,1)S(1)}, bf16[2,1536,128]{2,1,0:T(8,128)(2,1)S(1)}, u32[]{:S(2)}, u32[]{:S(2)}) collective-permute-start(bf16[2,1536,128]{2,1,0:T(8,128)(2,1)S(1)} %collective-permute-done.8.refs_4_), channel_id=1, source_target_pairs={{0,64},{64,0},{128,192},{192,128},{256,320},{320,256},{384,448},{4... | collective-permute-start | bytes 2359304 | tf_op jit(solution)/shard_map/ppermute | solution.py:263
  75.9 0.0 collective-permute-done.9.refs_5_
  75.9 1.9 %collective-permute-start.12 = (bf16[2,1536,128]{2,1,0:T(8,128)(2,1)S(1)}, bf16[2,1536,128]{2,1,0:T(8,128)(2,1)S(1)}, u32[]{:S(2)}, u32[]{:S(2)}) collective-permute-start(bf16[2,1536,128]{2,1,0:T(8,128)(2,1)S(1)} %collective-permute-done.9.refs_5_), channel_id=1, source_target_pairs={{0,64},{64,0},{128,192},{192,128},{256,320},{320,256},{384,448},{4... | collective-permute-start | bytes 2359304 | tf_op jit(solution)/shard_map/ppermute | solution.py:263
  77.9 0.0 collective-permute-done.7.refs_6_
  77.9 3.4 %collective-permute-start.13 = (bf16[2,1536,128]{2,1,0:T(8,128)(2,1)S(1)}, bf16[2,1536,128]{2,1,0:T(8,128)(2,1)S(1)}, u32[]{:S(2)}, u32[]{:S(2)}) collective-permute-start(bf16[2,1536,128]{2,1,0:T(8,128)(2,1)S(1)} %collective-permute-done.7.refs_6_), channel_id=1, source_target_pairs={{0,64},{64,0},{128,192},{192,128},{256,320},{320,256},{384,448},{4... | collective-permute-start | bytes 2359304 | tf_op jit(solution)/shard_map/ppermute | solution.py:263
  81.2 0.0 collective-permute-done.10.refs_7_
  81.2 3.3 %collective-permute-start.14 = (bf16[2,1536,128]{2,1,0:T(8,128)(2,1)S(1)}, bf16[2,1536,128]{2,1,0:T(8,128)(2,1)S(1)}, u32[]{:S(2)}, u32[]{:S(2)}) collective-permute-start(bf16[2,1536,128]{2,1,0:T(8,128)(2,1)S(1)} %collective-permute-done.10.refs_7_), channel_id=1, source_target_pairs={{0,64},{64,0},{128,192},{192,128},{256,320},{320,256},{384,448},{4... | collective-permute-start | bytes 2359304 | tf_op jit(solution)/shard_map/ppermute | solution.py:263
  84.5 0.0 collective-permute-done.11.refs_12_
  84.6 0.0 collective-permute-done.12.refs_13_
  84.6 0.0 collective-permute-done.13.refs_14_
  84.6 1.7 %collective-permute-done.14.refs_15_ = bf16[2,1536,128]{2,1,0:T(8,128)(2,1)S(1)} collective-permute-done((bf16[2,1536,128]{2,1,0:T(8,128)(2,1)S(1)}, bf16[2,1536,128]{2,1,0:T(8,128)(2,1)S(1)}, u32[]{:S(2)}, u32[]{:S(2)}) %collective-permute-start.14) | collective-permute-done | bytes 786464 | tf_op jit(solution)/shard_map/ppermute | solution.py:263
  86.3 0.0 copy-start
  86.3 1.1 copy-done
  87.4 0.0 copy-start.1
  87.4 1.1 copy-done.1
  88.5 16.6 %shard_map.61 = (bf16[4,128,128]{2,1,0:T(8,128)(2,1)}, f32[4,4096]{1,0:T(4,128)S(1)}) custom-call(s32[32,27]{1,0:T(8,128)S(1)} %bitcast.9, bf16[2,1536,128]{2,1,0:T(8,128)(2,1)S(1)} %copy-done, bf16[2,1536,128]{2,1,0:T(8,128)(2,1)S(1)} %copy-done.1, bf16[2,1536,128]{2,1,0:T(8,128)(2,1)S(1)} %collective-permute-done.refs_2_, ...), custom_call_target="tpu_custom_call" | custom-call | tf_op jit(solution)/shard_map/pallas_call | solution.py:203
  105.1 0.1 reshape.11
  105.2 0.1 copy.10
  105.3 0.1 reshape.12
  105.5 27.6 %all_to_all.10 = f32[64,1,256]{2,1,0:T(1,128)S(1)} all-to-all(f32[64,1,256]{2,1,0:T(1,128)S(1)} %reshape.12), channel_id=1, replica_groups=mesh['elem'=8,'band'=64] {'band'}, dimensions={0} | all-to-all | bytes 131072 | tf_op jit(solution)/shard_map/all_to_all | solution.py:304
  133.0 0.5 broadcast.7
  133.5 0.8 reduce
  134.4 0.1 reshape.13
  134.5 0.1 reduce_sum.9
  134.5 0.6 broadcast_multiply_fusion
  (7 shorter events, 0.0 us)
Async XLA Ops:
  0.7 5.7 %copy-start.3 = (s32[4,27]{1,0:T(4,128)S(1)}, s32[4,27]{1,0:T(4,128)}, u32[]{:S(2)}) copy-start(s32[4,27]{1,0:T(4,128)} %near_ref.1) | copy-start | bytes 1300
  0.7 5.7 %copy-start.2 = (bf16[4,128,128]{2,1,0:T(8,128)(2,1)S(1)}, bf16[4,128,128]{2,1,0:T(8,128)(2,1)}, u32[]{:S(2)}) copy-start(bf16[4,128,128]{2,1,0:T(8,128)(2,1)} %y_ref) | copy-start | bytes 393220
  7.3 23.3 %all-to-all-start = ((bf16[4,528,128]{2,1,0:T(8,128)(2,1)}), bf16[4,528,128]{2,1,0:T(8,128)(2,1)S(1)}, u32[]{:S(2)}, u32[]{:S(2)}) async-start(bf16[4,528,128]{2,1,0:T(8,128)(2,1)} %shard_map.60), calls=%async_computation | async-start | bytes 1081344 | tf_op jit(solution)/shard_map/all_to_all | solution.py:275
  15.1 19.3 %collective-permute-start.4 = (bf16[2,1536,128]{2,1,0:T(8,128)(2,1)}, bf16[2,1536,128]{2,1,0:T(8,128)(2,1)S(1)}, u32[]{:S(2)}, u32[]{:S(2)}) collective-permute-start(bf16[2,1536,128]{2,1,0:T(8,128)(2,1)} %get-tuple-element.24.refs_1_), channel_id=1, source_target_pairs={{0,64},{64,0},{128,192},{192,128},{256,320},{320,256},{384,448},{4... | collective-permute-start | bytes 2359304 | tf_op jit(solution)/shard_map/ppermute | solution.py:263
  19.6 25.0 %collective-permute-start = (bf16[2,1536,128]{2,1,0:T(8,128)(2,1)}, bf16[2,1536,128]{2,1,0:T(8,128)(2,1)S(1)}, u32[]{:S(2)}, u32[]{:S(2)}) collective-permute-start(bf16[2,1536,128]{2,1,0:T(8,128)(2,1)} %get-tuple-element.23.refs_0_), channel_id=1, source_target_pairs={{0,128},{64,192},{128,256},{192,320},{256,384},{320,448},{384,4},{... | collective-permute-start | bytes 2359304 | tf_op jit(solution)/shard_map/ppermute | solution.py:263
  23.2 22.5 %collective-permute-start.1 = (bf16[2,1536,128]{2,1,0:T(8,128)(2,1)}, bf16[2,1536,128]{2,1,0:T(8,128)(2,1)S(1)}, u32[]{:S(2)}, u32[]{:S(2)}) collective-permute-start(bf16[2,1536,128]{2,1,0:T(8,128)(2,1)} %get-tuple-element.24.refs_1_), channel_id=1, source_target_pairs={{0,388},{64,452},{128,0},{192,64},{256,128},{320,192},{384,256},{4... | collective-permute-start | bytes 2359304 | tf_op jit(solution)/shard_map/ppermute | solution.py:263
  28.4 17.3 %collective-permute-start.3 = (bf16[2,1536,128]{2,1,0:T(8,128)(2,1)}, bf16[2,1536,128]{2,1,0:T(8,128)(2,1)}, u32[]{:S(2)}, u32[]{:S(2)}) collective-permute-start(bf16[2,1536,128]{2,1,0:T(8,128)(2,1)} %get-tuple-element.23.refs_0_), channel_id=1, source_target_pairs={{0,64},{64,0},{128,192},{192,128},{256,320},{320,256},{384,448},{4... | collective-permute-start | bytes 2359304 | tf_op jit(solution)/shard_map/ppermute | solution.py:263
  30.6 15.1 %collective-permute-start.2 = (bf16[4,528,128]{2,1,0:T(8,128)(2,1)S(1)}, bf16[4,528,128]{2,1,0:T(8,128)(2,1)S(1)}, u32[]{:S(2)}, u32[]{:S(2)}) collective-permute-start(bf16[4,528,128]{2,1,0:T(8,128)(2,1)S(1)} %all-to-all-done.refs_16_), channel_id=1, source_target_pairs={{0,64},{64,0},{128,192},{192,128},{256,320},{320,256},{384,448},{4... | collective-permute-start | bytes 1622024 | tf_op jit(solution)/shard_map/ppermute | solution.py:263
  45.7 11.7 %collective-permute-start.5 = (bf16[2,1536,128]{2,1,0:T(8,128)(2,1)S(1)}, bf16[2,1536,128]{2,1,0:T(8,128)(2,1)}, u32[]{:S(2)}, u32[]{:S(2)}) collective-permute-start(bf16[2,1536,128]{2,1,0:T(8,128)(2,1)S(1)} %collective-permute-done.refs_2_), channel_id=1, source_target_pairs={{0,64},{64,0},{128,192},{192,128},{256,320},{320,256},{384,448},{4... | collective-permute-start | bytes 2359304 | tf_op jit(solution)/shard_map/ppermute | solution.py:263
  48.7 8.8 %collective-permute-start.6 = (bf16[2,1536,128]{2,1,0:T(8,128)(2,1)S(1)}, bf16[2,1536,128]{2,1,0:T(8,128)(2,1)}, u32[]{:S(2)}, u32[]{:S(2)}) collective-permute-start(bf16[2,1536,128]{2,1,0:T(8,128)(2,1)S(1)} %collective-permute-done.1.refs_3_), channel_id=1, source_target_pairs={{0,64},{64,0},{128,192},{192,128},{256,320},{320,256},{384,448},{4... | collective-permute-start | bytes 2359304 | tf_op jit(solution)/shard_map/ppermute | solution.py:263
  50.7 22.3 %collective-permute-start.8 = (bf16[2,1536,128]{2,1,0:T(8,128)(2,1)S(1)}, bf16[2,1536,128]{2,1,0:T(8,128)(2,1)S(1)}, u32[]{:S(2)}, u32[]{:S(2)}) collective-permute-start(bf16[2,1536,128]{2,1,0:T(8,128)(2,1)S(1)} %collective-permute-done.refs_2_), channel_id=1, source_target_pairs={{0,128},{64,192},{128,256},{192,320},{256,384},{320,448},{384,4},{... | collective-permute-start | bytes 2359304 | tf_op jit(solution)/shard_map/ppermute | solution.py:263
  53.8 22.1 %collective-permute-start.9 = (bf16[2,1536,128]{2,1,0:T(8,128)(2,1)S(1)}, bf16[2,1536,128]{2,1,0:T(8,128)(2,1)S(1)}, u32[]{:S(2)}, u32[]{:S(2)}) collective-permute-start(bf16[2,1536,128]{2,1,0:T(8,128)(2,1)S(1)} %collective-permute-done.1.refs_3_), channel_id=1, source_target_pairs={{0,388},{64,452},{128,0},{192,64},{256,128},{320,192},{384,256},{4... | collective-permute-start | bytes 2359304 | tf_op jit(solution)/shard_map/ppermute | solution.py:263
  57.5 20.4 %collective-permute-start.7 = (bf16[2,1536,128]{2,1,0:T(8,128)(2,1)S(1)}, bf16[2,1536,128]{2,1,0:T(8,128)(2,1)S(1)}, u32[]{:S(2)}, u32[]{:S(2)}) collective-permute-start(bf16[2,1536,128]{2,1,0:T(8,128)(2,1)S(1)} %collective-permute-done.refs_2_), channel_id=1, source_target_pairs={{0,1},{64,65},{128,129},{192,193},{256,257},{320,321},{384,385},{4... | collective-permute-start | bytes 2359304 | tf_op jit(solution)/shard_map/ppermute | solution.py:263
  60.6 20.6 %collective-permute-start.10 = (bf16[2,1536,128]{2,1,0:T(8,128)(2,1)S(1)}, bf16[2,1536,128]{2,1,0:T(8,128)(2,1)S(1)}, u32[]{:S(2)}, u32[]{:S(2)}) collective-permute-start(bf16[2,1536,128]{2,1,0:T(8,128)(2,1)S(1)} %collective-permute-done.1.refs_3_), channel_id=1, source_target_pairs={{0,8},{64,72},{128,136},{192,200},{256,264},{320,328},{384,392},{4... | collective-permute-start | bytes 2359304 | tf_op jit(solution)/shard_map/ppermute | solution.py:263
  73.0 11.6 %collective-permute-start.11 = (bf16[2,1536,128]{2,1,0:T(8,128)(2,1)S(1)}, bf16[2,1536,128]{2,1,0:T(8,128)(2,1)S(1)}, u32[]{:S(2)}, u32[]{:S(2)}) collective-permute-start(bf16[2,1536,128]{2,1,0:T(8,128)(2,1)S(1)} %collective-permute-done.8.refs_4_), channel_id=1, source_target_pairs={{0,64},{64,0},{128,192},{192,128},{256,320},{320,256},{384,448},{4... | collective-permute-start | bytes 2359304 | tf_op jit(solution)/shard_map/ppermute | solution.py:263
  75.9 8.6 %collective-permute-start.12 = (bf16[2,1536,128]{2,1,0:T(8,128)(2,1)S(1)}, bf16[2,1536,128]{2,1,0:T(8,128)(2,1)S(1)}, u32[]{:S(2)}, u32[]{:S(2)}) collective-permute-start(bf16[2,1536,128]{2,1,0:T(8,128)(2,1)S(1)} %collective-permute-done.9.refs_5_), channel_id=1, source_target_pairs={{0,64},{64,0},{128,192},{192,128},{256,320},{320,256},{384,448},{4... | collective-permute-start | bytes 2359304 | tf_op jit(solution)/shard_map/ppermute | solution.py:263
  77.9 6.7 %collective-permute-start.13 = (bf16[2,1536,128]{2,1,0:T(8,128)(2,1)S(1)}, bf16[2,1536,128]{2,1,0:T(8,128)(2,1)S(1)}, u32[]{:S(2)}, u32[]{:S(2)}) collective-permute-start(bf16[2,1536,128]{2,1,0:T(8,128)(2,1)S(1)} %collective-permute-done.7.refs_6_), channel_id=1, source_target_pairs={{0,64},{64,0},{128,192},{192,128},{256,320},{320,256},{384,448},{4... | collective-permute-start | bytes 2359304 | tf_op jit(solution)/shard_map/ppermute | solution.py:263
  81.2 5.0 %collective-permute-start.14 = (bf16[2,1536,128]{2,1,0:T(8,128)(2,1)S(1)}, bf16[2,1536,128]{2,1,0:T(8,128)(2,1)S(1)}, u32[]{:S(2)}, u32[]{:S(2)}) collective-permute-start(bf16[2,1536,128]{2,1,0:T(8,128)(2,1)S(1)} %collective-permute-done.10.refs_7_), channel_id=1, source_target_pairs={{0,64},{64,0},{128,192},{192,128},{256,320},{320,256},{384,448},{4... | collective-permute-start | bytes 2359304 | tf_op jit(solution)/shard_map/ppermute | solution.py:263
  86.3 1.1 copy-start
  87.4 1.1 copy-start.1

commit v3 on v2

--- a/solution.py
+++ b/solution.py
@@ -20,18 +20,26 @@
 NT = (((1,), (1,)), ((), ()))
 
 
-def fold_kernel(pair_ref, near_ref, h0_ref, h1_ref, h2_ref, a_ref, b_ref):
-    step = pl.program_id(0)
-    e = lax.rem(2 * pair_ref[0] + step, 4)
+def fold_kernel(pair_ref, near_ref, h_ref, out_ref, hbuf, sems):
+    first = 2 * pair_ref[0]
+    copies = [
+        pltpu.make_async_copy(
+            h_ref.at[first + k, pl.ds(9 * dx, 9)], hbuf.at[k, dx], sems.at[k, dx]
+        )
+        for k in range(2)
+        for dx in range(3)
+    ]
+    for copy in copies:
+        copy.start()
     rows = lax.broadcasted_iota(jnp.int32, (NB, NB), 0)
     cols = lax.broadcasted_iota(jnp.int32, (NB, NB), 1)
     eye = (rows == cols).astype(F32).astype(BF)
     choices = ((1,), (0, 2))
-
-    def write(out_ref):
-        for dx, h_ref in enumerate((h0_ref, h1_ref, h2_ref)):
+    for k in range(2):
+        for dx in range(3):
+            copies[3 * k + dx].wait()
             ids = [
-                near_ref[e, 9 * dx + 3 * b[0] + c[0]] for b in choices for c in choices
+                near_ref[first + k, 9 * dx + 3 * b[0] + c[0]] for b in choices for c in choices
             ]
             spot = 0
             for b in choices:
@@ -39,53 +47,35 @@
                     total = None
                     for i in b:
                         for j in c:
-                            part = h_ref[0, 3 * i + j].astype(F32)
+                            part = lax.dot_general(
+                                eye, hbuf[k, dx, 3 * i + j], NT, preferred_element_type=F32
+                            )
                             total = part if total is None else total + part
-                    turned = lax.dot_general(
-                        eye, total.astype(BF), NT, preferred_element_type=F32
-                    )
                     rank = jnp.int32(0)
                     for other in range(4):
                         if other != spot:
                             rank = rank + (ids[other] < ids[spot]).astype(jnp.int32)
                     row = pl.multiple_of((4 * dx + rank) * NB, NB)
-                    out_ref[0, pl.ds(row, NB), :] = turned.astype(BF)
+                    out_ref[k, pl.ds(row, NB), :] = total.astype(BF)
                     spot += 1
 
-    @pl.when(step < 2)
-    def _():
-        write(a_ref)
-
-    @pl.when(step >= 2)
-    def _():
-        write(b_ref)
-
 
 def fold(hamiltonian, neighbours, pair):
-    shape = jax.ShapeDtypeStruct((2, KDIM, NB), BF)
+    smem = pl.BlockSpec(memory_space=pltpu.SMEM)
     return pl.pallas_call(
         fold_kernel,
-        out_shape=(shape, shape),
-        grid_spec=pltpu.PrefetchScalarGridSpec(
-            num_scalar_prefetch=2,
-            grid=(4,),
-            in_specs=[
-                pl.BlockSpec(
-                    (1, 9, NB, NB),
-                    lambda t, pair, near, dx=dx: (lax.rem(2 * pair[0] + t, 4), dx, 0, 0),
-                )
-                for dx in range(3)
-            ],
-            out_specs=(
-                pl.BlockSpec((1, KDIM, NB), lambda t, pair, near: (jnp.minimum(t, 1), 0, 0)),
-                pl.BlockSpec((1, KDIM, NB), lambda t, pair, near: (jnp.maximum(t - 2, 0), 0, 0)),
-            ),
-        ),
+        out_shape=jax.ShapeDtypeStruct((2, KDIM, NB), BF),
+        in_specs=[smem, smem, pl.BlockSpec(memory_space=pltpu.HBM)],
+        out_specs=pl.BlockSpec(memory_space=pltpu.VMEM),
+        scratch_shapes=[
+            pltpu.VMEM((2, 3, 9, NB, NB), BF),
+            pltpu.SemaphoreType.DMA((2, 3)),
+        ],
         compiler_params=pltpu.CompilerParams(vmem_limit_bytes=60 * 2**20),
         cost_estimate=pl.CostEstimate(
-            flops=4 * 27 * 2 * NB**3, bytes_accessed=5200000, transcendentals=0
+            flops=2 * 27 * 2 * NB**3, bytes_accessed=2600000, transcendentals=0
         ),
-    )(pair, neighbours, hamiltonian, hamiltonian, hamiltonian)
+    )(pair, neighbours, hamiltonian)
 
 
 def turn_kernel(y_ref, near_ref, out_ref):
@@ -192,7 +182,8 @@
             phi = lax.dot_general(
                 last, bbuf[e, pl.ds(p, 512), :], NT, preferred_element_type=F32
             )
-            dens_ref[e : e + 1, p : p + 512] = jnp.sum(phi * phi, axis=0, keepdims=True)
+            total = jnp.sum(phi * phi, axis=0, keepdims=True)
+            dens_ref[e : e + 1, p : p + 512] = total * (1.0 / BANDS)
 
 
 def filtering(near, pieces, y_own, y_other, basis_values):
@@ -219,8 +210,18 @@
             pltpu.SemaphoreType.DMA((32,)),
             pltpu.SemaphoreType.DMA,
         ],
-        compiler_params=pltpu.CompilerParams(vmem_limit_bytes=40 * 2**20),
+        compiler_params=pltpu.CompilerParams(vmem_limit_bytes=38 * 2**20),
     )(near, *pieces, y_own, y_other, basis_values)
+
+
+def total_kernel(parts_ref, out_ref):
+    out_ref[...] = jnp.sum(parts_ref[...], axis=0)
+
+
+def total_of(parts):
+    return pl.pallas_call(
+        total_kernel, out_shape=jax.ShapeDtypeStruct(parts.shape[1:], F32)
+    )(parts)
 
 
 def routes(nbands):
@@ -262,7 +263,8 @@
     def move(value, pairs):
         return lax.ppermute(value, both, pairs)
 
-    own_a, own_b = fold(hamiltonian, neighbours, pa[None])
+    own_a = fold(hamiltonian, neighbours, pa[None])
+    own_b = fold(hamiltonian, neighbours, 1 - pa[None])
     from_below = move(own_a, up)
     from_above = move(own_b, down)
 
@@ -275,18 +277,15 @@
     y_own = lax.all_to_all(turned, "elem", 0, 0, axis_index_groups=groups)
     y_other = move(y_own, over_core)
 
+    own_a, own_b, y_own = lax.optimization_barrier((own_a, own_b, y_own))
     own_swapped = [move(own_a, over_core), move(own_b, over_core)]
     from_below, from_above, y_other, own_swapped = lax.optimization_barrier(
         (from_below, from_above, y_other, own_swapped)
     )
     far_a = move(from_below, up)
     far_b = move(from_above, down)
-    next_swapped = [move(from_below, over_core), move(from_above, over_core)]
-    for_x, for_y, next_swapped = lax.optimization_barrier(
-        (from_below, from_above, next_swapped)
-    )
-    below_b = move(for_x, over_x)
-    above_a = move(for_y, over_y)
+    below_b = move(from_below, over_x)
+    above_a = move(from_above, over_y)
 
 
     def table(y):
@@ -297,11 +296,11 @@
 
     ids, below_b = lax.optimization_barrier((ids, below_b))
     pieces = [own_a, own_b, from_below, from_above, far_a, far_b, below_b, above_a]
-    swapped = own_swapped + next_swapped + [move(piece, over_core) for piece in pieces[4:]]
+    swapped = own_swapped + [move(piece, over_core) for piece in pieces[2:]]
 
     filtered, partial = filtering(ids, pieces + swapped, y_own, y_other, basis_values)
     parts = partial.reshape(4, nbands, POINTS // nbands).swapaxes(0, 1)
-    density = jnp.sum(lax.all_to_all(parts, "band", 0, 0), axis=0) / BANDS
+    density = total_of(lax.all_to_all(parts, "band", 0, 0))
     return filtered, density
 
 

time: 136 us -> 133 us (0.978)
  waiting for transfers between devices: 22.1 us -> 12.5 us
  Pallas kernels: 23.2 us -> 29.1 us
  starting transfers between devices: 56.6 us -> 61.7 us
  blocking collectives: 27.6 us -> 23.9 us
    ppermute x15, waiting for transfers between devices: 22.1 us -> 12.5 us  [move(): return lax.ppermute(value, both, pairs)]
    pallas_call x1 -> x3, Pallas kernels: 5.66 us -> 11.4 us  [the longest x2 9.88 us: fold(): pl.pallas_call(fold_kernel, out_shape=jax.ShapeDtypeStruct((2, KDIM, NB),...]
    ppermute x15, starting transfers between devices: 48.8 us -> 53.9 us  [move(): return lax.ppermute(value, both, pairs)]
    all_to_all x1, blocking collectives: 27.6 us -> 23.9 us  [local(): density = total_of(lax.all_to_all(parts, 'band', 0, 0))]
  transfers between devices with their start and end apart: 16 -> 16, of which waited for: 4 -> 4; matrix products, arithmetic and copies ran while one was open for 0% -> 0% of each run, Pallas kernels for 0% -> 4%
where the time goes in v3:
time: 133 us; the launch traced here: 132 us
  starting transfers between devices  61.7 us (46%)
  Pallas kernels  29.1 us (22%)
  blocking collectives  23.9 us (18%)
  waiting for transfers between devices  12.5 us (9%)
  local copies, waits for them, and re-layouts  2.79 us (2%)
    ppermute x15, starting transfers between devices, move(): return lax.ppermute(value, both, pairs)  53.9 us
    all_to_all x1, blocking collectives, local(): density = total_of(lax.all_to_all(parts, 'band', 0, 0))  23.9 us
    pallas_call x1, Pallas kernels, filtering(): pl.pallas_call(filter_kernel, out_shape=(jax.ShapeDtypeStruct((4, NB, NB)...  16.7 us
    ppermute x15, waiting for transfers between devices, move(): return lax.ppermute(value, both, pairs)  12.5 us
    pallas_call x2, Pallas kernels, fold(): pl.pallas_call(fold_kernel, out_shape=jax.ShapeDtypeStruct((2, KDIM, NB),...  9.88 us
    all_to_all x1, starting transfers between devices, local(): y_own = lax.all_to_all(turned, 'elem', 0, 0, axis_index_groups=groups)  7.81 us
  transfers between devices with their start and end apart: 16, of which 4 were waited for; matrix products, arithmetic and copies ran while one was open for 0% of the time, Pallas kernels for 4%

profile of v3, /device:TPU:1, one launch (start us, length us, event | category | flops | bytes accessed | tf_op | source)
XLA Modules:
  0.0 131.8 jit_solution(14801472895431315243)
XLA Ops:
  0.6 0.0 copy-start.3
  0.6 0.0 copy-start.2
  0.7 5.0 %shard_map.60.refs_1_ = bf16[2,1536,128]{2,1,0:T(8,128)(2,1)} custom-call(s32[1]{0:T(128)S(6)} %sub.8.pair_ref, s32[4,27]{1,0:T(4,128)} %near_ref.3, bf16[4,27,128,128]{3,2,1,0:T(8,128)(2,1)} %h_ref.3), custom_call_target="tpu_custom_call" | custom-call | flops 226492416 | bytes 2600000 | tf_op jit(solution)/shard_map/pallas_call | solution.py:65
  5.7 0.0 copy-done.3
  5.7 0.0 copy-start
  5.7 0.0 copy-done.2
  5.7 0.9 shard_map.61
  6.7 7.8 %all-to-all-start = ((bf16[4,528,128]{2,1,0:T(8,128)(2,1)}), bf16[4,528,128]{2,1,0:T(8,128)(2,1)S(1)}, u32[]{:S(2)}, u32[]{:S(2)}) async-start(bf16[4,528,128]{2,1,0:T(8,128)(2,1)} %shard_map.61), calls=%async_computation | async-start | bytes 1081344 | tf_op jit(solution)/shard_map/all_to_all | solution.py:277
  14.5 8.2 %collective-permute-start.1 = (bf16[2,1536,128]{2,1,0:T(8,128)(2,1)}, bf16[2,1536,128]{2,1,0:T(8,128)(2,1)S(1)}, u32[]{:S(2)}, u32[]{:S(2)}) collective-permute-start(bf16[2,1536,128]{2,1,0:T(8,128)(2,1)} %shard_map.60.refs_1_), channel_id=1, source_target_pairs={{0,388},{64,452},{128,0},{192,64},{256,128},{320,192},{384,256},{4... | collective-permute-start | bytes 2359304 | tf_op jit(solution)/shard_map/ppermute | solution.py:264
  22.7 4.9 %shard_map.59.refs_0_ = bf16[2,1536,128]{2,1,0:T(8,128)(2,1)} custom-call(s32[1]{0:T(128)} %bitcast.pair_ref, s32[4,27]{1,0:T(4,128)} %near_ref.3, bf16[4,27,128,128]{3,2,1,0:T(8,128)(2,1)} %h_ref.3), custom_call_target="tpu_custom_call" | custom-call | flops 226492416 | bytes 2600000 | tf_op jit(solution)/shard_map/pallas_call | solution.py:65
  27.6 1.9 %collective-permute-start = (bf16[2,1536,128]{2,1,0:T(8,128)(2,1)}, bf16[2,1536,128]{2,1,0:T(8,128)(2,1)S(1)}, u32[]{:S(2)}, u32[]{:S(2)}) collective-permute-start(bf16[2,1536,128]{2,1,0:T(8,128)(2,1)} %shard_map.59.refs_0_), channel_id=1, source_target_pairs={{0,128},{64,192},{128,256},{192,320},{256,384},{320,448},{384,4},{... | collective-permute-start | bytes 2359304 | tf_op jit(solution)/shard_map/ppermute | solution.py:264
  29.5 0.0 all-to-all-done.refs_16_
  29.5 4.2 %collective-permute-start.3 = (bf16[2,1536,128]{2,1,0:T(8,128)(2,1)}, bf16[2,1536,128]{2,1,0:T(8,128)(2,1)}, u32[]{:S(2)}, u32[]{:S(2)}) collective-permute-start(bf16[2,1536,128]{2,1,0:T(8,128)(2,1)} %shard_map.59.refs_0_), channel_id=1, source_target_pairs={{0,64},{64,0},{128,192},{192,128},{256,320},{320,256},{384,448},{4... | collective-permute-start | bytes 2359304 | tf_op jit(solution)/shard_map/ppermute | solution.py:264
  33.8 0.0 copy-done
  33.8 1.9 %collective-permute-start.4 = (bf16[2,1536,128]{2,1,0:T(8,128)(2,1)S(1)}, bf16[2,1536,128]{2,1,0:T(8,128)(2,1)}, u32[]{:S(2)}, u32[]{:S(2)}) collective-permute-start(bf16[2,1536,128]{2,1,0:T(8,128)(2,1)S(1)} %copy-done), channel_id=1, source_target_pairs={{0,64},{64,0},{128,192},{192,128},{256,320},{320,256},{384,448},{4... | collective-permute-start | bytes 2359304 | tf_op jit(solution)/shard_map/ppermute | solution.py:264
  35.7 2.4 %collective-permute-start.2 = (bf16[4,528,128]{2,1,0:T(8,128)(2,1)S(1)}, bf16[4,528,128]{2,1,0:T(8,128)(2,1)S(1)}, u32[]{:S(2)}, u32[]{:S(2)}) collective-permute-start(bf16[4,528,128]{2,1,0:T(8,128)(2,1)S(1)} %all-to-all-done.refs_16_), channel_id=1, source_target_pairs={{0,64},{64,0},{128,192},{192,128},{256,320},{320,256},{384,448},{4... | collective-permute-start | bytes 1622024 | tf_op jit(solution)/shard_map/ppermute | solution.py:264
  38.2 3.7 %collective-permute-done.1.refs_3_ = bf16[2,1536,128]{2,1,0:T(8,128)(2,1)S(1)} collective-permute-done((bf16[2,1536,128]{2,1,0:T(8,128)(2,1)}, bf16[2,1536,128]{2,1,0:T(8,128)(2,1)S(1)}, u32[]{:S(2)}, u32[]{:S(2)}) %collective-permute-start.1) | collective-permute-done | bytes 786464 | tf_op jit(solution)/shard_map/ppermute | solution.py:264
  41.8 6.6 %collective-permute-done.refs_2_ = bf16[2,1536,128]{2,1,0:T(8,128)(2,1)S(1)} collective-permute-done((bf16[2,1536,128]{2,1,0:T(8,128)(2,1)}, bf16[2,1536,128]{2,1,0:T(8,128)(2,1)S(1)}, u32[]{:S(2)}, u32[]{:S(2)}) %collective-permute-start) | collective-permute-done | bytes 786464 | tf_op jit(solution)/shard_map/ppermute | solution.py:264
  48.4 0.0 collective-permute-done.2.refs_17_
  48.4 0.0 collective-permute-done.3.refs_8_
  48.5 0.0 collective-permute-done.4.refs_9_
  48.5 3.1 %collective-permute-start.5 = (bf16[2,1536,128]{2,1,0:T(8,128)(2,1)S(1)}, bf16[2,1536,128]{2,1,0:T(8,128)(2,1)S(1)}, u32[]{:S(2)}, u32[]{:S(2)}) collective-permute-start(bf16[2,1536,128]{2,1,0:T(8,128)(2,1)S(1)} %collective-permute-done.refs_2_), channel_id=1, source_target_pairs={{0,1},{64,65},{128,129},{192,193},{256,257},{320,321},{384,385},{4... | collective-permute-start | bytes 2359304 | tf_op jit(solution)/shard_map/ppermute | solution.py:264
  51.6 1.9 %collective-permute-start.6 = (bf16[2,1536,128]{2,1,0:T(8,128)(2,1)S(1)}, bf16[2,1536,128]{2,1,0:T(8,128)(2,1)S(1)}, u32[]{:S(2)}, u32[]{:S(2)}) collective-permute-start(bf16[2,1536,128]{2,1,0:T(8,128)(2,1)S(1)} %collective-permute-done.refs_2_), channel_id=1, source_target_pairs={{0,128},{64,192},{128,256},{192,320},{256,384},{320,448},{384,4},{... | collective-permute-start | bytes 2359304 | tf_op jit(solution)/shard_map/ppermute | solution.py:264
  53.5 4.6 %collective-permute-start.7 = (bf16[2,1536,128]{2,1,0:T(8,128)(2,1)S(1)}, bf16[2,1536,128]{2,1,0:T(8,128)(2,1)S(1)}, u32[]{:S(2)}, u32[]{:S(2)}) collective-permute-start(bf16[2,1536,128]{2,1,0:T(8,128)(2,1)S(1)} %collective-permute-done.1.refs_3_), channel_id=1, source_target_pairs={{0,388},{64,452},{128,0},{192,64},{256,128},{320,192},{384,256},{4... | collective-permute-start | bytes 2359304 | tf_op jit(solution)/shard_map/ppermute | solution.py:264
  58.1 3.2 %collective-permute-start.8 = (bf16[2,1536,128]{2,1,0:T(8,128)(2,1)S(1)}, bf16[2,1536,128]{2,1,0:T(8,128)(2,1)S(1)}, u32[]{:S(2)}, u32[]{:S(2)}) collective-permute-start(bf16[2,1536,128]{2,1,0:T(8,128)(2,1)S(1)} %collective-permute-done.1.refs_3_), channel_id=1, source_target_pairs={{0,8},{64,72},{128,136},{192,200},{256,264},{320,328},{384,392},{4... | collective-permute-start | bytes 2359304 | tf_op jit(solution)/shard_map/ppermute | solution.py:264
  61.3 5.5 %collective-permute-start.10 = (bf16[2,1536,128]{2,1,0:T(8,128)(2,1)S(1)}, bf16[2,1536,128]{2,1,0:T(8,128)(2,1)S(1)}, u32[]{:S(2)}, u32[]{:S(2)}) collective-permute-start(bf16[2,1536,128]{2,1,0:T(8,128)(2,1)S(1)} %collective-permute-done.1.refs_3_), channel_id=1, source_target_pairs={{0,64},{64,0},{128,192},{192,128},{256,320},{320,256},{384,448},{4... | collective-permute-start | bytes 2359304 | tf_op jit(solution)/shard_map/ppermute | solution.py:264
  66.8 0.1 collective-permute-done.5.refs_6_
  67.0 5.2 %collective-permute-start.9 = (bf16[2,1536,128]{2,1,0:T(8,128)(2,1)S(1)}, bf16[2,1536,128]{2,1,0:T(8,128)(2,1)S(1)}, u32[]{:S(2)}, u32[]{:S(2)}) collective-permute-start(bf16[2,1536,128]{2,1,0:T(8,128)(2,1)S(1)} %collective-permute-done.refs_2_), channel_id=1, source_target_pairs={{0,64},{64,0},{128,192},{192,128},{256,320},{320,256},{384,448},{4... | collective-permute-start | bytes 2359304 | tf_op jit(solution)/shard_map/ppermute | solution.py:264
  72.2 0.0 collective-permute-done.6.refs_4_
  72.2 4.3 %collective-permute-start.13 = (bf16[2,1536,128]{2,1,0:T(8,128)(2,1)S(1)}, bf16[2,1536,128]{2,1,0:T(8,128)(2,1)S(1)}, u32[]{:S(2)}, u32[]{:S(2)}) collective-permute-start(bf16[2,1536,128]{2,1,0:T(8,128)(2,1)S(1)} %collective-permute-done.5.refs_6_), channel_id=1, source_target_pairs={{0,64},{64,0},{128,192},{192,128},{256,320},{320,256},{384,448},{4... | collective-permute-start | bytes 2359304 | tf_op jit(solution)/shard_map/ppermute | solution.py:264
  76.5 0.0 collective-permute-done.7.refs_5_
  76.6 1.9 %collective-permute-start.11 = (bf16[2,1536,128]{2,1,0:T(8,128)(2,1)S(1)}, bf16[2,1536,128]{2,1,0:T(8,128)(2,1)S(1)}, u32[]{:S(2)}, u32[]{:S(2)}) collective-permute-start(bf16[2,1536,128]{2,1,0:T(8,128)(2,1)S(1)} %collective-permute-done.6.refs_4_), channel_id=1, source_target_pairs={{0,64},{64,0},{128,192},{192,128},{256,320},{320,256},{384,448},{4... | collective-permute-start | bytes 2359304 | tf_op jit(solution)/shard_map/ppermute | solution.py:264
  78.5 0.0 collective-permute-done.8.refs_7_
  78.5 3.3 %collective-permute-start.12 = (bf16[2,1536,128]{2,1,0:T(8,128)(2,1)S(1)}, bf16[2,1536,128]{2,1,0:T(8,128)(2,1)S(1)}, u32[]{:S(2)}, u32[]{:S(2)}) collective-permute-start(bf16[2,1536,128]{2,1,0:T(8,128)(2,1)S(1)} %collective-permute-done.7.refs_5_), channel_id=1, source_target_pairs={{0,64},{64,0},{128,192},{192,128},{256,320},{320,256},{384,448},{4... | collective-permute-start | bytes 2359304 | tf_op jit(solution)/shard_map/ppermute | solution.py:264
  81.8 0.0 collective-permute-done.10.refs_11_
  81.9 2.1 %collective-permute-start.14 = (bf16[2,1536,128]{2,1,0:T(8,128)(2,1)S(1)}, bf16[2,1536,128]{2,1,0:T(8,128)(2,1)S(1)}, u32[]{:S(2)}, u32[]{:S(2)}) collective-permute-start(bf16[2,1536,128]{2,1,0:T(8,128)(2,1)S(1)} %collective-permute-done.8.refs_7_), channel_id=1, source_target_pairs={{0,64},{64,0},{128,192},{192,128},{256,320},{320,256},{384,448},{4... | collective-permute-start | bytes 2359304 | tf_op jit(solution)/shard_map/ppermute | solution.py:264
  84.0 0.0 collective-permute-done.9.refs_10_
  84.0 0.0 collective-permute-done.13.refs_14_
  84.0 0.0 collective-permute-done.11.refs_12_
  84.0 0.0 collective-permute-done.12.refs_13_
  84.0 2.0 %collective-permute-done.14.refs_15_ = bf16[2,1536,128]{2,1,0:T(8,128)(2,1)S(1)} collective-permute-done((bf16[2,1536,128]{2,1,0:T(8,128)(2,1)S(1)}, bf16[2,1536,128]{2,1,0:T(8,128)(2,1)S(1)}, u32[]{:S(2)}, u32[]{:S(2)}) %collective-permute-start.14) | collective-permute-done | bytes 786464 | tf_op jit(solution)/shard_map/ppermute | solution.py:264
  86.0 0.0 copy-start.1
  86.0 1.1 copy-done.1
  87.2 16.7 %shard_map.62 = (bf16[4,128,128]{2,1,0:T(8,128)(2,1)}, f32[4,4096]{1,0:T(4,128)S(1)}) custom-call(s32[32,27]{1,0:T(8,128)S(1)} %bitcast.9, bf16[2,1536,128]{2,1,0:T(8,128)(2,1)S(1)} %copy-done.1, bf16[2,1536,128]{2,1,0:T(8,128)(2,1)S(1)} %copy-done, bf16[2,1536,128]{2,1,0:T(8,128)(2,1)S(1)} %collective-permute-done.refs_2_, ...), custom_call_target="tpu_custom_call" | custom-call | tf_op jit(solution)/shard_map/pallas_call | solution.py:194
  103.9 0.1 reshape.11
  104.0 0.1 copy.9
  104.1 0.1 reshape.12
  104.2 23.9 %all_to_all.10 = f32[64,1,256]{2,1,0:T(1,128)S(1)} all-to-all(f32[64,1,256]{2,1,0:T(1,128)S(1)} %reshape.12), channel_id=1, replica_groups=mesh['elem'=8,'band'=64] {'band'}, dimensions={0} | all-to-all | bytes 131072 | tf_op jit(solution)/shard_map/all_to_all | solution.py:303
  128.1 0.5 broadcast.6
  128.6 0.8 reduce
  129.4 0.8 reshape.13.parts_ref
  130.2 1.5 %shard_map.63 = f32[4,64]{1,0:T(4,128)} custom-call(f32[64,4,64]{2,1,0:T(4,128)} %reshape.13.parts_ref), custom_call_target="tpu_custom_call" | custom-call | tf_op jit(solution)/shard_map/pallas_call | solution.py:222
  (7 shorter events, 0.0 us)
Async XLA Ops:
  0.6 5.1 %copy-start.3 = (s32[4,27]{1,0:T(4,128)S(1)}, s32[4,27]{1,0:T(4,128)}, u32[]{:S(2)}) copy-start(s32[4,27]{1,0:T(4,128)} %near_ref.3) | copy-start | bytes 1300
  0.6 5.1 %copy-start.2 = (bf16[4,128,128]{2,1,0:T(8,128)(2,1)S(1)}, bf16[4,128,128]{2,1,0:T(8,128)(2,1)}, u32[]{:S(2)}) copy-start(bf16[4,128,128]{2,1,0:T(8,128)(2,1)} %y_ref) | copy-start | bytes 393220
  5.7 28.1 %copy-start = (bf16[2,1536,128]{2,1,0:T(8,128)(2,1)S(1)}, bf16[2,1536,128]{2,1,0:T(8,128)(2,1)}, u32[]{:S(2)}) copy-start(bf16[2,1536,128]{2,1,0:T(8,128)(2,1)} %shard_map.60.refs_1_) | copy-start | bytes 2359300
  6.7 22.8 %all-to-all-start = ((bf16[4,528,128]{2,1,0:T(8,128)(2,1)}), bf16[4,528,128]{2,1,0:T(8,128)(2,1)S(1)}, u32[]{:S(2)}, u32[]{:S(2)}) async-start(bf16[4,528,128]{2,1,0:T(8,128)(2,1)} %shard_map.61), calls=%async_computation | async-start | bytes 1081344 | tf_op jit(solution)/shard_map/all_to_all | solution.py:277
  14.5 27.3 %collective-permute-start.1 = (bf16[2,1536,128]{2,1,0:T(8,128)(2,1)}, bf16[2,1536,128]{2,1,0:T(8,128)(2,1)S(1)}, u32[]{:S(2)}, u32[]{:S(2)}) collective-permute-start(bf16[2,1536,128]{2,1,0:T(8,128)(2,1)} %shard_map.60.refs_1_), channel_id=1, source_target_pairs={{0,388},{64,452},{128,0},{192,64},{256,128},{320,192},{384,256},{4... | collective-permute-start | bytes 2359304 | tf_op jit(solution)/shard_map/ppermute | solution.py:264
  27.6 20.8 %collective-permute-start = (bf16[2,1536,128]{2,1,0:T(8,128)(2,1)}, bf16[2,1536,128]{2,1,0:T(8,128)(2,1)S(1)}, u32[]{:S(2)}, u32[]{:S(2)}) collective-permute-start(bf16[2,1536,128]{2,1,0:T(8,128)(2,1)} %shard_map.59.refs_0_), channel_id=1, source_target_pairs={{0,128},{64,192},{128,256},{192,320},{256,384},{320,448},{384,4},{... | collective-permute-start | bytes 2359304 | tf_op jit(solution)/shard_map/ppermute | solution.py:264
  29.5 18.9 %collective-permute-start.3 = (bf16[2,1536,128]{2,1,0:T(8,128)(2,1)}, bf16[2,1536,128]{2,1,0:T(8,128)(2,1)}, u32[]{:S(2)}, u32[]{:S(2)}) collective-permute-start(bf16[2,1536,128]{2,1,0:T(8,128)(2,1)} %shard_map.59.refs_0_), channel_id=1, source_target_pairs={{0,64},{64,0},{128,192},{192,128},{256,320},{320,256},{384,448},{4... | collective-permute-start | bytes 2359304 | tf_op jit(solution)/shard_map/ppermute | solution.py:264
  33.8 14.7 %collective-permute-start.4 = (bf16[2,1536,128]{2,1,0:T(8,128)(2,1)S(1)}, bf16[2,1536,128]{2,1,0:T(8,128)(2,1)}, u32[]{:S(2)}, u32[]{:S(2)}) collective-permute-start(bf16[2,1536,128]{2,1,0:T(8,128)(2,1)S(1)} %copy-done), channel_id=1, source_target_pairs={{0,64},{64,0},{128,192},{192,128},{256,320},{320,256},{384,448},{4... | collective-permute-start | bytes 2359304 | tf_op jit(solution)/shard_map/ppermute | solution.py:264
  35.7 12.7 %collective-permute-start.2 = (bf16[4,528,128]{2,1,0:T(8,128)(2,1)S(1)}, bf16[4,528,128]{2,1,0:T(8,128)(2,1)S(1)}, u32[]{:S(2)}, u32[]{:S(2)}) collective-permute-start(bf16[4,528,128]{2,1,0:T(8,128)(2,1)S(1)} %all-to-all-done.refs_16_), channel_id=1, source_target_pairs={{0,64},{64,0},{128,192},{192,128},{256,320},{320,256},{384,448},{4... | collective-permute-start | bytes 1622024 | tf_op jit(solution)/shard_map/ppermute | solution.py:264
  48.5 18.5 %collective-permute-start.5 = (bf16[2,1536,128]{2,1,0:T(8,128)(2,1)S(1)}, bf16[2,1536,128]{2,1,0:T(8,128)(2,1)S(1)}, u32[]{:S(2)}, u32[]{:S(2)}) collective-permute-start(bf16[2,1536,128]{2,1,0:T(8,128)(2,1)S(1)} %collective-permute-done.refs_2_), channel_id=1, source_target_pairs={{0,1},{64,65},{128,129},{192,193},{256,257},{320,321},{384,385},{4... | collective-permute-start | bytes 2359304 | tf_op jit(solution)/shard_map/ppermute | solution.py:264
  51.6 20.6 %collective-permute-start.6 = (bf16[2,1536,128]{2,1,0:T(8,128)(2,1)S(1)}, bf16[2,1536,128]{2,1,0:T(8,128)(2,1)S(1)}, u32[]{:S(2)}, u32[]{:S(2)}) collective-permute-start(bf16[2,1536,128]{2,1,0:T(8,128)(2,1)S(1)} %collective-permute-done.refs_2_), channel_id=1, source_target_pairs={{0,128},{64,192},{128,256},{192,320},{256,384},{320,448},{384,4},{... | collective-permute-start | bytes 2359304 | tf_op jit(solution)/shard_map/ppermute | solution.py:264
  53.5 23.0 %collective-permute-start.7 = (bf16[2,1536,128]{2,1,0:T(8,128)(2,1)S(1)}, bf16[2,1536,128]{2,1,0:T(8,128)(2,1)S(1)}, u32[]{:S(2)}, u32[]{:S(2)}) collective-permute-start(bf16[2,1536,128]{2,1,0:T(8,128)(2,1)S(1)} %collective-permute-done.1.refs_3_), channel_id=1, source_target_pairs={{0,388},{64,452},{128,0},{192,64},{256,128},{320,192},{384,256},{4... | collective-permute-start | bytes 2359304 | tf_op jit(solution)/shard_map/ppermute | solution.py:264
  58.1 20.4 %collective-permute-start.8 = (bf16[2,1536,128]{2,1,0:T(8,128)(2,1)S(1)}, bf16[2,1536,128]{2,1,0:T(8,128)(2,1)S(1)}, u32[]{:S(2)}, u32[]{:S(2)}) collective-permute-start(bf16[2,1536,128]{2,1,0:T(8,128)(2,1)S(1)} %collective-permute-done.1.refs_3_), channel_id=1, source_target_pairs={{0,8},{64,72},{128,136},{192,200},{256,264},{320,328},{384,392},{4... | collective-permute-start | bytes 2359304 | tf_op jit(solution)/shard_map/ppermute | solution.py:264
  61.3 20.5 %collective-permute-start.10 = (bf16[2,1536,128]{2,1,0:T(8,128)(2,1)S(1)}, bf16[2,1536,128]{2,1,0:T(8,128)(2,1)S(1)}, u32[]{:S(2)}, u32[]{:S(2)}) collective-permute-start(bf16[2,1536,128]{2,1,0:T(8,128)(2,1)S(1)} %collective-permute-done.1.refs_3_), channel_id=1, source_target_pairs={{0,64},{64,0},{128,192},{192,128},{256,320},{320,256},{384,448},{4... | collective-permute-start | bytes 2359304 | tf_op jit(solution)/shard_map/ppermute | solution.py:264
  67.0 17.0 %collective-permute-start.9 = (bf16[2,1536,128]{2,1,0:T(8,128)(2,1)S(1)}, bf16[2,1536,128]{2,1,0:T(8,128)(2,1)S(1)}, u32[]{:S(2)}, u32[]{:S(2)}) collective-permute-start(bf16[2,1536,128]{2,1,0:T(8,128)(2,1)S(1)} %collective-permute-done.refs_2_), channel_id=1, source_target_pairs={{0,64},{64,0},{128,192},{192,128},{256,320},{320,256},{384,448},{4... | collective-permute-start | bytes 2359304 | tf_op jit(solution)/shard_map/ppermute | solution.py:264
  72.2 11.8 %collective-permute-start.13 = (bf16[2,1536,128]{2,1,0:T(8,128)(2,1)S(1)}, bf16[2,1536,128]{2,1,0:T(8,128)(2,1)S(1)}, u32[]{:S(2)}, u32[]{:S(2)}) collective-permute-start(bf16[2,1536,128]{2,1,0:T(8,128)(2,1)S(1)} %collective-permute-done.5.refs_6_), channel_id=1, source_target_pairs={{0,64},{64,0},{128,192},{192,128},{256,320},{320,256},{384,448},{4... | collective-permute-start | bytes 2359304 | tf_op jit(solution)/shard_map/ppermute | solution.py:264
  76.6 7.4 %collective-permute-start.11 = (bf16[2,1536,128]{2,1,0:T(8,128)(2,1)S(1)}, bf16[2,1536,128]{2,1,0:T(8,128)(2,1)S(1)}, u32[]{:S(2)}, u32[]{:S(2)}) collective-permute-start(bf16[2,1536,128]{2,1,0:T(8,128)(2,1)S(1)} %collective-permute-done.6.refs_4_), channel_id=1, source_target_pairs={{0,64},{64,0},{128,192},{192,128},{256,320},{320,256},{384,448},{4... | collective-permute-start | bytes 2359304 | tf_op jit(solution)/shard_map/ppermute | solution.py:264
  78.5 5.5 %collective-permute-start.12 = (bf16[2,1536,128]{2,1,0:T(8,128)(2,1)S(1)}, bf16[2,1536,128]{2,1,0:T(8,128)(2,1)S(1)}, u32[]{:S(2)}, u32[]{:S(2)}) collective-permute-start(bf16[2,1536,128]{2,1,0:T(8,128)(2,1)S(1)} %collective-permute-done.7.refs_5_), channel_id=1, source_target_pairs={{0,64},{64,0},{128,192},{192,128},{256,320},{320,256},{384,448},{4... | collective-permute-start | bytes 2359304 | tf_op jit(solution)/shard_map/ppermute | solution.py:264
  81.9 4.2 %collective-permute-start.14 = (bf16[2,1536,128]{2,1,0:T(8,128)(2,1)S(1)}, bf16[2,1536,128]{2,1,0:T(8,128)(2,1)S(1)}, u32[]{:S(2)}, u32[]{:S(2)}) collective-permute-start(bf16[2,1536,128]{2,1,0:T(8,128)(2,1)S(1)} %collective-permute-done.8.refs_7_), channel_id=1, source_target_pairs={{0,64},{64,0},{128,192},{192,128},{256,320},{320,256},{384,448},{4... | collective-permute-start | bytes 2359304 | tf_op jit(solution)/shard_map/ppermute | solution.py:264
  86.0 1.1 copy-start.1

commit v4 on v2

--- a/solution.py
+++ b/solution.py
@@ -81,7 +81,7 @@
                 pl.BlockSpec((1, KDIM, NB), lambda t, pair, near: (jnp.maximum(t - 2, 0), 0, 0)),
             ),
         ),
-        compiler_params=pltpu.CompilerParams(vmem_limit_bytes=60 * 2**20),
+        compiler_params=pltpu.CompilerParams(vmem_limit_bytes=16 * 2**20),
         cost_estimate=pl.CostEstimate(
             flops=4 * 27 * 2 * NB**3, bytes_accessed=5200000, transcendentals=0
         ),
@@ -192,7 +192,8 @@
             phi = lax.dot_general(
                 last, bbuf[e, pl.ds(p, 512), :], NT, preferred_element_type=F32
             )
-            dens_ref[e : e + 1, p : p + 512] = jnp.sum(phi * phi, axis=0, keepdims=True)
+            total = jnp.sum(phi * phi, axis=0, keepdims=True)
+            dens_ref[e : e + 1, p : p + 512] = total * (1.0 / BANDS)
 
 
 def filtering(near, pieces, y_own, y_other, basis_values):
@@ -219,7 +220,7 @@
             pltpu.SemaphoreType.DMA((32,)),
             pltpu.SemaphoreType.DMA,
         ],
-        compiler_params=pltpu.CompilerParams(vmem_limit_bytes=40 * 2**20),
+        compiler_params=pltpu.CompilerParams(vmem_limit_bytes=38 * 2**20),
     )(near, *pieces, y_own, y_other, basis_values)
 
 
@@ -266,9 +267,6 @@
     from_below = move(own_a, up)
     from_above = move(own_b, down)
 
-    coefficients, neighbours, own_b = lax.optimization_barrier(
-        (coefficients, neighbours, own_b)
-    )
     near = jnp.pad(neighbours.astype(BF), ((0, EDGE - 4), (0, NB - 27)))
     turned = turn(coefficients, near)
     groups = [[2 * z + c for z in range(4)] for c in range(2)]
@@ -276,17 +274,13 @@
     y_other = move(y_own, over_core)
 
     own_swapped = [move(own_a, over_core), move(own_b, over_core)]
-    from_below, from_above, y_other, own_swapped = lax.optimization_barrier(
-        (from_below, from_above, y_other, own_swapped)
+    from_above, y_other, own_swapped = lax.optimization_barrier(
+        (from_above, y_other, own_swapped)
     )
     far_a = move(from_below, up)
     far_b = move(from_above, down)
-    next_swapped = [move(from_below, over_core), move(from_above, over_core)]
-    for_x, for_y, next_swapped = lax.optimization_barrier(
-        (from_below, from_above, next_swapped)
-    )
-    below_b = move(for_x, over_x)
-    above_a = move(for_y, over_y)
+    below_b = move(from_below, over_x)
+    above_a = move(from_above, over_y)
 
 
     def table(y):
@@ -297,12 +291,13 @@
 
     ids, below_b = lax.optimization_barrier((ids, below_b))
     pieces = [own_a, own_b, from_below, from_above, far_a, far_b, below_b, above_a]
-    swapped = own_swapped + next_swapped + [move(piece, over_core) for piece in pieces[4:]]
+    swapped = own_swapped + [move(piece, over_core) for piece in pieces[2:]]
 
     filtered, partial = filtering(ids, pieces + swapped, y_own, y_other, basis_values)
-    parts = partial.reshape(4, nbands, POINTS // nbands).swapaxes(0, 1)
-    density = jnp.sum(lax.all_to_all(parts, "band", 0, 0), axis=0) / BANDS
-    return filtered, density
+    points = POINTS // nbands
+    parts = partial.reshape(4, nbands, points).swapaxes(0, 1)
+    parts = lax.all_to_all(parts.reshape(nbands, points // 32, 128), "band", 0, 0)
+    return filtered, jnp.sum(parts, axis=0).reshape(4, points)
 
 
 def solution(mesh):

time: 136 us -> 128 us (0.941)
  waiting for transfers between devices: 22.1 us -> 17.3 us
  Pallas kernels: 23.2 us -> 19.7 us
  starting transfers between devices: 56.6 us -> 55.1 us
    ppermute x15, waiting for transfers between devices: 22.1 us -> 17.3 us  [move(): return lax.ppermute(value, both, pairs)]
    pallas_call x1, Pallas kernels: 5.66 us -> 2.24 us  [fold(): pl.pallas_call(fold_kernel, out_shape=(shape, shape), grid_spec=pltpu.Pre...]
    ppermute x15, starting transfers between devices: 48.8 us -> 47.3 us  [move(): return lax.ppermute(value, both, pairs)]
    unnamed x10 -> x6, local copies, waits for them, and re-layouts: 2.52 us -> 3.58 us
  transfers between devices with their start and end apart: 16 -> 16, of which waited for: 4 -> 3; matrix products, arithmetic and copies ran while one was open for 0% -> 0% of each run, Pallas kernels for 0% -> 2%
where the time goes in v4:
time: 128 us; the launch traced here: 127 us
  starting transfers between devices  55.1 us (43%)
  blocking collectives  28.6 us (22%)
  Pallas kernels  19.7 us (15%)
  waiting for transfers between devices  17.3 us (14%)
  local copies, waits for them, and re-layouts  4.61 us (4%)
    ppermute x15, starting transfers between devices, move(): return lax.ppermute(value, both, pairs)  47.3 us
    all_to_all x1, blocking collectives, local(): lax.all_to_all(parts.reshape(nbands, points // 32, 128), 'band', 0, 0)  28.6 us
    ppermute x15, waiting for transfers between devices, move(): return lax.ppermute(value, both, pairs)  17.3 us
    pallas_call x1, Pallas kernels, filtering(): pl.pallas_call(filter_kernel, out_shape=(jax.ShapeDtypeStruct((4, NB, NB)...  16.6 us
    all_to_all x1, starting transfers between devices, local(): y_own = lax.all_to_all(turned, 'elem', 0, 0, axis_index_groups=groups)  7.81 us
    unnamed x6, local copies, waits for them, and re-layouts  3.58 us
  transfers between devices with their start and end apart: 16, of which 3 were waited for; matrix products, arithmetic and copies ran while one was open for 0% of the time, Pallas kernels for 2%

profile of v4, /device:TPU:1, one launch (start us, length us, event | category | flops | bytes accessed | tf_op | source)
XLA Modules:
  0.0 127.1 jit_solution(6512845422059173870)
XLA Ops:
  0.6 0.7 convert_element_type.4
  1.3 0.0 copy-start.1
  1.3 0.9 copy-done.1
  2.2 0.9 shard_map.59
  3.1 7.8 %all-to-all-start = ((bf16[4,528,128]{2,1,0:T(8,128)(2,1)}), bf16[4,528,128]{2,1,0:T(8,128)(2,1)S(1)}, u32[]{:S(2)}, u32[]{:S(2)}) async-start(bf16[4,528,128]{2,1,0:T(8,128)(2,1)} %shard_map.59), calls=%async_computation | async-start | bytes 1081344 | tf_op jit(solution)/shard_map/all_to_all | solution.py:273
  11.0 0.0 copy-start
  11.0 2.0 %copy-done = bf16[4,27,128,128]{3,2,1,0:T(8,128)(2,1)S(1)} copy-done((bf16[4,27,128,128]{3,2,1,0:T(8,128)(2,1)S(1)}, bf16[4,27,128,128]{3,2,1,0:T(8,128)(2,1)}, u32[]{:S(2)}) %copy-start) | copy-done | bytes 3538968
  13.0 0.0 copy-start.2
  13.0 0.7 copy-done.2
  13.6 2.2 %shard_map.60 = (bf16[2,1536,128]{2,1,0:T(8,128)(2,1)S(1)}, bf16[2,1536,128]{2,1,0:T(8,128)(2,1)S(1)}) custom-call(s32[1]{0:T(128)} %bitcast.1.pair_ref, s32[4,27]{1,0:T(4,128)S(1)} %copy-done.2, bf16[4,27,128,128]{3,2,1,0:T(8,128)(2,1)S(1)} %copy-done, bf16[4,27,128,128]{3,2,1,0:T(8,128)(2,1)S(1)} %copy-done, bf16[4,27,128,128]{3,2,1,0:T(8,128)(2,1)S(1)} %copy-done), custom_call_target="tpu_custom_call" | custom-call | flops 452984832 | bytes 5200000 | tf_op jit(solution)/shard_map/pallas_call | solution.py:66
  15.9 3.4 %collective-permute-start.4 = (bf16[2,1536,128]{2,1,0:T(8,128)(2,1)S(1)}, bf16[2,1536,128]{2,1,0:T(8,128)(2,1)S(1)}, u32[]{:S(2)}, u32[]{:S(2)}) collective-permute-start(bf16[2,1536,128]{2,1,0:T(8,128)(2,1)S(1)} %get-tuple-element.13.refs_0_), channel_id=1, source_target_pairs={{0,128},{64,192},{128,256},{192,320},{256,384},{320,448},{384,4},{... | collective-permute-start | bytes 2359304 | tf_op jit(solution)/shard_map/ppermute | solution.py:264
  19.3 5.0 %collective-permute-start.3 = (bf16[2,1536,128]{2,1,0:T(8,128)(2,1)S(1)}, bf16[2,1536,128]{2,1,0:T(8,128)(2,1)}, u32[]{:S(2)}, u32[]{:S(2)}) collective-permute-start(bf16[2,1536,128]{2,1,0:T(8,128)(2,1)S(1)} %get-tuple-element.12.refs_1_), channel_id=1, source_target_pairs={{0,64},{64,0},{128,192},{192,128},{256,320},{320,256},{384,448},{4... | collective-permute-start | bytes 2359304 | tf_op jit(solution)/shard_map/ppermute | solution.py:264
  24.3 4.9 %collective-permute-start = (bf16[2,1536,128]{2,1,0:T(8,128)(2,1)S(1)}, bf16[2,1536,128]{2,1,0:T(8,128)(2,1)}, u32[]{:S(2)}, u32[]{:S(2)}) collective-permute-start(bf16[2,1536,128]{2,1,0:T(8,128)(2,1)S(1)} %get-tuple-element.12.refs_1_), channel_id=1, source_target_pairs={{0,388},{64,452},{128,0},{192,64},{256,128},{320,192},{384,256},{4... | collective-permute-start | bytes 2359304 | tf_op jit(solution)/shard_map/ppermute | solution.py:264
  29.2 2.2 %collective-permute-start.2 = (bf16[2,1536,128]{2,1,0:T(8,128)(2,1)S(1)}, bf16[2,1536,128]{2,1,0:T(8,128)(2,1)}, u32[]{:S(2)}, u32[]{:S(2)}) collective-permute-start(bf16[2,1536,128]{2,1,0:T(8,128)(2,1)S(1)} %get-tuple-element.13.refs_0_), channel_id=1, source_target_pairs={{0,64},{64,0},{128,192},{192,128},{256,320},{320,256},{384,448},{4... | collective-permute-start | bytes 2359304 | tf_op jit(solution)/shard_map/ppermute | solution.py:264
  31.4 0.0 all-to-all-done.refs_16_
  31.4 2.1 %collective-permute-start.1 = (bf16[4,528,128]{2,1,0:T(8,128)(2,1)S(1)}, bf16[4,528,128]{2,1,0:T(8,128)(2,1)S(1)}, u32[]{:S(2)}, u32[]{:S(2)}) collective-permute-start(bf16[4,528,128]{2,1,0:T(8,128)(2,1)S(1)} %all-to-all-done.refs_16_), channel_id=1, source_target_pairs={{0,64},{64,0},{128,192},{192,128},{256,320},{320,256},{384,448},{4... | collective-permute-start | bytes 1622024 | tf_op jit(solution)/shard_map/ppermute | solution.py:264
  33.6 7.2 %collective-permute-done.4.refs_2_ = bf16[2,1536,128]{2,1,0:T(8,128)(2,1)S(1)} collective-permute-done((bf16[2,1536,128]{2,1,0:T(8,128)(2,1)S(1)}, bf16[2,1536,128]{2,1,0:T(8,128)(2,1)S(1)}, u32[]{:S(2)}, u32[]{:S(2)}) %collective-permute-start.4) | collective-permute-done | bytes 786464 | tf_op jit(solution)/shard_map/ppermute | solution.py:264
  40.7 3.8 %collective-permute-start.9 = (bf16[2,1536,128]{2,1,0:T(8,128)(2,1)S(1)}, bf16[2,1536,128]{2,1,0:T(8,128)(2,1)S(1)}, u32[]{:S(2)}, u32[]{:S(2)}) collective-permute-start(bf16[2,1536,128]{2,1,0:T(8,128)(2,1)S(1)} %collective-permute-done.4.refs_2_), channel_id=1, source_target_pairs={{0,64},{64,0},{128,192},{192,128},{256,320},{320,256},{384,448},{4... | collective-permute-start | bytes 2359304 | tf_op jit(solution)/shard_map/ppermute | solution.py:264
  44.5 0.0 collective-permute-done.3.refs_9_
  44.5 1.9 %collective-permute-start.6 = (bf16[2,1536,128]{2,1,0:T(8,128)(2,1)S(1)}, bf16[2,1536,128]{2,1,0:T(8,128)(2,1)S(1)}, u32[]{:S(2)}, u32[]{:S(2)}) collective-permute-start(bf16[2,1536,128]{2,1,0:T(8,128)(2,1)S(1)} %collective-permute-done.4.refs_2_), channel_id=1, source_target_pairs={{0,128},{64,192},{128,256},{192,320},{256,384},{320,448},{384,4},{... | collective-permute-start | bytes 2359304 | tf_op jit(solution)/shard_map/ppermute | solution.py:264
  46.4 0.0 collective-permute-done.refs_3_
  46.4 3.1 %collective-permute-start.5 = (bf16[2,1536,128]{2,1,0:T(8,128)(2,1)S(1)}, bf16[2,1536,128]{2,1,0:T(8,128)(2,1)S(1)}, u32[]{:S(2)}, u32[]{:S(2)}) collective-permute-start(bf16[2,1536,128]{2,1,0:T(8,128)(2,1)S(1)} %collective-permute-done.4.refs_2_), channel_id=1, source_target_pairs={{0,1},{64,65},{128,129},{192,193},{256,257},{320,321},{384,385},{4... | collective-permute-start | bytes 2359304 | tf_op jit(solution)/shard_map/ppermute | solution.py:264
  49.6 0.0 collective-permute-done.2.refs_8_
  49.6 0.0 collective-permute-done.1.refs_17_
  49.6 3.2 %collective-permute-start.8 = (bf16[2,1536,128]{2,1,0:T(8,128)(2,1)}, bf16[2,1536,128]{2,1,0:T(8,128)(2,1)S(1)}, u32[]{:S(2)}, u32[]{:S(2)}) collective-permute-start(bf16[2,1536,128]{2,1,0:T(8,128)(2,1)} %collective-permute-done.refs_3_), channel_id=1, source_target_pairs={{0,8},{64,72},{128,136},{192,200},{256,264},{320,328},{384,392},{4... | collective-permute-start | bytes 2359304 | tf_op jit(solution)/shard_map/ppermute | solution.py:264
  52.8 5.6 %collective-permute-start.7 = (bf16[2,1536,128]{2,1,0:T(8,128)(2,1)}, bf16[2,1536,128]{2,1,0:T(8,128)(2,1)S(1)}, u32[]{:S(2)}, u32[]{:S(2)}) collective-permute-start(bf16[2,1536,128]{2,1,0:T(8,128)(2,1)} %collective-permute-done.refs_3_), channel_id=1, source_target_pairs={{0,388},{64,452},{128,0},{192,64},{256,128},{320,192},{384,256},{4... | collective-permute-start | bytes 2359304 | tf_op jit(solution)/shard_map/ppermute | solution.py:264
  58.5 8.5 %collective-permute-done.5.refs_6_ = bf16[2,1536,128]{2,1,0:T(8,128)(2,1)S(1)} collective-permute-done((bf16[2,1536,128]{2,1,0:T(8,128)(2,1)S(1)}, bf16[2,1536,128]{2,1,0:T(8,128)(2,1)S(1)}, u32[]{:S(2)}, u32[]{:S(2)}) %collective-permute-start.5) | collective-permute-done | bytes 786464 | tf_op jit(solution)/shard_map/ppermute | solution.py:264
  67.0 3.2 %collective-permute-start.10 = (bf16[2,1536,128]{2,1,0:T(8,128)(2,1)}, bf16[2,1536,128]{2,1,0:T(8,128)(2,1)S(1)}, u32[]{:S(2)}, u32[]{:S(2)}) collective-permute-start(bf16[2,1536,128]{2,1,0:T(8,128)(2,1)} %collective-permute-done.refs_3_), channel_id=1, source_target_pairs={{0,64},{64,0},{128,192},{192,128},{256,320},{320,256},{384,448},{4... | collective-permute-start | bytes 2359304 | tf_op jit(solution)/shard_map/ppermute | solution.py:264
  70.2 0.0 collective-permute-done.9.refs_10_
  70.2 1.9 %collective-permute-start.13 = (bf16[2,1536,128]{2,1,0:T(8,128)(2,1)S(1)}, bf16[2,1536,128]{2,1,0:T(8,128)(2,1)S(1)}, u32[]{:S(2)}, u32[]{:S(2)}) collective-permute-start(bf16[2,1536,128]{2,1,0:T(8,128)(2,1)S(1)} %collective-permute-done.5.refs_6_), channel_id=1, source_target_pairs={{0,64},{64,0},{128,192},{192,128},{256,320},{320,256},{384,448},{4... | collective-permute-start | bytes 2359304 | tf_op jit(solution)/shard_map/ppermute | solution.py:264
  72.1 0.0 collective-permute-done.6.refs_4_
  72.2 2.4 %collective-permute-start.11 = (bf16[2,1536,128]{2,1,0:T(8,128)(2,1)S(1)}, bf16[2,1536,128]{2,1,0:T(8,128)(2,1)S(1)}, u32[]{:S(2)}, u32[]{:S(2)}) collective-permute-start(bf16[2,1536,128]{2,1,0:T(8,128)(2,1)S(1)} %collective-permute-done.6.refs_4_), channel_id=1, source_target_pairs={{0,64},{64,0},{128,192},{192,128},{256,320},{320,256},{384,448},{4... | collective-permute-start | bytes 2359304 | tf_op jit(solution)/shard_map/ppermute | solution.py:264
  74.6 0.0 collective-permute-done.8.refs_7_
  74.6 1.9 %collective-permute-start.14 = (bf16[2,1536,128]{2,1,0:T(8,128)(2,1)S(1)}, bf16[2,1536,128]{2,1,0:T(8,128)(2,1)S(1)}, u32[]{:S(2)}, u32[]{:S(2)}) collective-permute-start(bf16[2,1536,128]{2,1,0:T(8,128)(2,1)S(1)} %collective-permute-done.8.refs_7_), channel_id=1, source_target_pairs={{0,64},{64,0},{128,192},{192,128},{256,320},{320,256},{384,448},{4... | collective-permute-start | bytes 2359304 | tf_op jit(solution)/shard_map/ppermute | solution.py:264
  76.5 0.0 collective-permute-done.7.refs_5_
  76.5 2.6 %collective-permute-start.12 = (bf16[2,1536,128]{2,1,0:T(8,128)(2,1)S(1)}, bf16[2,1536,128]{2,1,0:T(8,128)(2,1)S(1)}, u32[]{:S(2)}, u32[]{:S(2)}) collective-permute-start(bf16[2,1536,128]{2,1,0:T(8,128)(2,1)S(1)} %collective-permute-done.7.refs_5_), channel_id=1, source_target_pairs={{0,64},{64,0},{128,192},{192,128},{256,320},{320,256},{384,448},{4... | collective-permute-start | bytes 2359304 | tf_op jit(solution)/shard_map/ppermute | solution.py:264
  79.1 0.0 collective-permute-done.10.refs_11_
  79.1 0.0 collective-permute-done.11.refs_12_
  79.1 0.0 collective-permute-done.13.refs_14_
  79.1 0.0 collective-permute-done.14.refs_15_
  79.2 1.7 %collective-permute-done.12.refs_13_ = bf16[2,1536,128]{2,1,0:T(8,128)(2,1)S(1)} collective-permute-done((bf16[2,1536,128]{2,1,0:T(8,128)(2,1)S(1)}, bf16[2,1536,128]{2,1,0:T(8,128)(2,1)S(1)}, u32[]{:S(2)}, u32[]{:S(2)}) %collective-permute-start.12) | collective-permute-done | bytes 786464 | tf_op jit(solution)/shard_map/ppermute | solution.py:264
  80.8 16.6 %shard_map.61 = (bf16[4,128,128]{2,1,0:T(8,128)(2,1)}, f32[4,4096]{1,0:T(4,128)S(1)}) custom-call(s32[32,27]{1,0:T(8,128)S(1)} %bitcast.9, bf16[2,1536,128]{2,1,0:T(8,128)(2,1)S(1)} %get-tuple-element.13.refs_0_, bf16[2,1536,128]{2,1,0:T(8,128)(2,1)S(1)} %get-tuple-element.12.refs_1_, bf16[2,1536,128]{2,1,0:T(8,128)(2,1)S(1)} %collective-permute-done.4.refs_2_, ...), custom_call_target="tpu_custom_call" | custom-call | tf_op jit(solution)/shard_map/pallas_call | solution.py:204
  97.4 0.1 reshape.17
  97.5 0.1 copy.9
  97.6 0.1 reshape.18
  97.8 28.6 %all_to_all.10 = f32[64,2,128]{2,1,0:T(2,128)S(1)} all-to-all(f32[64,2,128]{2,1,0:T(2,128)S(1)} %reshape.18), channel_id=1, replica_groups=mesh['elem'=8,'band'=64] {'band'}, dimensions={0} | all-to-all | bytes 131072 | tf_op jit(solution)/shard_map/all_to_all | solution.py:299
  126.3 0.1 reduce_sum.9
  126.4 0.7 reshape.19
  (6 shorter events, 0.0 us)
Async XLA Ops:
  1.3 0.9 copy-start.1
  3.1 28.3 %all-to-all-start = ((bf16[4,528,128]{2,1,0:T(8,128)(2,1)}), bf16[4,528,128]{2,1,0:T(8,128)(2,1)S(1)}, u32[]{:S(2)}, u32[]{:S(2)}) async-start(bf16[4,528,128]{2,1,0:T(8,128)(2,1)} %shard_map.59), calls=%async_computation | async-start | bytes 1081344 | tf_op jit(solution)/shard_map/all_to_all | solution.py:273
  11.0 2.0 %copy-start = (bf16[4,27,128,128]{3,2,1,0:T(8,128)(2,1)S(1)}, bf16[4,27,128,128]{3,2,1,0:T(8,128)(2,1)}, u32[]{:S(2)}) copy-start(bf16[4,27,128,128]{3,2,1,0:T(8,128)(2,1)} %h2_ref.1) | copy-start | bytes 10616836
  13.0 0.7 copy-start.2
  15.9 24.8 %collective-permute-start.4 = (bf16[2,1536,128]{2,1,0:T(8,128)(2,1)S(1)}, bf16[2,1536,128]{2,1,0:T(8,128)(2,1)S(1)}, u32[]{:S(2)}, u32[]{:S(2)}) collective-permute-start(bf16[2,1536,128]{2,1,0:T(8,128)(2,1)S(1)} %get-tuple-element.13.refs_0_), channel_id=1, source_target_pairs={{0,128},{64,192},{128,256},{192,320},{256,384},{320,448},{384,4},{... | collective-permute-start | bytes 2359304 | tf_op jit(solution)/shard_map/ppermute | solution.py:264
  19.3 25.2 %collective-permute-start.3 = (bf16[2,1536,128]{2,1,0:T(8,128)(2,1)S(1)}, bf16[2,1536,128]{2,1,0:T(8,128)(2,1)}, u32[]{:S(2)}, u32[]{:S(2)}) collective-permute-start(bf16[2,1536,128]{2,1,0:T(8,128)(2,1)S(1)} %get-tuple-element.12.refs_1_), channel_id=1, source_target_pairs={{0,64},{64,0},{128,192},{192,128},{256,320},{320,256},{384,448},{4... | collective-permute-start | bytes 2359304 | tf_op jit(solution)/shard_map/ppermute | solution.py:264
  24.3 22.2 %collective-permute-start = (bf16[2,1536,128]{2,1,0:T(8,128)(2,1)S(1)}, bf16[2,1536,128]{2,1,0:T(8,128)(2,1)}, u32[]{:S(2)}, u32[]{:S(2)}) collective-permute-start(bf16[2,1536,128]{2,1,0:T(8,128)(2,1)S(1)} %get-tuple-element.12.refs_1_), channel_id=1, source_target_pairs={{0,388},{64,452},{128,0},{192,64},{256,128},{320,192},{384,256},{4... | collective-permute-start | bytes 2359304 | tf_op jit(solution)/shard_map/ppermute | solution.py:264
  29.2 20.4 %collective-permute-start.2 = (bf16[2,1536,128]{2,1,0:T(8,128)(2,1)S(1)}, bf16[2,1536,128]{2,1,0:T(8,128)(2,1)}, u32[]{:S(2)}, u32[]{:S(2)}) collective-permute-start(bf16[2,1536,128]{2,1,0:T(8,128)(2,1)S(1)} %get-tuple-element.13.refs_0_), channel_id=1, source_target_pairs={{0,64},{64,0},{128,192},{192,128},{256,320},{320,256},{384,448},{4... | collective-permute-start | bytes 2359304 | tf_op jit(solution)/shard_map/ppermute | solution.py:264
  31.4 18.2 %collective-permute-start.1 = (bf16[4,528,128]{2,1,0:T(8,128)(2,1)S(1)}, bf16[4,528,128]{2,1,0:T(8,128)(2,1)S(1)}, u32[]{:S(2)}, u32[]{:S(2)}) collective-permute-start(bf16[4,528,128]{2,1,0:T(8,128)(2,1)S(1)} %all-to-all-done.refs_16_), channel_id=1, source_target_pairs={{0,64},{64,0},{128,192},{192,128},{256,320},{320,256},{384,448},{4... | collective-permute-start | bytes 1622024 | tf_op jit(solution)/shard_map/ppermute | solution.py:264
  40.7 29.5 %collective-permute-start.9 = (bf16[2,1536,128]{2,1,0:T(8,128)(2,1)S(1)}, bf16[2,1536,128]{2,1,0:T(8,128)(2,1)S(1)}, u32[]{:S(2)}, u32[]{:S(2)}) collective-permute-start(bf16[2,1536,128]{2,1,0:T(8,128)(2,1)S(1)} %collective-permute-done.4.refs_2_), channel_id=1, source_target_pairs={{0,64},{64,0},{128,192},{192,128},{256,320},{320,256},{384,448},{4... | collective-permute-start | bytes 2359304 | tf_op jit(solution)/shard_map/ppermute | solution.py:264
  44.5 27.6 %collective-permute-start.6 = (bf16[2,1536,128]{2,1,0:T(8,128)(2,1)S(1)}, bf16[2,1536,128]{2,1,0:T(8,128)(2,1)S(1)}, u32[]{:S(2)}, u32[]{:S(2)}) collective-permute-start(bf16[2,1536,128]{2,1,0:T(8,128)(2,1)S(1)} %collective-permute-done.4.refs_2_), channel_id=1, source_target_pairs={{0,128},{64,192},{128,256},{192,320},{256,384},{320,448},{384,4},{... | collective-permute-start | bytes 2359304 | tf_op jit(solution)/shard_map/ppermute | solution.py:264
  46.4 20.5 %collective-permute-start.5 = (bf16[2,1536,128]{2,1,0:T(8,128)(2,1)S(1)}, bf16[2,1536,128]{2,1,0:T(8,128)(2,1)S(1)}, u32[]{:S(2)}, u32[]{:S(2)}) collective-permute-start(bf16[2,1536,128]{2,1,0:T(8,128)(2,1)S(1)} %collective-permute-done.4.refs_2_), channel_id=1, source_target_pairs={{0,1},{64,65},{128,129},{192,193},{256,257},{320,321},{384,385},{4... | collective-permute-start | bytes 2359304 | tf_op jit(solution)/shard_map/ppermute | solution.py:264
  49.6 25.0 %collective-permute-start.8 = (bf16[2,1536,128]{2,1,0:T(8,128)(2,1)}, bf16[2,1536,128]{2,1,0:T(8,128)(2,1)S(1)}, u32[]{:S(2)}, u32[]{:S(2)}) collective-permute-start(bf16[2,1536,128]{2,1,0:T(8,128)(2,1)} %collective-permute-done.refs_3_), channel_id=1, source_target_pairs={{0,8},{64,72},{128,136},{192,200},{256,264},{320,328},{384,392},{4... | collective-permute-start | bytes 2359304 | tf_op jit(solution)/shard_map/ppermute | solution.py:264
  52.8 23.7 %collective-permute-start.7 = (bf16[2,1536,128]{2,1,0:T(8,128)(2,1)}, bf16[2,1536,128]{2,1,0:T(8,128)(2,1)S(1)}, u32[]{:S(2)}, u32[]{:S(2)}) collective-permute-start(bf16[2,1536,128]{2,1,0:T(8,128)(2,1)} %collective-permute-done.refs_3_), channel_id=1, source_target_pairs={{0,388},{64,452},{128,0},{192,64},{256,128},{320,192},{384,256},{4... | collective-permute-start | bytes 2359304 | tf_op jit(solution)/shard_map/ppermute | solution.py:264
  67.0 12.1 %collective-permute-start.10 = (bf16[2,1536,128]{2,1,0:T(8,128)(2,1)}, bf16[2,1536,128]{2,1,0:T(8,128)(2,1)S(1)}, u32[]{:S(2)}, u32[]{:S(2)}) collective-permute-start(bf16[2,1536,128]{2,1,0:T(8,128)(2,1)} %collective-permute-done.refs_3_), channel_id=1, source_target_pairs={{0,64},{64,0},{128,192},{192,128},{256,320},{320,256},{384,448},{4... | collective-permute-start | bytes 2359304 | tf_op jit(solution)/shard_map/ppermute | solution.py:264
  70.2 8.9 %collective-permute-start.13 = (bf16[2,1536,128]{2,1,0:T(8,128)(2,1)S(1)}, bf16[2,1536,128]{2,1,0:T(8,128)(2,1)S(1)}, u32[]{:S(2)}, u32[]{:S(2)}) collective-permute-start(bf16[2,1536,128]{2,1,0:T(8,128)(2,1)S(1)} %collective-permute-done.5.refs_6_), channel_id=1, source_target_pairs={{0,64},{64,0},{128,192},{192,128},{256,320},{320,256},{384,448},{4... | collective-permute-start | bytes 2359304 | tf_op jit(solution)/shard_map/ppermute | solution.py:264
  72.2 7.0 %collective-permute-start.11 = (bf16[2,1536,128]{2,1,0:T(8,128)(2,1)S(1)}, bf16[2,1536,128]{2,1,0:T(8,128)(2,1)S(1)}, u32[]{:S(2)}, u32[]{:S(2)}) collective-permute-start(bf16[2,1536,128]{2,1,0:T(8,128)(2,1)S(1)} %collective-permute-done.6.refs_4_), channel_id=1, source_target_pairs={{0,64},{64,0},{128,192},{192,128},{256,320},{320,256},{384,448},{4... | collective-permute-start | bytes 2359304 | tf_op jit(solution)/shard_map/ppermute | solution.py:264
  74.6 4.6 %collective-permute-start.14 = (bf16[2,1536,128]{2,1,0:T(8,128)(2,1)S(1)}, bf16[2,1536,128]{2,1,0:T(8,128)(2,1)S(1)}, u32[]{:S(2)}, u32[]{:S(2)}) collective-permute-start(bf16[2,1536,128]{2,1,0:T(8,128)(2,1)S(1)} %collective-permute-done.8.refs_7_), channel_id=1, source_target_pairs={{0,64},{64,0},{128,192},{192,128},{256,320},{320,256},{384,448},{4... | collective-permute-start | bytes 2359304 | tf_op jit(solution)/shard_map/ppermute | solution.py:264
  76.5 4.3 %collective-permute-start.12 = (bf16[2,1536,128]{2,1,0:T(8,128)(2,1)S(1)}, bf16[2,1536,128]{2,1,0:T(8,128)(2,1)S(1)}, u32[]{:S(2)}, u32[]{:S(2)}) collective-permute-start(bf16[2,1536,128]{2,1,0:T(8,128)(2,1)S(1)} %collective-permute-done.7.refs_5_), channel_id=1, source_target_pairs={{0,64},{64,0},{128,192},{192,128},{256,320},{320,256},{384,448},{4... | collective-permute-start | bytes 2359304 | tf_op jit(solution)/shard_map/ppermute | solution.py:264

commit v5 on v4

--- a/solution.py
+++ b/solution.py
@@ -267,6 +267,9 @@
     from_below = move(own_a, up)
     from_above = move(own_b, down)
 
+    coefficients, neighbours, own_b = lax.optimization_barrier(
+        (coefficients, neighbours, own_b)
+    )
     near = jnp.pad(neighbours.astype(BF), ((0, EDGE - 4), (0, NB - 27)))
     turned = turn(coefficients, near)
     groups = [[2 * z + c for z in range(4)] for c in range(2)]
@@ -274,13 +277,13 @@
     y_other = move(y_own, over_core)
 
     own_swapped = [move(own_a, over_core), move(own_b, over_core)]
-    from_above, y_other, own_swapped = lax.optimization_barrier(
-        (from_above, y_other, own_swapped)
-    )
+    from_above, own_swapped = lax.optimization_barrier((from_above, own_swapped))
     far_a = move(from_below, up)
     far_b = move(from_above, down)
     below_b = move(from_below, over_x)
-    above_a = move(from_above, over_y)
+    below_swapped = move(from_below, over_core)
+    for_y, below_swapped = lax.optimization_barrier((from_above, below_swapped))
+    above_a = move(for_y, over_y)
 
 
     def table(y):
@@ -291,7 +294,7 @@
 
     ids, below_b = lax.optimization_barrier((ids, below_b))
     pieces = [own_a, own_b, from_below, from_above, far_a, far_b, below_b, above_a]
-    swapped = own_swapped + [move(piece, over_core) for piece in pieces[2:]]
+    swapped = own_swapped + [below_swapped] + [move(piece, over_core) for piece in pieces[3:]]
 
     filtered, partial = filtering(ids, pieces + swapped, y_own, y_other, basis_values)
     points = POINTS // nbands

time: 128 us -> 132 us (1.031)
  waiting for transfers between devices: 17.3 us -> 23.2 us
  blocking collectives: 28.6 us -> 26.2 us
  starting transfers between devices: 55.1 us -> 57.3 us
    ppermute x15, waiting for transfers between devices: 17.3 us -> 23.2 us  [move(): return lax.ppermute(value, both, pairs)]
    all_to_all x1, blocking collectives: 28.6 us -> 26.2 us  [local(): lax.all_to_all(parts.reshape(nbands, points // 32, 128), 'band', 0, 0)]
    ppermute x15, starting transfers between devices: 47.3 us -> 49.1 us  [move(): return lax.ppermute(value, both, pairs)]
  transfers between devices with their start and end apart: 16 -> 16, of which waited for: 3 -> 4; matrix products, arithmetic and copies ran while one was open for 0% -> 0% of each run, Pallas kernels for 2% -> 1%
where the time goes in v5:
time: 132 us; the launch traced here: 131 us
  starting transfers between devices  57.3 us (43%)
  blocking collectives  26.2 us (20%)
  waiting for transfers between devices  23.2 us (18%)
  Pallas kernels  19.6 us (15%)
  local copies, waits for them, and re-layouts  3.7 us (3%)
    ppermute x15, starting transfers between devices, move(): return lax.ppermute(value, both, pairs)  49.1 us
    all_to_all x1, blocking collectives, local(): lax.all_to_all(parts.reshape(nbands, points // 32, 128), 'band', 0, 0)  26.2 us
    ppermute x15, waiting for transfers between devices, move(): return lax.ppermute(value, both, pairs)  23.2 us
    pallas_call x1, Pallas kernels, filtering(): pl.pallas_call(filter_kernel, out_shape=(jax.ShapeDtypeStruct((4, NB, NB)...  16.5 us
    all_to_all x1, starting transfers between devices, local(): y_own = lax.all_to_all(turned, 'elem', 0, 0, axis_index_groups=groups)  8.19 us
    unnamed x6, local copies, waits for them, and re-layouts  2.68 us
  transfers between devices with their start and end apart: 16, of which 4 were waited for; matrix products, arithmetic and copies ran while one was open for 0% of the time, Pallas kernels for 1%

profile of v5, /device:TPU:1, one launch (start us, length us, event | category | flops | bytes accessed | tf_op | source)
XLA Modules:
  0.0 131.1 jit_solution(1848586336524661439)
XLA Ops:
  0.7 0.0 copy-start
  0.7 2.0 %copy-done = bf16[4,27,128,128]{3,2,1,0:T(8,128)(2,1)S(1)} copy-done((bf16[4,27,128,128]{3,2,1,0:T(8,128)(2,1)S(1)}, bf16[4,27,128,128]{3,2,1,0:T(8,128)(2,1)}, u32[]{:S(2)}) %copy-start) | copy-done | bytes 3538968
  2.7 0.0 copy-start.2
  2.7 0.7 copy-done.2
  3.4 0.0 copy-start.1
  3.4 2.2 %shard_map.59 = (bf16[2,1536,128]{2,1,0:T(8,128)(2,1)S(1)}, bf16[2,1536,128]{2,1,0:T(8,128)(2,1)S(1)}) custom-call(s32[1]{0:T(128)} %bitcast.pair_ref, s32[4,27]{1,0:T(4,128)S(1)} %copy-done.2, bf16[4,27,128,128]{3,2,1,0:T(8,128)(2,1)S(1)} %copy-done, bf16[4,27,128,128]{3,2,1,0:T(8,128)(2,1)S(1)} %copy-done, bf16[4,27,128,128]{3,2,1,0:T(8,128)(2,1)S(1)} %copy-done), custom_call_target="tpu_custom_call" | custom-call | flops 452984832 | bytes 5200000 | tf_op jit(solution)/shard_map/pallas_call | solution.py:66
  5.6 4.8 %collective-permute-start.1 = (bf16[2,1536,128]{2,1,0:T(8,128)(2,1)S(1)}, bf16[2,1536,128]{2,1,0:T(8,128)(2,1)S(1)}, u32[]{:S(2)}, u32[]{:S(2)}) collective-permute-start(bf16[2,1536,128]{2,1,0:T(8,128)(2,1)S(1)} %get-tuple-element.19.refs_0_), channel_id=1, source_target_pairs={{0,128},{64,192},{128,256},{192,320},{256,384},{320,448},{384,4},{... | collective-permute-start | bytes 2359304 | tf_op jit(solution)/shard_map/ppermute | solution.py:264
  10.5 0.0 copy-done.1
  10.5 0.9 shard_map.60
  11.4 8.2 %all-to-all-start = ((bf16[4,528,128]{2,1,0:T(8,128)(2,1)}), bf16[4,528,128]{2,1,0:T(8,128)(2,1)S(1)}, u32[]{:S(2)}, u32[]{:S(2)}) async-start(bf16[4,528,128]{2,1,0:T(8,128)(2,1)} %shard_map.60), calls=%async_computation | async-start | bytes 1081344 | tf_op jit(solution)/shard_map/all_to_all | solution.py:276
  19.6 3.1 %collective-permute-start.5 = (bf16[2,1536,128]{2,1,0:T(8,128)(2,1)S(1)}, bf16[2,1536,128]{2,1,0:T(8,128)(2,1)}, u32[]{:S(2)}, u32[]{:S(2)}) collective-permute-start(bf16[2,1536,128]{2,1,0:T(8,128)(2,1)S(1)} %get-tuple-element.21.refs_1_), channel_id=1, source_target_pairs={{0,64},{64,0},{128,192},{192,128},{256,320},{320,256},{384,448},{4... | collective-permute-start | bytes 2359304 | tf_op jit(solution)/shard_map/ppermute | solution.py:264
  22.7 5.5 %collective-permute-start.3 = (bf16[2,1536,128]{2,1,0:T(8,128)(2,1)S(1)}, bf16[2,1536,128]{2,1,0:T(8,128)(2,1)}, u32[]{:S(2)}, u32[]{:S(2)}) collective-permute-start(bf16[2,1536,128]{2,1,0:T(8,128)(2,1)S(1)} %get-tuple-element.21.refs_1_), channel_id=1, source_target_pairs={{0,388},{64,452},{128,0},{192,64},{256,128},{320,192},{384,256},{4... | collective-permute-start | bytes 2359304 | tf_op jit(solution)/shard_map/ppermute | solution.py:264
  28.2 2.2 %collective-permute-start.4 = (bf16[2,1536,128]{2,1,0:T(8,128)(2,1)S(1)}, bf16[2,1536,128]{2,1,0:T(8,128)(2,1)}, u32[]{:S(2)}, u32[]{:S(2)}) collective-permute-start(bf16[2,1536,128]{2,1,0:T(8,128)(2,1)S(1)} %get-tuple-element.19.refs_0_), channel_id=1, source_target_pairs={{0,64},{64,0},{128,192},{192,128},{256,320},{320,256},{384,448},{4... | collective-permute-start | bytes 2359304 | tf_op jit(solution)/shard_map/ppermute | solution.py:264
  30.4 3.9 %collective-permute-done.1.refs_2_ = bf16[2,1536,128]{2,1,0:T(8,128)(2,1)S(1)} collective-permute-done((bf16[2,1536,128]{2,1,0:T(8,128)(2,1)S(1)}, bf16[2,1536,128]{2,1,0:T(8,128)(2,1)S(1)}, u32[]{:S(2)}, u32[]{:S(2)}) %collective-permute-start.1) | collective-permute-done | bytes 786464 | tf_op jit(solution)/shard_map/ppermute | solution.py:264
  34.4 3.1 %collective-permute-start.8 = (bf16[2,1536,128]{2,1,0:T(8,128)(2,1)S(1)}, bf16[2,1536,128]{2,1,0:T(8,128)(2,1)}, u32[]{:S(2)}, u32[]{:S(2)}) collective-permute-start(bf16[2,1536,128]{2,1,0:T(8,128)(2,1)S(1)} %collective-permute-done.1.refs_2_), channel_id=1, source_target_pairs={{0,64},{64,0},{128,192},{192,128},{256,320},{320,256},{384,448},{4... | collective-permute-start | bytes 2359304 | tf_op jit(solution)/shard_map/ppermute | solution.py:264
  37.5 0.0 all-to-all-done.refs_16_
  37.5 1.9 %collective-permute-start = (bf16[4,528,128]{2,1,0:T(8,128)(2,1)S(1)}, bf16[4,528,128]{2,1,0:T(8,128)(2,1)S(1)}, u32[]{:S(2)}, u32[]{:S(2)}) collective-permute-start(bf16[4,528,128]{2,1,0:T(8,128)(2,1)S(1)} %all-to-all-done.refs_16_), channel_id=1, source_target_pairs={{0,64},{64,0},{128,192},{192,128},{256,320},{320,256},{384,448},{4... | collective-permute-start | bytes 1622024 | tf_op jit(solution)/shard_map/ppermute | solution.py:264
  39.4 0.0 collective-permute-done.5.refs_9_
  39.5 8.7 %collective-permute-done.3.refs_3_ = bf16[2,1536,128]{2,1,0:T(8,128)(2,1)} collective-permute-done((bf16[2,1536,128]{2,1,0:T(8,128)(2,1)S(1)}, bf16[2,1536,128]{2,1,0:T(8,128)(2,1)}, u32[]{:S(2)}, u32[]{:S(2)}) %collective-permute-start.3) | collective-permute-done | bytes 786464 | tf_op jit(solution)/shard_map/ppermute | solution.py:264
  48.1 0.0 collective-permute-done.4.refs_8_
  48.1 4.4 %collective-permute-start.7 = (bf16[2,1536,128]{2,1,0:T(8,128)(2,1)}, bf16[2,1536,128]{2,1,0:T(8,128)(2,1)S(1)}, u32[]{:S(2)}, u32[]{:S(2)}) collective-permute-start(bf16[2,1536,128]{2,1,0:T(8,128)(2,1)} %collective-permute-done.3.refs_3_), channel_id=1, source_target_pairs={{0,388},{64,452},{128,0},{192,64},{256,128},{320,192},{384,256},{4... | collective-permute-start | bytes 2359304 | tf_op jit(solution)/shard_map/ppermute | solution.py:264
  52.5 2.5 %collective-permute-start.6 = (bf16[2,1536,128]{2,1,0:T(8,128)(2,1)S(1)}, bf16[2,1536,128]{2,1,0:T(8,128)(2,1)S(1)}, u32[]{:S(2)}, u32[]{:S(2)}) collective-permute-start(bf16[2,1536,128]{2,1,0:T(8,128)(2,1)S(1)} %collective-permute-done.1.refs_2_), channel_id=1, source_target_pairs={{0,128},{64,192},{128,256},{192,320},{256,384},{320,448},{384,4},{... | collective-permute-start | bytes 2359304 | tf_op jit(solution)/shard_map/ppermute | solution.py:264
  55.0 3.1 %collective-permute-start.2 = (bf16[2,1536,128]{2,1,0:T(8,128)(2,1)S(1)}, bf16[2,1536,128]{2,1,0:T(8,128)(2,1)S(1)}, u32[]{:S(2)}, u32[]{:S(2)}) collective-permute-start(bf16[2,1536,128]{2,1,0:T(8,128)(2,1)S(1)} %collective-permute-done.1.refs_2_), channel_id=1, source_target_pairs={{0,1},{64,65},{128,129},{192,193},{256,257},{320,321},{384,385},{4... | collective-permute-start | bytes 2359304 | tf_op jit(solution)/shard_map/ppermute | solution.py:264
  58.1 0.0 collective-permute-done.8.refs_10_
  58.1 3.2 %collective-permute-start.9 = (bf16[2,1536,128]{2,1,0:T(8,128)(2,1)}, bf16[2,1536,128]{2,1,0:T(8,128)(2,1)S(1)}, u32[]{:S(2)}, u32[]{:S(2)}) collective-permute-start(bf16[2,1536,128]{2,1,0:T(8,128)(2,1)} %collective-permute-done.3.refs_3_), channel_id=1, source_target_pairs={{0,8},{64,72},{128,136},{192,200},{256,264},{320,328},{384,392},{4... | collective-permute-start | bytes 2359304 | tf_op jit(solution)/shard_map/ppermute | solution.py:264
  61.3 0.0 collective-permute-done.refs_17_
  61.4 4.2 %collective-permute-start.10 = (bf16[2,1536,128]{2,1,0:T(8,128)(2,1)}, bf16[2,1536,128]{2,1,0:T(8,128)(2,1)S(1)}, u32[]{:S(2)}, u32[]{:S(2)}) collective-permute-start(bf16[2,1536,128]{2,1,0:T(8,128)(2,1)} %collective-permute-done.3.refs_3_), channel_id=1, source_target_pairs={{0,64},{64,0},{128,192},{192,128},{256,320},{320,256},{384,448},{4... | collective-permute-start | bytes 2359304 | tf_op jit(solution)/shard_map/ppermute | solution.py:264
  65.6 8.5 %collective-permute-done.2.refs_6_ = bf16[2,1536,128]{2,1,0:T(8,128)(2,1)S(1)} collective-permute-done((bf16[2,1536,128]{2,1,0:T(8,128)(2,1)S(1)}, bf16[2,1536,128]{2,1,0:T(8,128)(2,1)S(1)}, u32[]{:S(2)}, u32[]{:S(2)}) %collective-permute-start.2) | collective-permute-done | bytes 786464 | tf_op jit(solution)/shard_map/ppermute | solution.py:264
  74.2 4.6 %collective-permute-start.13 = (bf16[2,1536,128]{2,1,0:T(8,128)(2,1)S(1)}, bf16[2,1536,128]{2,1,0:T(8,128)(2,1)S(1)}, u32[]{:S(2)}, u32[]{:S(2)}) collective-permute-start(bf16[2,1536,128]{2,1,0:T(8,128)(2,1)S(1)} %collective-permute-done.2.refs_6_), channel_id=1, source_target_pairs={{0,64},{64,0},{128,192},{192,128},{256,320},{320,256},{384,448},{4... | collective-permute-start | bytes 2359304 | tf_op jit(solution)/shard_map/ppermute | solution.py:264
  78.7 0.0 collective-permute-done.7.refs_5_
  78.8 1.9 %collective-permute-start.12 = (bf16[2,1536,128]{2,1,0:T(8,128)(2,1)S(1)}, bf16[2,1536,128]{2,1,0:T(8,128)(2,1)S(1)}, u32[]{:S(2)}, u32[]{:S(2)}) collective-permute-start(bf16[2,1536,128]{2,1,0:T(8,128)(2,1)S(1)} %collective-permute-done.7.refs_5_), channel_id=1, source_target_pairs={{0,64},{64,0},{128,192},{192,128},{256,320},{320,256},{384,448},{4... | collective-permute-start | bytes 2359304 | tf_op jit(solution)/shard_map/ppermute | solution.py:264
  80.7 0.0 collective-permute-done.6.refs_4_
  80.7 2.4 %collective-permute-start.11 = (bf16[2,1536,128]{2,1,0:T(8,128)(2,1)S(1)}, bf16[2,1536,128]{2,1,0:T(8,128)(2,1)S(1)}, u32[]{:S(2)}, u32[]{:S(2)}) collective-permute-start(bf16[2,1536,128]{2,1,0:T(8,128)(2,1)S(1)} %collective-permute-done.6.refs_4_), channel_id=1, source_target_pairs={{0,64},{64,0},{128,192},{192,128},{256,320},{320,256},{384,448},{4... | collective-permute-start | bytes 2359304 | tf_op jit(solution)/shard_map/ppermute | solution.py:264
  83.1 0.0 collective-permute-done.9.refs_7_
  83.1 2.1 %collective-permute-start.14 = (bf16[2,1536,128]{2,1,0:T(8,128)(2,1)S(1)}, bf16[2,1536,128]{2,1,0:T(8,128)(2,1)S(1)}, u32[]{:S(2)}, u32[]{:S(2)}) collective-permute-start(bf16[2,1536,128]{2,1,0:T(8,128)(2,1)S(1)} %collective-permute-done.9.refs_7_), channel_id=1, source_target_pairs={{0,64},{64,0},{128,192},{192,128},{256,320},{320,256},{384,448},{4... | collective-permute-start | bytes 2359304 | tf_op jit(solution)/shard_map/ppermute | solution.py:264
  85.2 0.0 collective-permute-done.10.refs_11_
  85.2 0.0 collective-permute-done.12.refs_13_
  85.2 0.0 collective-permute-done.11.refs_12_
  85.3 0.0 collective-permute-done.13.refs_14_
  85.3 2.0 %collective-permute-done.14.refs_15_ = bf16[2,1536,128]{2,1,0:T(8,128)(2,1)S(1)} collective-permute-done((bf16[2,1536,128]{2,1,0:T(8,128)(2,1)S(1)}, bf16[2,1536,128]{2,1,0:T(8,128)(2,1)S(1)}, u32[]{:S(2)}, u32[]{:S(2)}) %collective-permute-start.14) | collective-permute-done | bytes 786464 | tf_op jit(solution)/shard_map/ppermute | solution.py:264
  87.3 16.5 %shard_map.61 = (bf16[4,128,128]{2,1,0:T(8,128)(2,1)}, f32[4,4096]{1,0:T(4,128)S(1)}) custom-call(s32[32,27]{1,0:T(8,128)S(1)} %bitcast.9, bf16[2,1536,128]{2,1,0:T(8,128)(2,1)S(1)} %get-tuple-element.19.refs_0_, bf16[2,1536,128]{2,1,0:T(8,128)(2,1)S(1)} %get-tuple-element.21.refs_1_, bf16[2,1536,128]{2,1,0:T(8,128)(2,1)S(1)} %collective-permute-done.1.refs_2_, ...), custom_call_target="tpu_custom_call" | custom-call | tf_op jit(solution)/shard_map/pallas_call | solution.py:204
  103.8 0.1 reshape.17
  103.9 0.1 copy.9
  104.0 0.1 reshape.18
  104.1 26.2 %all_to_all.10 = f32[64,2,128]{2,1,0:T(2,128)S(1)} all-to-all(f32[64,2,128]{2,1,0:T(2,128)S(1)} %reshape.18), channel_id=1, replica_groups=mesh['elem'=8,'band'=64] {'band'}, dimensions={0} | all-to-all | bytes 131072 | tf_op jit(solution)/shard_map/all_to_all | solution.py:302
  130.4 0.1 reduce_sum.9
  130.4 0.7 reshape.19
  (7 shorter events, 0.0 us)
Async XLA Ops:
  0.7 2.0 %copy-start = (bf16[4,27,128,128]{3,2,1,0:T(8,128)(2,1)S(1)}, bf16[4,27,128,128]{3,2,1,0:T(8,128)(2,1)}, u32[]{:S(2)}) copy-start(bf16[4,27,128,128]{3,2,1,0:T(8,128)(2,1)} %h2_ref.1) | copy-start | bytes 10616836
  2.7 0.7 copy-start.2
  3.4 7.1 %copy-start.1 = (bf16[4,128,128]{2,1,0:T(8,128)(2,1)S(1)}, bf16[4,128,128]{2,1,0:T(8,128)(2,1)}, u32[]{:S(2)}) copy-start(bf16[4,128,128]{2,1,0:T(8,128)(2,1)} %y_ref) | copy-start | bytes 393220
  5.6 28.8 %collective-permute-start.1 = (bf16[2,1536,128]{2,1,0:T(8,128)(2,1)S(1)}, bf16[2,1536,128]{2,1,0:T(8,128)(2,1)S(1)}, u32[]{:S(2)}, u32[]{:S(2)}) collective-permute-start(bf16[2,1536,128]{2,1,0:T(8,128)(2,1)S(1)} %get-tuple-element.19.refs_0_), channel_id=1, source_target_pairs={{0,128},{64,192},{128,256},{192,320},{256,384},{320,448},{384,4},{... | collective-permute-start | bytes 2359304 | tf_op jit(solution)/shard_map/ppermute | solution.py:264
  11.4 26.1 %all-to-all-start = ((bf16[4,528,128]{2,1,0:T(8,128)(2,1)}), bf16[4,528,128]{2,1,0:T(8,128)(2,1)S(1)}, u32[]{:S(2)}, u32[]{:S(2)}) async-start(bf16[4,528,128]{2,1,0:T(8,128)(2,1)} %shard_map.60), calls=%async_computation | async-start | bytes 1081344 | tf_op jit(solution)/shard_map/all_to_all | solution.py:276
  19.6 19.9 %collective-permute-start.5 = (bf16[2,1536,128]{2,1,0:T(8,128)(2,1)S(1)}, bf16[2,1536,128]{2,1,0:T(8,128)(2,1)}, u32[]{:S(2)}, u32[]{:S(2)}) collective-permute-start(bf16[2,1536,128]{2,1,0:T(8,128)(2,1)S(1)} %get-tuple-element.21.refs_1_), channel_id=1, source_target_pairs={{0,64},{64,0},{128,192},{192,128},{256,320},{320,256},{384,448},{4... | collective-permute-start | bytes 2359304 | tf_op jit(solution)/shard_map/ppermute | solution.py:264
  22.7 25.4 %collective-permute-start.3 = (bf16[2,1536,128]{2,1,0:T(8,128)(2,1)S(1)}, bf16[2,1536,128]{2,1,0:T(8,128)(2,1)}, u32[]{:S(2)}, u32[]{:S(2)}) collective-permute-start(bf16[2,1536,128]{2,1,0:T(8,128)(2,1)S(1)} %get-tuple-element.21.refs_1_), channel_id=1, source_target_pairs={{0,388},{64,452},{128,0},{192,64},{256,128},{320,192},{384,256},{4... | collective-permute-start | bytes 2359304 | tf_op jit(solution)/shard_map/ppermute | solution.py:264
  28.2 19.9 %collective-permute-start.4 = (bf16[2,1536,128]{2,1,0:T(8,128)(2,1)S(1)}, bf16[2,1536,128]{2,1,0:T(8,128)(2,1)}, u32[]{:S(2)}, u32[]{:S(2)}) collective-permute-start(bf16[2,1536,128]{2,1,0:T(8,128)(2,1)S(1)} %get-tuple-element.19.refs_0_), channel_id=1, source_target_pairs={{0,64},{64,0},{128,192},{192,128},{256,320},{320,256},{384,448},{4... | collective-permute-start | bytes 2359304 | tf_op jit(solution)/shard_map/ppermute | solution.py:264
  34.4 23.8 %collective-permute-start.8 = (bf16[2,1536,128]{2,1,0:T(8,128)(2,1)S(1)}, bf16[2,1536,128]{2,1,0:T(8,128)(2,1)}, u32[]{:S(2)}, u32[]{:S(2)}) collective-permute-start(bf16[2,1536,128]{2,1,0:T(8,128)(2,1)S(1)} %collective-permute-done.1.refs_2_), channel_id=1, source_target_pairs={{0,64},{64,0},{128,192},{192,128},{256,320},{320,256},{384,448},{4... | collective-permute-start | bytes 2359304 | tf_op jit(solution)/shard_map/ppermute | solution.py:264
  37.5 23.8 %collective-permute-start = (bf16[4,528,128]{2,1,0:T(8,128)(2,1)S(1)}, bf16[4,528,128]{2,1,0:T(8,128)(2,1)S(1)}, u32[]{:S(2)}, u32[]{:S(2)}) collective-permute-start(bf16[4,528,128]{2,1,0:T(8,128)(2,1)S(1)} %all-to-all-done.refs_16_), channel_id=1, source_target_pairs={{0,64},{64,0},{128,192},{192,128},{256,320},{320,256},{384,448},{4... | collective-permute-start | bytes 1622024 | tf_op jit(solution)/shard_map/ppermute | solution.py:264
  48.1 30.6 %collective-permute-start.7 = (bf16[2,1536,128]{2,1,0:T(8,128)(2,1)}, bf16[2,1536,128]{2,1,0:T(8,128)(2,1)S(1)}, u32[]{:S(2)}, u32[]{:S(2)}) collective-permute-start(bf16[2,1536,128]{2,1,0:T(8,128)(2,1)} %collective-permute-done.3.refs_3_), channel_id=1, source_target_pairs={{0,388},{64,452},{128,0},{192,64},{256,128},{320,192},{384,256},{4... | collective-permute-start | bytes 2359304 | tf_op jit(solution)/shard_map/ppermute | solution.py:264
  52.5 28.2 %collective-permute-start.6 = (bf16[2,1536,128]{2,1,0:T(8,128)(2,1)S(1)}, bf16[2,1536,128]{2,1,0:T(8,128)(2,1)S(1)}, u32[]{:S(2)}, u32[]{:S(2)}) collective-permute-start(bf16[2,1536,128]{2,1,0:T(8,128)(2,1)S(1)} %collective-permute-done.1.refs_2_), channel_id=1, source_target_pairs={{0,128},{64,192},{128,256},{192,320},{256,384},{320,448},{384,4},{... | collective-permute-start | bytes 2359304 | tf_op jit(solution)/shard_map/ppermute | solution.py:264
  55.0 19.2 %collective-permute-start.2 = (bf16[2,1536,128]{2,1,0:T(8,128)(2,1)S(1)}, bf16[2,1536,128]{2,1,0:T(8,128)(2,1)S(1)}, u32[]{:S(2)}, u32[]{:S(2)}) collective-permute-start(bf16[2,1536,128]{2,1,0:T(8,128)(2,1)S(1)} %collective-permute-done.1.refs_2_), channel_id=1, source_target_pairs={{0,1},{64,65},{128,129},{192,193},{256,257},{320,321},{384,385},{4... | collective-permute-start | bytes 2359304 | tf_op jit(solution)/shard_map/ppermute | solution.py:264
  58.1 25.0 %collective-permute-start.9 = (bf16[2,1536,128]{2,1,0:T(8,128)(2,1)}, bf16[2,1536,128]{2,1,0:T(8,128)(2,1)S(1)}, u32[]{:S(2)}, u32[]{:S(2)}) collective-permute-start(bf16[2,1536,128]{2,1,0:T(8,128)(2,1)} %collective-permute-done.3.refs_3_), channel_id=1, source_target_pairs={{0,8},{64,72},{128,136},{192,200},{256,264},{320,328},{384,392},{4... | collective-permute-start | bytes 2359304 | tf_op jit(solution)/shard_map/ppermute | solution.py:264
  61.4 23.9 %collective-permute-start.10 = (bf16[2,1536,128]{2,1,0:T(8,128)(2,1)}, bf16[2,1536,128]{2,1,0:T(8,128)(2,1)S(1)}, u32[]{:S(2)}, u32[]{:S(2)}) collective-permute-start(bf16[2,1536,128]{2,1,0:T(8,128)(2,1)} %collective-permute-done.3.refs_3_), channel_id=1, source_target_pairs={{0,64},{64,0},{128,192},{192,128},{256,320},{320,256},{384,448},{4... | collective-permute-start | bytes 2359304 | tf_op jit(solution)/shard_map/ppermute | solution.py:264
  74.2 11.1 %collective-permute-start.13 = (bf16[2,1536,128]{2,1,0:T(8,128)(2,1)S(1)}, bf16[2,1536,128]{2,1,0:T(8,128)(2,1)S(1)}, u32[]{:S(2)}, u32[]{:S(2)}) collective-permute-start(bf16[2,1536,128]{2,1,0:T(8,128)(2,1)S(1)} %collective-permute-done.2.refs_6_), channel_id=1, source_target_pairs={{0,64},{64,0},{128,192},{192,128},{256,320},{320,256},{384,448},{4... | collective-permute-start | bytes 2359304 | tf_op jit(solution)/shard_map/ppermute | solution.py:264
  78.8 6.5 %collective-permute-start.12 = (bf16[2,1536,128]{2,1,0:T(8,128)(2,1)S(1)}, bf16[2,1536,128]{2,1,0:T(8,128)(2,1)S(1)}, u32[]{:S(2)}, u32[]{:S(2)}) collective-permute-start(bf16[2,1536,128]{2,1,0:T(8,128)(2,1)S(1)} %collective-permute-done.7.refs_5_), channel_id=1, source_target_pairs={{0,64},{64,0},{128,192},{192,128},{256,320},{320,256},{384,448},{4... | collective-permute-start | bytes 2359304 | tf_op jit(solution)/shard_map/ppermute | solution.py:264
  80.7 4.6 %collective-permute-start.11 = (bf16[2,1536,128]{2,1,0:T(8,128)(2,1)S(1)}, bf16[2,1536,128]{2,1,0:T(8,128)(2,1)S(1)}, u32[]{:S(2)}, u32[]{:S(2)}) collective-permute-start(bf16[2,1536,128]{2,1,0:T(8,128)(2,1)S(1)} %collective-permute-done.6.refs_4_), channel_id=1, source_target_pairs={{0,64},{64,0},{128,192},{192,128},{256,320},{320,256},{384,448},{4... | collective-permute-start | bytes 2359304 | tf_op jit(solution)/shard_map/ppermute | solution.py:264
  83.1 4.2 %collective-permute-start.14 = (bf16[2,1536,128]{2,1,0:T(8,128)(2,1)S(1)}, bf16[2,1536,128]{2,1,0:T(8,128)(2,1)S(1)}, u32[]{:S(2)}, u32[]{:S(2)}) collective-permute-start(bf16[2,1536,128]{2,1,0:T(8,128)(2,1)S(1)} %collective-permute-done.9.refs_7_), channel_id=1, source_target_pairs={{0,64},{64,0},{128,192},{192,128},{256,320},{320,256},{384,448},{4... | collective-permute-start | bytes 2359304 | tf_op jit(solution)/shard_map/ppermute | solution.py:264

commit v6 on v4

--- a/solution.py
+++ b/solution.py
@@ -274,13 +274,16 @@
     y_other = move(y_own, over_core)
 
     own_swapped = [move(own_a, over_core), move(own_b, over_core)]
+    from_below, y_other = lax.optimization_barrier((from_below, y_other))
     from_above, y_other, own_swapped = lax.optimization_barrier(
         (from_above, y_other, own_swapped)
     )
     far_a = move(from_below, up)
     far_b = move(from_above, down)
     below_b = move(from_below, over_x)
-    above_a = move(from_above, over_y)
+    below_swapped = move(from_below, over_core)
+    for_y, below_swapped = lax.optimization_barrier((from_above, below_swapped))
+    above_a = move(for_y, over_y)
 
 
     def table(y):
@@ -291,7 +294,7 @@
 
     ids, below_b = lax.optimization_barrier((ids, below_b))
     pieces = [own_a, own_b, from_below, from_above, far_a, far_b, below_b, above_a]
-    swapped = own_swapped + [move(piece, over_core) for piece in pieces[2:]]
+    swapped = own_swapped + [below_swapped] + [move(piece, over_core) for piece in pieces[3:]]
 
     filtered, partial = filtering(ids, pieces + swapped, y_own, y_other, basis_values)
     points = POINTS // nbands

time: 128 us -> 129 us (level)
  starting transfers between devices: 55.1 us -> 60 us
  blocking collectives: 28.6 us -> 24.5 us
    all_to_all x1, waiting for transfers between devices: 0.01 us -> 5.2 us  [local(): y_own = lax.all_to_all(turned, 'elem', 0, 0, axis_index_groups=groups)]
    ppermute x15, starting transfers between devices: 47.3 us -> 52.2 us  [move(): return lax.ppermute(value, both, pairs)]
    ppermute x15, waiting for transfers between devices: 17.3 us -> 12.7 us  [move(): return lax.ppermute(value, both, pairs)]
    all_to_all x1, blocking collectives: 28.6 us -> 24.5 us  [local(): lax.all_to_all(parts.reshape(nbands, points // 32, 128), 'band', 0, 0)]
  transfers between devices with their start and end apart: 16 -> 16, of which waited for: 3 -> 5; matrix products, arithmetic and copies ran while one was open for 0% -> 0% of each run, Pallas kernels for 2% -> 2%
where the time goes in v6:
time: 129 us; the launch traced here: 128 us
  starting transfers between devices  60 us (47%)
  blocking collectives  24.5 us (19%)
  Pallas kernels  19.6 us (15%)
  waiting for transfers between devices  17.9 us (14%)
  local copies, waits for them, and re-layouts  4.61 us (4%)
    ppermute x15, starting transfers between devices, move(): return lax.ppermute(value, both, pairs)  52.2 us
    all_to_all x1, blocking collectives, local(): lax.all_to_all(parts.reshape(nbands, points // 32, 128), 'band', 0, 0)  24.5 us
    pallas_call x1, Pallas kernels, filtering(): pl.pallas_call(filter_kernel, out_shape=(jax.ShapeDtypeStruct((4, NB, NB)...  16.5 us
    ppermute x15, waiting for transfers between devices, move(): return lax.ppermute(value, both, pairs)  12.7 us
    all_to_all x1, starting transfers between devices, local(): y_own = lax.all_to_all(turned, 'elem', 0, 0, axis_index_groups=groups)  7.81 us
    all_to_all x1, waiting for transfers between devices, local(): y_own = lax.all_to_all(turned, 'elem', 0, 0, axis_index_groups=groups)  5.2 us
    unnamed x6, local copies, waits for them, and re-layouts  3.58 us
  transfers between devices with their start and end apart: 16, of which 5 were waited for; matrix products, arithmetic and copies ran while one was open for 0% of the time, Pallas kernels for 2%

profile of v6, /device:TPU:1, one launch (start us, length us, event | category | flops | bytes accessed | tf_op | source)
XLA Modules:
  0.0 128.3 jit_solution(6149664094540294974)
XLA Ops:
  0.6 0.7 convert_element_type.4
  1.3 0.0 copy-start.1
  1.3 0.9 copy-done.1
  2.2 0.9 shard_map.59
  3.1 7.8 %all-to-all-start = ((bf16[4,528,128]{2,1,0:T(8,128)(2,1)}), bf16[4,528,128]{2,1,0:T(8,128)(2,1)S(1)}, u32[]{:S(2)}, u32[]{:S(2)}) async-start(bf16[4,528,128]{2,1,0:T(8,128)(2,1)} %shard_map.59), calls=%async_computation | async-start | bytes 1081344 | tf_op jit(solution)/shard_map/all_to_all | solution.py:273
  10.9 0.0 copy-start
  10.9 2.0 %copy-done = bf16[4,27,128,128]{3,2,1,0:T(8,128)(2,1)S(1)} copy-done((bf16[4,27,128,128]{3,2,1,0:T(8,128)(2,1)S(1)}, bf16[4,27,128,128]{3,2,1,0:T(8,128)(2,1)}, u32[]{:S(2)}) %copy-start) | copy-done | bytes 3538968
  12.9 0.0 copy-start.2
  12.9 0.7 copy-done.2
  13.6 2.2 %shard_map.60 = (bf16[2,1536,128]{2,1,0:T(8,128)(2,1)S(1)}, bf16[2,1536,128]{2,1,0:T(8,128)(2,1)S(1)}) custom-call(s32[1]{0:T(128)} %bitcast.1.pair_ref, s32[4,27]{1,0:T(4,128)S(1)} %copy-done.2, bf16[4,27,128,128]{3,2,1,0:T(8,128)(2,1)S(1)} %copy-done, bf16[4,27,128,128]{3,2,1,0:T(8,128)(2,1)S(1)} %copy-done, bf16[4,27,128,128]{3,2,1,0:T(8,128)(2,1)S(1)} %copy-done), custom_call_target="tpu_custom_call" | custom-call | flops 452984832 | bytes 5200000 | tf_op jit(solution)/shard_map/pallas_call | solution.py:66
  15.9 3.4 %collective-permute-start.1 = (bf16[2,1536,128]{2,1,0:T(8,128)(2,1)S(1)}, bf16[2,1536,128]{2,1,0:T(8,128)(2,1)S(1)}, u32[]{:S(2)}, u32[]{:S(2)}) collective-permute-start(bf16[2,1536,128]{2,1,0:T(8,128)(2,1)S(1)} %get-tuple-element.17.refs_0_), channel_id=1, source_target_pairs={{0,128},{64,192},{128,256},{192,320},{256,384},{320,448},{384,4},{... | collective-permute-start | bytes 2359304 | tf_op jit(solution)/shard_map/ppermute | solution.py:264
  19.3 5.2 %all-to-all-done.refs_16_ = bf16[4,528,128]{2,1,0:T(8,128)(2,1)S(1)} async-done(((bf16[4,528,128]{2,1,0:T(8,128)(2,1)}), bf16[4,528,128]{2,1,0:T(8,128)(2,1)S(1)}, u32[]{:S(2)}, u32[]{:S(2)}) %all-to-all-start) | async-done | bytes 540704 | tf_op jit(solution)/shard_map/all_to_all | solution.py:273
  24.5 4.2 %collective-permute-start.2 = (bf16[4,528,128]{2,1,0:T(8,128)(2,1)S(1)}, bf16[4,528,128]{2,1,0:T(8,128)(2,1)S(1)}, u32[]{:S(2)}, u32[]{:S(2)}) collective-permute-start(bf16[4,528,128]{2,1,0:T(8,128)(2,1)S(1)} %all-to-all-done.refs_16_), channel_id=1, source_target_pairs={{0,64},{64,0},{128,192},{192,128},{256,320},{320,256},{384,448},{4... | collective-permute-start | bytes 1622024 | tf_op jit(solution)/shard_map/ppermute | solution.py:264
  28.6 1.9 %collective-permute-start.4 = (bf16[2,1536,128]{2,1,0:T(8,128)(2,1)S(1)}, bf16[2,1536,128]{2,1,0:T(8,128)(2,1)}, u32[]{:S(2)}, u32[]{:S(2)}) collective-permute-start(bf16[2,1536,128]{2,1,0:T(8,128)(2,1)S(1)} %get-tuple-element.16.refs_1_), channel_id=1, source_target_pairs={{0,64},{64,0},{128,192},{192,128},{256,320},{320,256},{384,448},{4... | collective-permute-start | bytes 2359304 | tf_op jit(solution)/shard_map/ppermute | solution.py:264
  30.6 7.6 %collective-permute-start = (bf16[2,1536,128]{2,1,0:T(8,128)(2,1)S(1)}, bf16[2,1536,128]{2,1,0:T(8,128)(2,1)}, u32[]{:S(2)}, u32[]{:S(2)}) collective-permute-start(bf16[2,1536,128]{2,1,0:T(8,128)(2,1)S(1)} %get-tuple-element.16.refs_1_), channel_id=1, source_target_pairs={{0,388},{64,452},{128,0},{192,64},{256,128},{320,192},{384,256},{4... | collective-permute-start | bytes 2359304 | tf_op jit(solution)/shard_map/ppermute | solution.py:264
  38.2 2.7 %collective-permute-start.3 = (bf16[2,1536,128]{2,1,0:T(8,128)(2,1)S(1)}, bf16[2,1536,128]{2,1,0:T(8,128)(2,1)}, u32[]{:S(2)}, u32[]{:S(2)}) collective-permute-start(bf16[2,1536,128]{2,1,0:T(8,128)(2,1)S(1)} %get-tuple-element.17.refs_0_), channel_id=1, source_target_pairs={{0,64},{64,0},{128,192},{192,128},{256,320},{320,256},{384,448},{4... | collective-permute-start | bytes 2359304 | tf_op jit(solution)/shard_map/ppermute | solution.py:264
  40.9 0.0 collective-permute-done.1.refs_2_
  40.9 0.0 collective-permute-done.2.refs_17_
  40.9 3.6 %collective-permute-start.8 = (bf16[2,1536,128]{2,1,0:T(8,128)(2,1)S(1)}, bf16[2,1536,128]{2,1,0:T(8,128)(2,1)}, u32[]{:S(2)}, u32[]{:S(2)}) collective-permute-start(bf16[2,1536,128]{2,1,0:T(8,128)(2,1)S(1)} %collective-permute-done.1.refs_2_), channel_id=1, source_target_pairs={{0,64},{64,0},{128,192},{192,128},{256,320},{320,256},{384,448},{4... | collective-permute-start | bytes 2359304 | tf_op jit(solution)/shard_map/ppermute | solution.py:264
  44.5 1.9 %collective-permute-start.6 = (bf16[2,1536,128]{2,1,0:T(8,128)(2,1)S(1)}, bf16[2,1536,128]{2,1,0:T(8,128)(2,1)S(1)}, u32[]{:S(2)}, u32[]{:S(2)}) collective-permute-start(bf16[2,1536,128]{2,1,0:T(8,128)(2,1)S(1)} %collective-permute-done.1.refs_2_), channel_id=1, source_target_pairs={{0,128},{64,192},{128,256},{192,320},{256,384},{320,448},{384,4},{... | collective-permute-start | bytes 2359304 | tf_op jit(solution)/shard_map/ppermute | solution.py:264
  46.4 0.0 collective-permute-done.4.refs_9_
  46.4 3.1 %collective-permute-start.5 = (bf16[2,1536,128]{2,1,0:T(8,128)(2,1)S(1)}, bf16[2,1536,128]{2,1,0:T(8,128)(2,1)S(1)}, u32[]{:S(2)}, u32[]{:S(2)}) collective-permute-start(bf16[2,1536,128]{2,1,0:T(8,128)(2,1)S(1)} %collective-permute-done.1.refs_2_), channel_id=1, source_target_pairs={{0,1},{64,65},{128,129},{192,193},{256,257},{320,321},{384,385},{4... | collective-permute-start | bytes 2359304 | tf_op jit(solution)/shard_map/ppermute | solution.py:264
  49.6 5.0 %collective-permute-done.refs_3_ = bf16[2,1536,128]{2,1,0:T(8,128)(2,1)} collective-permute-done((bf16[2,1536,128]{2,1,0:T(8,128)(2,1)S(1)}, bf16[2,1536,128]{2,1,0:T(8,128)(2,1)}, u32[]{:S(2)}, u32[]{:S(2)}) %collective-permute-start) | collective-permute-done | bytes 786464 | tf_op jit(solution)/shard_map/ppermute | solution.py:264
  54.6 0.0 collective-permute-done.3.refs_8_
  54.6 5.4 %collective-permute-start.7 = (bf16[2,1536,128]{2,1,0:T(8,128)(2,1)}, bf16[2,1536,128]{2,1,0:T(8,128)(2,1)S(1)}, u32[]{:S(2)}, u32[]{:S(2)}) collective-permute-start(bf16[2,1536,128]{2,1,0:T(8,128)(2,1)} %collective-permute-done.refs_3_), channel_id=1, source_target_pairs={{0,388},{64,452},{128,0},{192,64},{256,128},{320,192},{384,256},{4... | collective-permute-start | bytes 2359304 | tf_op jit(solution)/shard_map/ppermute | solution.py:264
  60.0 0.0 collective-permute-done.8.refs_10_
  60.0 3.2 %collective-permute-start.9 = (bf16[2,1536,128]{2,1,0:T(8,128)(2,1)}, bf16[2,1536,128]{2,1,0:T(8,128)(2,1)S(1)}, u32[]{:S(2)}, u32[]{:S(2)}) collective-permute-start(bf16[2,1536,128]{2,1,0:T(8,128)(2,1)} %collective-permute-done.refs_3_), channel_id=1, source_target_pairs={{0,8},{64,72},{128,136},{192,200},{256,264},{320,328},{384,392},{4... | collective-permute-start | bytes 2359304 | tf_op jit(solution)/shard_map/ppermute | solution.py:264
  63.2 3.8 %collective-permute-start.10 = (bf16[2,1536,128]{2,1,0:T(8,128)(2,1)}, bf16[2,1536,128]{2,1,0:T(8,128)(2,1)S(1)}, u32[]{:S(2)}, u32[]{:S(2)}) collective-permute-start(bf16[2,1536,128]{2,1,0:T(8,128)(2,1)} %collective-permute-done.refs_3_), channel_id=1, source_target_pairs={{0,64},{64,0},{128,192},{192,128},{256,320},{320,256},{384,448},{4... | collective-permute-start | bytes 2359304 | tf_op jit(solution)/shard_map/ppermute | solution.py:264
  67.1 0.4 collective-permute-done.5.refs_6_
  67.5 2.7 %collective-permute-start.13 = (bf16[2,1536,128]{2,1,0:T(8,128)(2,1)S(1)}, bf16[2,1536,128]{2,1,0:T(8,128)(2,1)S(1)}, u32[]{:S(2)}, u32[]{:S(2)}) collective-permute-start(bf16[2,1536,128]{2,1,0:T(8,128)(2,1)S(1)} %collective-permute-done.5.refs_6_), channel_id=1, source_target_pairs={{0,64},{64,0},{128,192},{192,128},{256,320},{320,256},{384,448},{4... | collective-permute-start | bytes 2359304 | tf_op jit(solution)/shard_map/ppermute | solution.py:264
  70.2 5.6 %collective-permute-done.7.refs_5_ = bf16[2,1536,128]{2,1,0:T(8,128)(2,1)S(1)} collective-permute-done((bf16[2,1536,128]{2,1,0:T(8,128)(2,1)}, bf16[2,1536,128]{2,1,0:T(8,128)(2,1)S(1)}, u32[]{:S(2)}, u32[]{:S(2)}) %collective-permute-start.7) | collective-permute-done | bytes 786464 | tf_op jit(solution)/shard_map/ppermute | solution.py:264
  75.8 4.2 %collective-permute-start.12 = (bf16[2,1536,128]{2,1,0:T(8,128)(2,1)S(1)}, bf16[2,1536,128]{2,1,0:T(8,128)(2,1)S(1)}, u32[]{:S(2)}, u32[]{:S(2)}) collective-permute-start(bf16[2,1536,128]{2,1,0:T(8,128)(2,1)S(1)} %collective-permute-done.7.refs_5_), channel_id=1, source_target_pairs={{0,64},{64,0},{128,192},{192,128},{256,320},{320,256},{384,448},{4... | collective-permute-start | bytes 2359304 | tf_op jit(solution)/shard_map/ppermute | solution.py:264
  80.0 0.0 collective-permute-done.6.refs_4_
  80.0 1.9 %collective-permute-start.11 = (bf16[2,1536,128]{2,1,0:T(8,128)(2,1)S(1)}, bf16[2,1536,128]{2,1,0:T(8,128)(2,1)S(1)}, u32[]{:S(2)}, u32[]{:S(2)}) collective-permute-start(bf16[2,1536,128]{2,1,0:T(8,128)(2,1)S(1)} %collective-permute-done.6.refs_4_), channel_id=1, source_target_pairs={{0,64},{64,0},{128,192},{192,128},{256,320},{320,256},{384,448},{4... | collective-permute-start | bytes 2359304 | tf_op jit(solution)/shard_map/ppermute | solution.py:264
  81.9 0.0 collective-permute-done.9.refs_7_
  81.9 2.6 %collective-permute-start.14 = (bf16[2,1536,128]{2,1,0:T(8,128)(2,1)S(1)}, bf16[2,1536,128]{2,1,0:T(8,128)(2,1)S(1)}, u32[]{:S(2)}, u32[]{:S(2)}) collective-permute-start(bf16[2,1536,128]{2,1,0:T(8,128)(2,1)S(1)} %collective-permute-done.9.refs_7_), channel_id=1, source_target_pairs={{0,64},{64,0},{128,192},{192,128},{256,320},{320,256},{384,448},{4... | collective-permute-start | bytes 2359304 | tf_op jit(solution)/shard_map/ppermute | solution.py:264
  84.5 0.0 collective-permute-done.10.refs_11_
  84.5 0.0 collective-permute-done.12.refs_13_
  84.5 0.0 collective-permute-done.11.refs_12_
  84.5 0.0 collective-permute-done.13.refs_14_
  84.5 1.7 %collective-permute-done.14.refs_15_ = bf16[2,1536,128]{2,1,0:T(8,128)(2,1)S(1)} collective-permute-done((bf16[2,1536,128]{2,1,0:T(8,128)(2,1)S(1)}, bf16[2,1536,128]{2,1,0:T(8,128)(2,1)S(1)}, u32[]{:S(2)}, u32[]{:S(2)}) %collective-permute-start.14) | collective-permute-done | bytes 786464 | tf_op jit(solution)/shard_map/ppermute | solution.py:264
  86.2 16.5 %shard_map.61 = (bf16[4,128,128]{2,1,0:T(8,128)(2,1)}, f32[4,4096]{1,0:T(4,128)S(1)}) custom-call(s32[32,27]{1,0:T(8,128)S(1)} %bitcast.9, bf16[2,1536,128]{2,1,0:T(8,128)(2,1)S(1)} %get-tuple-element.17.refs_0_, bf16[2,1536,128]{2,1,0:T(8,128)(2,1)S(1)} %get-tuple-element.16.refs_1_, bf16[2,1536,128]{2,1,0:T(8,128)(2,1)S(1)} %collective-permute-done.1.refs_2_, ...), custom_call_target="tpu_custom_call" | custom-call | tf_op jit(solution)/shard_map/pallas_call | solution.py:204
  102.7 0.1 reshape.17
  102.8 0.1 copy.9
  102.9 0.1 reshape.18
  103.0 24.5 %all_to_all.10 = f32[64,2,128]{2,1,0:T(2,128)S(1)} all-to-all(f32[64,2,128]{2,1,0:T(2,128)S(1)} %reshape.18), channel_id=1, replica_groups=mesh['elem'=8,'band'=64] {'band'}, dimensions={0} | all-to-all | bytes 131072 | tf_op jit(solution)/shard_map/all_to_all | solution.py:302
  127.5 0.1 reduce_sum.9
  127.6 0.7 reshape.19
  (6 shorter events, 0.0 us)
Async XLA Ops:
  1.3 0.9 copy-start.1
  3.1 21.3 %all-to-all-start = ((bf16[4,528,128]{2,1,0:T(8,128)(2,1)}), bf16[4,528,128]{2,1,0:T(8,128)(2,1)S(1)}, u32[]{:S(2)}, u32[]{:S(2)}) async-start(bf16[4,528,128]{2,1,0:T(8,128)(2,1)} %shard_map.59), calls=%async_computation | async-start | bytes 1081344 | tf_op jit(solution)/shard_map/all_to_all | solution.py:273
  10.9 2.0 %copy-start = (bf16[4,27,128,128]{3,2,1,0:T(8,128)(2,1)S(1)}, bf16[4,27,128,128]{3,2,1,0:T(8,128)(2,1)}, u32[]{:S(2)}) copy-start(bf16[4,27,128,128]{3,2,1,0:T(8,128)(2,1)} %h2_ref.1) | copy-start | bytes 10616836
  12.9 0.7 copy-start.2
  15.9 25.0 %collective-permute-start.1 = (bf16[2,1536,128]{2,1,0:T(8,128)(2,1)S(1)}, bf16[2,1536,128]{2,1,0:T(8,128)(2,1)S(1)}, u32[]{:S(2)}, u32[]{:S(2)}) collective-permute-start(bf16[2,1536,128]{2,1,0:T(8,128)(2,1)S(1)} %get-tuple-element.17.refs_0_), channel_id=1, source_target_pairs={{0,128},{64,192},{128,256},{192,320},{256,384},{320,448},{384,4},{... | collective-permute-start | bytes 2359304 | tf_op jit(solution)/shard_map/ppermute | solution.py:264
  24.5 16.4 %collective-permute-start.2 = (bf16[4,528,128]{2,1,0:T(8,128)(2,1)S(1)}, bf16[4,528,128]{2,1,0:T(8,128)(2,1)S(1)}, u32[]{:S(2)}, u32[]{:S(2)}) collective-permute-start(bf16[4,528,128]{2,1,0:T(8,128)(2,1)S(1)} %all-to-all-done.refs_16_), channel_id=1, source_target_pairs={{0,64},{64,0},{128,192},{192,128},{256,320},{320,256},{384,448},{4... | collective-permute-start | bytes 1622024 | tf_op jit(solution)/shard_map/ppermute | solution.py:264
  28.6 17.8 %collective-permute-start.4 = (bf16[2,1536,128]{2,1,0:T(8,128)(2,1)S(1)}, bf16[2,1536,128]{2,1,0:T(8,128)(2,1)}, u32[]{:S(2)}, u32[]{:S(2)}) collective-permute-start(bf16[2,1536,128]{2,1,0:T(8,128)(2,1)S(1)} %get-tuple-element.16.refs_1_), channel_id=1, source_target_pairs={{0,64},{64,0},{128,192},{192,128},{256,320},{320,256},{384,448},{4... | collective-permute-start | bytes 2359304 | tf_op jit(solution)/shard_map/ppermute | solution.py:264
  30.6 24.0 %collective-permute-start = (bf16[2,1536,128]{2,1,0:T(8,128)(2,1)S(1)}, bf16[2,1536,128]{2,1,0:T(8,128)(2,1)}, u32[]{:S(2)}, u32[]{:S(2)}) collective-permute-start(bf16[2,1536,128]{2,1,0:T(8,128)(2,1)S(1)} %get-tuple-element.16.refs_1_), channel_id=1, source_target_pairs={{0,388},{64,452},{128,0},{192,64},{256,128},{320,192},{384,256},{4... | collective-permute-start | bytes 2359304 | tf_op jit(solution)/shard_map/ppermute | solution.py:264
  38.2 16.4 %collective-permute-start.3 = (bf16[2,1536,128]{2,1,0:T(8,128)(2,1)S(1)}, bf16[2,1536,128]{2,1,0:T(8,128)(2,1)}, u32[]{:S(2)}, u32[]{:S(2)}) collective-permute-start(bf16[2,1536,128]{2,1,0:T(8,128)(2,1)S(1)} %get-tuple-element.17.refs_0_), channel_id=1, source_target_pairs={{0,64},{64,0},{128,192},{192,128},{256,320},{320,256},{384,448},{4... | collective-permute-start | bytes 2359304 | tf_op jit(solution)/shard_map/ppermute | solution.py:264
  40.9 19.1 %collective-permute-start.8 = (bf16[2,1536,128]{2,1,0:T(8,128)(2,1)S(1)}, bf16[2,1536,128]{2,1,0:T(8,128)(2,1)}, u32[]{:S(2)}, u32[]{:S(2)}) collective-permute-start(bf16[2,1536,128]{2,1,0:T(8,128)(2,1)S(1)} %collective-permute-done.1.refs_2_), channel_id=1, source_target_pairs={{0,64},{64,0},{128,192},{192,128},{256,320},{320,256},{384,448},{4... | collective-permute-start | bytes 2359304 | tf_op jit(solution)/shard_map/ppermute | solution.py:264
  44.5 35.5 %collective-permute-start.6 = (bf16[2,1536,128]{2,1,0:T(8,128)(2,1)S(1)}, bf16[2,1536,128]{2,1,0:T(8,128)(2,1)S(1)}, u32[]{:S(2)}, u32[]{:S(2)}) collective-permute-start(bf16[2,1536,128]{2,1,0:T(8,128)(2,1)S(1)} %collective-permute-done.1.refs_2_), channel_id=1, source_target_pairs={{0,128},{64,192},{128,256},{192,320},{256,384},{320,448},{384,4},{... | collective-permute-start | bytes 2359304 | tf_op jit(solution)/shard_map/ppermute | solution.py:264
  46.4 21.1 %collective-permute-start.5 = (bf16[2,1536,128]{2,1,0:T(8,128)(2,1)S(1)}, bf16[2,1536,128]{2,1,0:T(8,128)(2,1)S(1)}, u32[]{:S(2)}, u32[]{:S(2)}) collective-permute-start(bf16[2,1536,128]{2,1,0:T(8,128)(2,1)S(1)} %collective-permute-done.1.refs_2_), channel_id=1, source_target_pairs={{0,1},{64,65},{128,129},{192,193},{256,257},{320,321},{384,385},{4... | collective-permute-start | bytes 2359304 | tf_op jit(solution)/shard_map/ppermute | solution.py:264
  54.6 21.2 %collective-permute-start.7 = (bf16[2,1536,128]{2,1,0:T(8,128)(2,1)}, bf16[2,1536,128]{2,1,0:T(8,128)(2,1)S(1)}, u32[]{:S(2)}, u32[]{:S(2)}) collective-permute-start(bf16[2,1536,128]{2,1,0:T(8,128)(2,1)} %collective-permute-done.refs_3_), channel_id=1, source_target_pairs={{0,388},{64,452},{128,0},{192,64},{256,128},{320,192},{384,256},{4... | collective-permute-start | bytes 2359304 | tf_op jit(solution)/shard_map/ppermute | solution.py:264
  60.0 21.9 %collective-permute-start.9 = (bf16[2,1536,128]{2,1,0:T(8,128)(2,1)}, bf16[2,1536,128]{2,1,0:T(8,128)(2,1)S(1)}, u32[]{:S(2)}, u32[]{:S(2)}) collective-permute-start(bf16[2,1536,128]{2,1,0:T(8,128)(2,1)} %collective-permute-done.refs_3_), channel_id=1, source_target_pairs={{0,8},{64,72},{128,136},{192,200},{256,264},{320,328},{384,392},{4... | collective-permute-start | bytes 2359304 | tf_op jit(solution)/shard_map/ppermute | solution.py:264
  63.2 21.3 %collective-permute-start.10 = (bf16[2,1536,128]{2,1,0:T(8,128)(2,1)}, bf16[2,1536,128]{2,1,0:T(8,128)(2,1)S(1)}, u32[]{:S(2)}, u32[]{:S(2)}) collective-permute-start(bf16[2,1536,128]{2,1,0:T(8,128)(2,1)} %collective-permute-done.refs_3_), channel_id=1, source_target_pairs={{0,64},{64,0},{128,192},{192,128},{256,320},{320,256},{384,448},{4... | collective-permute-start | bytes 2359304 | tf_op jit(solution)/shard_map/ppermute | solution.py:264
  67.5 17.0 %collective-permute-start.13 = (bf16[2,1536,128]{2,1,0:T(8,128)(2,1)S(1)}, bf16[2,1536,128]{2,1,0:T(8,128)(2,1)S(1)}, u32[]{:S(2)}, u32[]{:S(2)}) collective-permute-start(bf16[2,1536,128]{2,1,0:T(8,128)(2,1)S(1)} %collective-permute-done.5.refs_6_), channel_id=1, source_target_pairs={{0,64},{64,0},{128,192},{192,128},{256,320},{320,256},{384,448},{4... | collective-permute-start | bytes 2359304 | tf_op jit(solution)/shard_map/ppermute | solution.py:264
  75.8 8.7 %collective-permute-start.12 = (bf16[2,1536,128]{2,1,0:T(8,128)(2,1)S(1)}, bf16[2,1536,128]{2,1,0:T(8,128)(2,1)S(1)}, u32[]{:S(2)}, u32[]{:S(2)}) collective-permute-start(bf16[2,1536,128]{2,1,0:T(8,128)(2,1)S(1)} %collective-permute-done.7.refs_5_), channel_id=1, source_target_pairs={{0,64},{64,0},{128,192},{192,128},{256,320},{320,256},{384,448},{4... | collective-permute-start | bytes 2359304 | tf_op jit(solution)/shard_map/ppermute | solution.py:264
  80.0 4.6 %collective-permute-start.11 = (bf16[2,1536,128]{2,1,0:T(8,128)(2,1)S(1)}, bf16[2,1536,128]{2,1,0:T(8,128)(2,1)S(1)}, u32[]{:S(2)}, u32[]{:S(2)}) collective-permute-start(bf16[2,1536,128]{2,1,0:T(8,128)(2,1)S(1)} %collective-permute-done.6.refs_4_), channel_id=1, source_target_pairs={{0,64},{64,0},{128,192},{192,128},{256,320},{320,256},{384,448},{4... | collective-permute-start | bytes 2359304 | tf_op jit(solution)/shard_map/ppermute | solution.py:264
  81.9 4.3 %collective-permute-start.14 = (bf16[2,1536,128]{2,1,0:T(8,128)(2,1)S(1)}, bf16[2,1536,128]{2,1,0:T(8,128)(2,1)S(1)}, u32[]{:S(2)}, u32[]{:S(2)}) collective-permute-start(bf16[2,1536,128]{2,1,0:T(8,128)(2,1)S(1)} %collective-permute-done.9.refs_7_), channel_id=1, source_target_pairs={{0,64},{64,0},{128,192},{192,128},{256,320},{320,256},{384,448},{4... | collective-permute-start | bytes 2359304 | tf_op jit(solution)/shard_map/ppermute | solution.py:264

commit v7 on v6

--- a/solution.py
+++ b/solution.py
@@ -275,14 +275,14 @@
 
     own_swapped = [move(own_a, over_core), move(own_b, over_core)]
     from_below, y_other = lax.optimization_barrier((from_below, y_other))
-    from_above, y_other, own_swapped = lax.optimization_barrier(
-        (from_above, y_other, own_swapped)
-    )
+    from_above, y_other = lax.optimization_barrier((from_above, y_other))
     far_a = move(from_below, up)
     far_b = move(from_above, down)
     below_b = move(from_below, over_x)
     below_swapped = move(from_below, over_core)
-    for_y, below_swapped = lax.optimization_barrier((from_above, below_swapped))
+    for_y, below_swapped, own_swapped = lax.optimization_barrier(
+        (from_above, below_swapped, own_swapped)
+    )
     above_a = move(for_y, over_y)
 
 

time: 129 us -> 130 us (level)
  waiting for transfers between devices: 17.9 us -> 19.4 us
    ppermute x15, waiting for transfers between devices: 12.7 us -> 14.2 us  [move(): return lax.ppermute(value, both, pairs)]
  transfers between devices with their start and end apart: 16 -> 16, of which waited for: 5 -> 6; matrix products, arithmetic and copies ran while one was open for 0% -> 0% of each run, Pallas kernels for 2% -> 2%
where the time goes in v7:
time: 130 us
  starting transfers between devices  60.2 us (46%)
  blocking collectives  24.2 us (19%)
  Pallas kernels  19.6 us (15%)
  waiting for transfers between devices  19.4 us (15%)
  local copies, waits for them, and re-layouts  4.61 us (4%)
    ppermute x15, starting transfers between devices, move(): return lax.ppermute(value, both, pairs)  52.4 us
    all_to_all x1, blocking collectives, local(): lax.all_to_all(parts.reshape(nbands, points // 32, 128), 'band', 0, 0)  24.2 us
    pallas_call x1, Pallas kernels, filtering(): pl.pallas_call(filter_kernel, out_shape=(jax.ShapeDtypeStruct((4, NB, NB)...  16.5 us
    ppermute x15, waiting for transfers between devices, move(): return lax.ppermute(value, both, pairs)  14.2 us
    all_to_all x1, starting transfers between devices, local(): y_own = lax.all_to_all(turned, 'elem', 0, 0, axis_index_groups=groups)  7.81 us
    all_to_all x1, waiting for transfers between devices, local(): y_own = lax.all_to_all(turned, 'elem', 0, 0, axis_index_groups=groups)  5.2 us
    unnamed x6, local copies, waits for them, and re-layouts  3.58 us
  transfers between devices with their start and end apart: 16, of which 6 were waited for; matrix products, arithmetic and copies ran while one was open for 0% of the time, Pallas kernels for 2%

profile of v7, /device:TPU:1, one launch (start us, length us, event | category | flops | bytes accessed | tf_op | source)
XLA Modules:
  0.0 129.7 jit_solution(10941169815699645968)
XLA Ops:
  0.6 0.7 convert_element_type.4
  1.3 0.0 copy-start.1
  1.3 0.9 copy-done.1
  2.2 0.9 shard_map.59
  3.1 7.8 %all-to-all-start = ((bf16[4,528,128]{2,1,0:T(8,128)(2,1)}), bf16[4,528,128]{2,1,0:T(8,128)(2,1)S(1)}, u32[]{:S(2)}, u32[]{:S(2)}) async-start(bf16[4,528,128]{2,1,0:T(8,128)(2,1)} %shard_map.59), calls=%async_computation | async-start | bytes 1081344 | tf_op jit(solution)/shard_map/all_to_all | solution.py:273
  10.9 0.0 copy-start
  10.9 2.0 %copy-done = bf16[4,27,128,128]{3,2,1,0:T(8,128)(2,1)S(1)} copy-done((bf16[4,27,128,128]{3,2,1,0:T(8,128)(2,1)S(1)}, bf16[4,27,128,128]{3,2,1,0:T(8,128)(2,1)}, u32[]{:S(2)}) %copy-start) | copy-done | bytes 3538968
  12.9 0.0 copy-start.2
  12.9 0.7 copy-done.2
  13.6 2.2 %shard_map.60 = (bf16[2,1536,128]{2,1,0:T(8,128)(2,1)S(1)}, bf16[2,1536,128]{2,1,0:T(8,128)(2,1)S(1)}) custom-call(s32[1]{0:T(128)} %bitcast.1.pair_ref, s32[4,27]{1,0:T(4,128)S(1)} %copy-done.2, bf16[4,27,128,128]{3,2,1,0:T(8,128)(2,1)S(1)} %copy-done, bf16[4,27,128,128]{3,2,1,0:T(8,128)(2,1)S(1)} %copy-done, bf16[4,27,128,128]{3,2,1,0:T(8,128)(2,1)S(1)} %copy-done), custom_call_target="tpu_custom_call" | custom-call | flops 452984832 | bytes 5200000 | tf_op jit(solution)/shard_map/pallas_call | solution.py:66
  15.9 3.4 %collective-permute-start.1 = (bf16[2,1536,128]{2,1,0:T(8,128)(2,1)S(1)}, bf16[2,1536,128]{2,1,0:T(8,128)(2,1)S(1)}, u32[]{:S(2)}, u32[]{:S(2)}) collective-permute-start(bf16[2,1536,128]{2,1,0:T(8,128)(2,1)S(1)} %get-tuple-element.17.refs_0_), channel_id=1, source_target_pairs={{0,128},{64,192},{128,256},{192,320},{256,384},{320,448},{384,4},{... | collective-permute-start | bytes 2359304 | tf_op jit(solution)/shard_map/ppermute | solution.py:264
  19.3 5.2 %all-to-all-done.refs_16_ = bf16[4,528,128]{2,1,0:T(8,128)(2,1)S(1)} async-done(((bf16[4,528,128]{2,1,0:T(8,128)(2,1)}), bf16[4,528,128]{2,1,0:T(8,128)(2,1)S(1)}, u32[]{:S(2)}, u32[]{:S(2)}) %all-to-all-start) | async-done | bytes 540704 | tf_op jit(solution)/shard_map/all_to_all | solution.py:273
  24.5 4.2 %collective-permute-start.2 = (bf16[4,528,128]{2,1,0:T(8,128)(2,1)S(1)}, bf16[4,528,128]{2,1,0:T(8,128)(2,1)S(1)}, u32[]{:S(2)}, u32[]{:S(2)}) collective-permute-start(bf16[4,528,128]{2,1,0:T(8,128)(2,1)S(1)} %all-to-all-done.refs_16_), channel_id=1, source_target_pairs={{0,64},{64,0},{128,192},{192,128},{256,320},{320,256},{384,448},{4... | collective-permute-start | bytes 1622024 | tf_op jit(solution)/shard_map/ppermute | solution.py:264
  28.6 7.6 %collective-permute-start = (bf16[2,1536,128]{2,1,0:T(8,128)(2,1)S(1)}, bf16[2,1536,128]{2,1,0:T(8,128)(2,1)}, u32[]{:S(2)}, u32[]{:S(2)}) collective-permute-start(bf16[2,1536,128]{2,1,0:T(8,128)(2,1)S(1)} %get-tuple-element.16.refs_1_), channel_id=1, source_target_pairs={{0,388},{64,452},{128,0},{192,64},{256,128},{320,192},{384,256},{4... | collective-permute-start | bytes 2359304 | tf_op jit(solution)/shard_map/ppermute | solution.py:264
  36.3 2.2 %collective-permute-start.8 = (bf16[2,1536,128]{2,1,0:T(8,128)(2,1)S(1)}, bf16[2,1536,128]{2,1,0:T(8,128)(2,1)}, u32[]{:S(2)}, u32[]{:S(2)}) collective-permute-start(bf16[2,1536,128]{2,1,0:T(8,128)(2,1)S(1)} %get-tuple-element.16.refs_1_), channel_id=1, source_target_pairs={{0,64},{64,0},{128,192},{192,128},{256,320},{320,256},{384,448},{4... | collective-permute-start | bytes 2359304 | tf_op jit(solution)/shard_map/ppermute | solution.py:264
  38.5 2.1 %collective-permute-start.7 = (bf16[2,1536,128]{2,1,0:T(8,128)(2,1)S(1)}, bf16[2,1536,128]{2,1,0:T(8,128)(2,1)}, u32[]{:S(2)}, u32[]{:S(2)}) collective-permute-start(bf16[2,1536,128]{2,1,0:T(8,128)(2,1)S(1)} %get-tuple-element.17.refs_0_), channel_id=1, source_target_pairs={{0,64},{64,0},{128,192},{192,128},{256,320},{320,256},{384,448},{4... | collective-permute-start | bytes 2359304 | tf_op jit(solution)/shard_map/ppermute | solution.py:264
  40.6 0.1 collective-permute-done.1.refs_2_
  40.7 0.0 collective-permute-done.2.refs_17_
  40.7 3.8 %collective-permute-start.6 = (bf16[2,1536,128]{2,1,0:T(8,128)(2,1)S(1)}, bf16[2,1536,128]{2,1,0:T(8,128)(2,1)}, u32[]{:S(2)}, u32[]{:S(2)}) collective-permute-start(bf16[2,1536,128]{2,1,0:T(8,128)(2,1)S(1)} %collective-permute-done.1.refs_2_), channel_id=1, source_target_pairs={{0,64},{64,0},{128,192},{192,128},{256,320},{320,256},{384,448},{4... | collective-permute-start | bytes 2359304 | tf_op jit(solution)/shard_map/ppermute | solution.py:264
  44.5 1.9 %collective-permute-start.4 = (bf16[2,1536,128]{2,1,0:T(8,128)(2,1)S(1)}, bf16[2,1536,128]{2,1,0:T(8,128)(2,1)S(1)}, u32[]{:S(2)}, u32[]{:S(2)}) collective-permute-start(bf16[2,1536,128]{2,1,0:T(8,128)(2,1)S(1)} %collective-permute-done.1.refs_2_), channel_id=1, source_target_pairs={{0,128},{64,192},{128,256},{192,320},{256,384},{320,448},{384,4},{... | collective-permute-start | bytes 2359304 | tf_op jit(solution)/shard_map/ppermute | solution.py:264
  46.4 6.8 %collective-permute-done.refs_3_ = bf16[2,1536,128]{2,1,0:T(8,128)(2,1)} collective-permute-done((bf16[2,1536,128]{2,1,0:T(8,128)(2,1)S(1)}, bf16[2,1536,128]{2,1,0:T(8,128)(2,1)}, u32[]{:S(2)}, u32[]{:S(2)}) %collective-permute-start) | collective-permute-done | bytes 786464 | tf_op jit(solution)/shard_map/ppermute | solution.py:264
  53.2 3.1 %collective-permute-start.3 = (bf16[2,1536,128]{2,1,0:T(8,128)(2,1)S(1)}, bf16[2,1536,128]{2,1,0:T(8,128)(2,1)S(1)}, u32[]{:S(2)}, u32[]{:S(2)}) collective-permute-start(bf16[2,1536,128]{2,1,0:T(8,128)(2,1)S(1)} %collective-permute-done.1.refs_2_), channel_id=1, source_target_pairs={{0,1},{64,65},{128,129},{192,193},{256,257},{320,321},{384,385},{4... | collective-permute-start | bytes 2359304 | tf_op jit(solution)/shard_map/ppermute | solution.py:264
  56.3 0.0 collective-permute-done.8.refs_9_
  56.3 5.4 %collective-permute-start.5 = (bf16[2,1536,128]{2,1,0:T(8,128)(2,1)}, bf16[2,1536,128]{2,1,0:T(8,128)(2,1)S(1)}, u32[]{:S(2)}, u32[]{:S(2)}) collective-permute-start(bf16[2,1536,128]{2,1,0:T(8,128)(2,1)} %collective-permute-done.refs_3_), channel_id=1, source_target_pairs={{0,388},{64,452},{128,0},{192,64},{256,128},{320,192},{384,256},{4... | collective-permute-start | bytes 2359304 | tf_op jit(solution)/shard_map/ppermute | solution.py:264
  61.8 0.0 collective-permute-done.7.refs_8_
  61.8 0.0 collective-permute-done.6.refs_10_
  61.8 3.2 %collective-permute-start.9 = (bf16[2,1536,128]{2,1,0:T(8,128)(2,1)}, bf16[2,1536,128]{2,1,0:T(8,128)(2,1)S(1)}, u32[]{:S(2)}, u32[]{:S(2)}) collective-permute-start(bf16[2,1536,128]{2,1,0:T(8,128)(2,1)} %collective-permute-done.refs_3_), channel_id=1, source_target_pairs={{0,8},{64,72},{128,136},{192,200},{256,264},{320,328},{384,392},{4... | collective-permute-start | bytes 2359304 | tf_op jit(solution)/shard_map/ppermute | solution.py:264
  65.0 3.5 %collective-permute-start.10 = (bf16[2,1536,128]{2,1,0:T(8,128)(2,1)}, bf16[2,1536,128]{2,1,0:T(8,128)(2,1)S(1)}, u32[]{:S(2)}, u32[]{:S(2)}) collective-permute-start(bf16[2,1536,128]{2,1,0:T(8,128)(2,1)} %collective-permute-done.refs_3_), channel_id=1, source_target_pairs={{0,64},{64,0},{128,192},{192,128},{256,320},{320,256},{384,448},{4... | collective-permute-start | bytes 2359304 | tf_op jit(solution)/shard_map/ppermute | solution.py:264
  68.6 4.7 %collective-permute-done.3.refs_6_ = bf16[2,1536,128]{2,1,0:T(8,128)(2,1)S(1)} collective-permute-done((bf16[2,1536,128]{2,1,0:T(8,128)(2,1)S(1)}, bf16[2,1536,128]{2,1,0:T(8,128)(2,1)S(1)}, u32[]{:S(2)}, u32[]{:S(2)}) %collective-permute-start.3) | collective-permute-done | bytes 786464 | tf_op jit(solution)/shard_map/ppermute | solution.py:264
  73.4 3.6 %collective-permute-start.13 = (bf16[2,1536,128]{2,1,0:T(8,128)(2,1)S(1)}, bf16[2,1536,128]{2,1,0:T(8,128)(2,1)S(1)}, u32[]{:S(2)}, u32[]{:S(2)}) collective-permute-start(bf16[2,1536,128]{2,1,0:T(8,128)(2,1)S(1)} %collective-permute-done.3.refs_6_), channel_id=1, source_target_pairs={{0,64},{64,0},{128,192},{192,128},{256,320},{320,256},{384,448},{4... | collective-permute-start | bytes 2359304 | tf_op jit(solution)/shard_map/ppermute | solution.py:264
  76.9 0.9 collective-permute-done.5.refs_5_
  77.8 3.9 %collective-permute-start.12 = (bf16[2,1536,128]{2,1,0:T(8,128)(2,1)S(1)}, bf16[2,1536,128]{2,1,0:T(8,128)(2,1)S(1)}, u32[]{:S(2)}, u32[]{:S(2)}) collective-permute-start(bf16[2,1536,128]{2,1,0:T(8,128)(2,1)S(1)} %collective-permute-done.5.refs_5_), channel_id=1, source_target_pairs={{0,64},{64,0},{128,192},{192,128},{256,320},{320,256},{384,448},{4... | collective-permute-start | bytes 2359304 | tf_op jit(solution)/shard_map/ppermute | solution.py:264
  81.7 0.0 collective-permute-done.4.refs_4_
  81.7 1.9 %collective-permute-start.11 = (bf16[2,1536,128]{2,1,0:T(8,128)(2,1)S(1)}, bf16[2,1536,128]{2,1,0:T(8,128)(2,1)S(1)}, u32[]{:S(2)}, u32[]{:S(2)}) collective-permute-start(bf16[2,1536,128]{2,1,0:T(8,128)(2,1)S(1)} %collective-permute-done.4.refs_4_), channel_id=1, source_target_pairs={{0,64},{64,0},{128,192},{192,128},{256,320},{320,256},{384,448},{4... | collective-permute-start | bytes 2359304 | tf_op jit(solution)/shard_map/ppermute | solution.py:264
  83.7 0.0 collective-permute-done.9.refs_7_
  83.7 2.6 %collective-permute-start.14 = (bf16[2,1536,128]{2,1,0:T(8,128)(2,1)S(1)}, bf16[2,1536,128]{2,1,0:T(8,128)(2,1)S(1)}, u32[]{:S(2)}, u32[]{:S(2)}) collective-permute-start(bf16[2,1536,128]{2,1,0:T(8,128)(2,1)S(1)} %collective-permute-done.9.refs_7_), channel_id=1, source_target_pairs={{0,64},{64,0},{128,192},{192,128},{256,320},{320,256},{384,448},{4... | collective-permute-start | bytes 2359304 | tf_op jit(solution)/shard_map/ppermute | solution.py:264
  86.3 0.0 collective-permute-done.10.refs_11_
  86.3 0.0 collective-permute-done.12.refs_13_
  86.3 0.0 collective-permute-done.11.refs_12_
  86.3 0.0 collective-permute-done.13.refs_14_
  86.3 1.7 %collective-permute-done.14.refs_15_ = bf16[2,1536,128]{2,1,0:T(8,128)(2,1)S(1)} collective-permute-done((bf16[2,1536,128]{2,1,0:T(8,128)(2,1)S(1)}, bf16[2,1536,128]{2,1,0:T(8,128)(2,1)S(1)}, u32[]{:S(2)}, u32[]{:S(2)}) %collective-permute-start.14) | collective-permute-done | bytes 786464 | tf_op jit(solution)/shard_map/ppermute | solution.py:264
  88.0 16.5 %shard_map.61 = (bf16[4,128,128]{2,1,0:T(8,128)(2,1)}, f32[4,4096]{1,0:T(4,128)S(1)}) custom-call(s32[32,27]{1,0:T(8,128)S(1)} %bitcast.9, bf16[2,1536,128]{2,1,0:T(8,128)(2,1)S(1)} %get-tuple-element.17.refs_0_, bf16[2,1536,128]{2,1,0:T(8,128)(2,1)S(1)} %get-tuple-element.16.refs_1_, bf16[2,1536,128]{2,1,0:T(8,128)(2,1)S(1)} %collective-permute-done.1.refs_2_, ...), custom_call_target="tpu_custom_call" | custom-call | tf_op jit(solution)/shard_map/pallas_call | solution.py:204
  104.4 0.1 reshape.17
  104.6 0.1 copy.9
  104.7 0.1 reshape.18
  104.8 24.2 %all_to_all.10 = f32[64,2,128]{2,1,0:T(2,128)S(1)} all-to-all(f32[64,2,128]{2,1,0:T(2,128)S(1)} %reshape.18), channel_id=1, replica_groups=mesh['elem'=8,'band'=64] {'band'}, dimensions={0} | all-to-all | bytes 131072 | tf_op jit(solution)/shard_map/all_to_all | solution.py:302
  128.9 0.1 reduce_sum.9
  129.0 0.7 reshape.19
  (6 shorter events, 0.0 us)
Async XLA Ops:
  1.3 0.9 copy-start.1
  3.1 21.3 %all-to-all-start = ((bf16[4,528,128]{2,1,0:T(8,128)(2,1)}), bf16[4,528,128]{2,1,0:T(8,128)(2,1)S(1)}, u32[]{:S(2)}, u32[]{:S(2)}) async-start(bf16[4,528,128]{2,1,0:T(8,128)(2,1)} %shard_map.59), calls=%async_computation | async-start | bytes 1081344 | tf_op jit(solution)/shard_map/all_to_all | solution.py:273
  10.9 2.0 %copy-start = (bf16[4,27,128,128]{3,2,1,0:T(8,128)(2,1)S(1)}, bf16[4,27,128,128]{3,2,1,0:T(8,128)(2,1)}, u32[]{:S(2)}) copy-start(bf16[4,27,128,128]{3,2,1,0:T(8,128)(2,1)} %h2_ref.1) | copy-start | bytes 10616836
  12.9 0.7 copy-start.2
  15.9 24.8 %collective-permute-start.1 = (bf16[2,1536,128]{2,1,0:T(8,128)(2,1)S(1)}, bf16[2,1536,128]{2,1,0:T(8,128)(2,1)S(1)}, u32[]{:S(2)}, u32[]{:S(2)}) collective-permute-start(bf16[2,1536,128]{2,1,0:T(8,128)(2,1)S(1)} %get-tuple-element.17.refs_0_), channel_id=1, source_target_pairs={{0,128},{64,192},{128,256},{192,320},{256,384},{320,448},{384,4},{... | collective-permute-start | bytes 2359304 | tf_op jit(solution)/shard_map/ppermute | solution.py:264
  24.5 16.3 %collective-permute-start.2 = (bf16[4,528,128]{2,1,0:T(8,128)(2,1)S(1)}, bf16[4,528,128]{2,1,0:T(8,128)(2,1)S(1)}, u32[]{:S(2)}, u32[]{:S(2)}) collective-permute-start(bf16[4,528,128]{2,1,0:T(8,128)(2,1)S(1)} %all-to-all-done.refs_16_), channel_id=1, source_target_pairs={{0,64},{64,0},{128,192},{192,128},{256,320},{320,256},{384,448},{4... | collective-permute-start | bytes 1622024 | tf_op jit(solution)/shard_map/ppermute | solution.py:264
  28.6 24.6 %collective-permute-start = (bf16[2,1536,128]{2,1,0:T(8,128)(2,1)S(1)}, bf16[2,1536,128]{2,1,0:T(8,128)(2,1)}, u32[]{:S(2)}, u32[]{:S(2)}) collective-permute-start(bf16[2,1536,128]{2,1,0:T(8,128)(2,1)S(1)} %get-tuple-element.16.refs_1_), channel_id=1, source_target_pairs={{0,388},{64,452},{128,0},{192,64},{256,128},{320,192},{384,256},{4... | collective-permute-start | bytes 2359304 | tf_op jit(solution)/shard_map/ppermute | solution.py:264
  36.3 20.1 %collective-permute-start.8 = (bf16[2,1536,128]{2,1,0:T(8,128)(2,1)S(1)}, bf16[2,1536,128]{2,1,0:T(8,128)(2,1)}, u32[]{:S(2)}, u32[]{:S(2)}) collective-permute-start(bf16[2,1536,128]{2,1,0:T(8,128)(2,1)S(1)} %get-tuple-element.16.refs_1_), channel_id=1, source_target_pairs={{0,64},{64,0},{128,192},{192,128},{256,320},{320,256},{384,448},{4... | collective-permute-start | bytes 2359304 | tf_op jit(solution)/shard_map/ppermute | solution.py:264
  38.5 23.3 %collective-permute-start.7 = (bf16[2,1536,128]{2,1,0:T(8,128)(2,1)S(1)}, bf16[2,1536,128]{2,1,0:T(8,128)(2,1)}, u32[]{:S(2)}, u32[]{:S(2)}) collective-permute-start(bf16[2,1536,128]{2,1,0:T(8,128)(2,1)S(1)} %get-tuple-element.17.refs_0_), channel_id=1, source_target_pairs={{0,64},{64,0},{128,192},{192,128},{256,320},{320,256},{384,448},{4... | collective-permute-start | bytes 2359304 | tf_op jit(solution)/shard_map/ppermute | solution.py:264
  40.7 21.1 %collective-permute-start.6 = (bf16[2,1536,128]{2,1,0:T(8,128)(2,1)S(1)}, bf16[2,1536,128]{2,1,0:T(8,128)(2,1)}, u32[]{:S(2)}, u32[]{:S(2)}) collective-permute-start(bf16[2,1536,128]{2,1,0:T(8,128)(2,1)S(1)} %collective-permute-done.1.refs_2_), channel_id=1, source_target_pairs={{0,64},{64,0},{128,192},{192,128},{256,320},{320,256},{384,448},{4... | collective-permute-start | bytes 2359304 | tf_op jit(solution)/shard_map/ppermute | solution.py:264
  44.5 37.2 %collective-permute-start.4 = (bf16[2,1536,128]{2,1,0:T(8,128)(2,1)S(1)}, bf16[2,1536,128]{2,1,0:T(8,128)(2,1)S(1)}, u32[]{:S(2)}, u32[]{:S(2)}) collective-permute-start(bf16[2,1536,128]{2,1,0:T(8,128)(2,1)S(1)} %collective-permute-done.1.refs_2_), channel_id=1, source_target_pairs={{0,128},{64,192},{128,256},{192,320},{256,384},{320,448},{384,4},{... | collective-permute-start | bytes 2359304 | tf_op jit(solution)/shard_map/ppermute | solution.py:264
  53.2 20.2 %collective-permute-start.3 = (bf16[2,1536,128]{2,1,0:T(8,128)(2,1)S(1)}, bf16[2,1536,128]{2,1,0:T(8,128)(2,1)S(1)}, u32[]{:S(2)}, u32[]{:S(2)}) collective-permute-start(bf16[2,1536,128]{2,1,0:T(8,128)(2,1)S(1)} %collective-permute-done.1.refs_2_), channel_id=1, source_target_pairs={{0,1},{64,65},{128,129},{192,193},{256,257},{320,321},{384,385},{4... | collective-permute-start | bytes 2359304 | tf_op jit(solution)/shard_map/ppermute | solution.py:264
  56.3 21.5 %collective-permute-start.5 = (bf16[2,1536,128]{2,1,0:T(8,128)(2,1)}, bf16[2,1536,128]{2,1,0:T(8,128)(2,1)S(1)}, u32[]{:S(2)}, u32[]{:S(2)}) collective-permute-start(bf16[2,1536,128]{2,1,0:T(8,128)(2,1)} %collective-permute-done.refs_3_), channel_id=1, source_target_pairs={{0,388},{64,452},{128,0},{192,64},{256,128},{320,192},{384,256},{4... | collective-permute-start | bytes 2359304 | tf_op jit(solution)/shard_map/ppermute | solution.py:264
  61.8 21.9 %collective-permute-start.9 = (bf16[2,1536,128]{2,1,0:T(8,128)(2,1)}, bf16[2,1536,128]{2,1,0:T(8,128)(2,1)S(1)}, u32[]{:S(2)}, u32[]{:S(2)}) collective-permute-start(bf16[2,1536,128]{2,1,0:T(8,128)(2,1)} %collective-permute-done.refs_3_), channel_id=1, source_target_pairs={{0,8},{64,72},{128,136},{192,200},{256,264},{320,328},{384,392},{4... | collective-permute-start | bytes 2359304 | tf_op jit(solution)/shard_map/ppermute | solution.py:264
  65.0 21.3 %collective-permute-start.10 = (bf16[2,1536,128]{2,1,0:T(8,128)(2,1)}, bf16[2,1536,128]{2,1,0:T(8,128)(2,1)S(1)}, u32[]{:S(2)}, u32[]{:S(2)}) collective-permute-start(bf16[2,1536,128]{2,1,0:T(8,128)(2,1)} %collective-permute-done.refs_3_), channel_id=1, source_target_pairs={{0,64},{64,0},{128,192},{192,128},{256,320},{320,256},{384,448},{4... | collective-permute-start | bytes 2359304 | tf_op jit(solution)/shard_map/ppermute | solution.py:264
  73.4 12.9 %collective-permute-start.13 = (bf16[2,1536,128]{2,1,0:T(8,128)(2,1)S(1)}, bf16[2,1536,128]{2,1,0:T(8,128)(2,1)S(1)}, u32[]{:S(2)}, u32[]{:S(2)}) collective-permute-start(bf16[2,1536,128]{2,1,0:T(8,128)(2,1)S(1)} %collective-permute-done.3.refs_6_), channel_id=1, source_target_pairs={{0,64},{64,0},{128,192},{192,128},{256,320},{320,256},{384,448},{4... | collective-permute-start | bytes 2359304 | tf_op jit(solution)/shard_map/ppermute | solution.py:264
  77.8 8.5 %collective-permute-start.12 = (bf16[2,1536,128]{2,1,0:T(8,128)(2,1)S(1)}, bf16[2,1536,128]{2,1,0:T(8,128)(2,1)S(1)}, u32[]{:S(2)}, u32[]{:S(2)}) collective-permute-start(bf16[2,1536,128]{2,1,0:T(8,128)(2,1)S(1)} %collective-permute-done.5.refs_5_), channel_id=1, source_target_pairs={{0,64},{64,0},{128,192},{192,128},{256,320},{320,256},{384,448},{4... | collective-permute-start | bytes 2359304 | tf_op jit(solution)/shard_map/ppermute | solution.py:264
  81.7 4.6 %collective-permute-start.11 = (bf16[2,1536,128]{2,1,0:T(8,128)(2,1)S(1)}, bf16[2,1536,128]{2,1,0:T(8,128)(2,1)S(1)}, u32[]{:S(2)}, u32[]{:S(2)}) collective-permute-start(bf16[2,1536,128]{2,1,0:T(8,128)(2,1)S(1)} %collective-permute-done.4.refs_4_), channel_id=1, source_target_pairs={{0,64},{64,0},{128,192},{192,128},{256,320},{320,256},{384,448},{4... | collective-permute-start | bytes 2359304 | tf_op jit(solution)/shard_map/ppermute | solution.py:264
  83.7 4.3 %collective-permute-start.14 = (bf16[2,1536,128]{2,1,0:T(8,128)(2,1)S(1)}, bf16[2,1536,128]{2,1,0:T(8,128)(2,1)S(1)}, u32[]{:S(2)}, u32[]{:S(2)}) collective-permute-start(bf16[2,1536,128]{2,1,0:T(8,128)(2,1)S(1)} %collective-permute-done.9.refs_7_), channel_id=1, source_target_pairs={{0,64},{64,0},{128,192},{192,128},{256,320},{320,256},{384,448},{4... | collective-permute-start | bytes 2359304 | tf_op jit(solution)/shard_map/ppermute | solution.py:264

commit v8 on v4

--- a/solution.py
+++ b/solution.py
@@ -138,15 +138,14 @@
         s = slot[g]
         return s // 4, pl.multiple_of((s % 4) * NB, NB), s
 
-    def h_copy(ref, k, g):
-        x, lane, s = place(g)
-        return pltpu.make_async_copy(
-            ref.at[k], hbuf.at[x, :, pl.ds(lane, NB)], h_sems.at[s]
-        )
-
-    for i, ref in enumerate(h_refs):
-        for k in range(2):
-            h_copy(ref, k, bases[i] + k).start()
+    for dx in range(3):
+        share = pl.ds(dx * WIDE, WIDE)
+        for i, ref in enumerate(h_refs):
+            for k in range(2):
+                x, lane, s = place(bases[i] + k)
+                pltpu.make_async_copy(
+                    ref.at[k, share], hbuf.at[x, share, pl.ds(lane, NB)], h_sems.at[dx, s]
+                ).start()
 
     for source, side in ((y_own, core), (y_other, 1 - core)):
         for z in range(4):
@@ -161,20 +160,34 @@
             [ybuf[src, (x + 7) % 8], ybuf[src, x], ybuf[src, (x + 1) % 8]], axis=1
         )
 
+    for dx in range(3):
+        share = pl.ds(dx * WIDE, WIDE)
+        for x in range(PLANES):
+            for r in range(4):
+                pltpu.make_async_copy(
+                    h_refs[0].at[0, share],
+                    hbuf.at[x, share, pl.ds(r * NB, NB)],
+                    h_sems.at[dx, 4 * x + r],
+                ).wait()
+            part = jnp.dot(
+                ybuf[0, (x + dx + 7) % 8],
+                hbuf[x, dx * WIDE : (dx + 1) * WIDE],
+                preferred_element_type=F32,
+            )
+            new = part if dx == 0 else zb[x] + part
+            zb[x] = new
+            if dx == 2:
+                ybuf[1, x] = new.astype(BF)
+
     b_copy = pltpu.make_async_copy(b_ref, bbuf, b_sem)
-    for step in range(5):
+    for step in range(1, 5):
         if step == 1:
             b_copy.start()
         src, dst = step % 2, 1 - step % 2
         past = zb if step % 2 == 0 else za
         for x in range(PLANES):
-            if step == 0:
-                for r in range(4):
-                    pltpu.make_async_copy(
-                        h_refs[0].at[0], hbuf.at[x, :, pl.ds(r * NB, NB)], h_sems.at[4 * x + r]
-                    ).wait()
             acc = jnp.dot(around(src, x), hbuf[x], preferred_element_type=F32)
-            new = acc if step == 0 else 2.0 * acc - past[x]
+            new = 2.0 * acc - past[x]
             past[x] = new
             ybuf[dst, x] = new.astype(BF)
 
@@ -217,7 +230,7 @@
             pltpu.VMEM((4, POINTS, NB), BF),
             pltpu.SMEM((32,), jnp.int32),
             pltpu.SMEM((32,), jnp.int32),
-            pltpu.SemaphoreType.DMA((32,)),
+            pltpu.SemaphoreType.DMA((3, 32)),
             pltpu.SemaphoreType.DMA,
         ],
         compiler_params=pltpu.CompilerParams(vmem_limit_bytes=38 * 2**20),

time: 128 us -> 131 us (1.023)
  Pallas kernels: 19.7 us -> 22.2 us
    pallas_call x1, Pallas kernels: 16.6 us -> 19.1 us  [filtering(): pl.pallas_call(filter_kernel, out_shape=(jax.ShapeDtypeStruct((4, NB, NB)...]
where the time goes in v8:
time: 131 us; the launch traced here: 130 us
  starting transfers between devices  55.1 us (42%)
  blocking collectives  28.6 us (22%)
  Pallas kernels  22.2 us (17%)
  waiting for transfers between devices  17.3 us (13%)
  local copies, waits for them, and re-layouts  4.61 us (4%)
    ppermute x15, starting transfers between devices, move(): return lax.ppermute(value, both, pairs)  47.3 us
    all_to_all x1, blocking collectives, local(): lax.all_to_all(parts.reshape(nbands, points // 32, 128), 'band', 0, 0)  28.6 us
    pallas_call x1, Pallas kernels, filtering(): pl.pallas_call(filter_kernel, out_shape=(jax.ShapeDtypeStruct((4, NB, NB)...  19.1 us
    ppermute x15, waiting for transfers between devices, move(): return lax.ppermute(value, both, pairs)  17.3 us
    all_to_all x1, starting transfers between devices, local(): y_own = lax.all_to_all(turned, 'elem', 0, 0, axis_index_groups=groups)  7.81 us
    unnamed x6, local copies, waits for them, and re-layouts  3.58 us
  transfers between devices with their start and end apart: 16, of which 3 were waited for; matrix products, arithmetic and copies ran while one was open for 0% of the time, Pallas kernels for 2%

profile of v8, /device:TPU:1, one launch (start us, length us, event | category | flops | bytes accessed | tf_op | source)
XLA Modules:
  0.0 129.6 jit_solution(8642346785105913475)
XLA Ops:
  0.6 0.7 convert_element_type.4
  1.3 0.0 copy-start.1
  1.3 0.9 copy-done.1
  2.2 0.9 shard_map.59
  3.1 7.8 %all-to-all-start = ((bf16[4,528,128]{2,1,0:T(8,128)(2,1)}), bf16[4,528,128]{2,1,0:T(8,128)(2,1)S(1)}, u32[]{:S(2)}, u32[]{:S(2)}) async-start(bf16[4,528,128]{2,1,0:T(8,128)(2,1)} %shard_map.59), calls=%async_computation | async-start | bytes 1081344 | tf_op jit(solution)/shard_map/all_to_all | solution.py:286
  11.0 0.0 copy-start
  11.0 2.0 %copy-done = bf16[4,27,128,128]{3,2,1,0:T(8,128)(2,1)S(1)} copy-done((bf16[4,27,128,128]{3,2,1,0:T(8,128)(2,1)S(1)}, bf16[4,27,128,128]{3,2,1,0:T(8,128)(2,1)}, u32[]{:S(2)}) %copy-start) | copy-done | bytes 3538968
  13.0 0.0 copy-start.2
  13.0 0.7 copy-done.2
  13.6 2.2 %shard_map.60 = (bf16[2,1536,128]{2,1,0:T(8,128)(2,1)S(1)}, bf16[2,1536,128]{2,1,0:T(8,128)(2,1)S(1)}) custom-call(s32[1]{0:T(128)} %bitcast.1.pair_ref, s32[4,27]{1,0:T(4,128)S(1)} %copy-done.2, bf16[4,27,128,128]{3,2,1,0:T(8,128)(2,1)S(1)} %copy-done, bf16[4,27,128,128]{3,2,1,0:T(8,128)(2,1)S(1)} %copy-done, bf16[4,27,128,128]{3,2,1,0:T(8,128)(2,1)S(1)} %copy-done), custom_call_target="tpu_custom_call" | custom-call | flops 452984832 | bytes 5200000 | tf_op jit(solution)/shard_map/pallas_call | solution.py:66
  15.9 3.4 %collective-permute-start.4 = (bf16[2,1536,128]{2,1,0:T(8,128)(2,1)S(1)}, bf16[2,1536,128]{2,1,0:T(8,128)(2,1)S(1)}, u32[]{:S(2)}, u32[]{:S(2)}) collective-permute-start(bf16[2,1536,128]{2,1,0:T(8,128)(2,1)S(1)} %get-tuple-element.13.refs_0_), channel_id=1, source_target_pairs={{0,128},{64,192},{128,256},{192,320},{256,384},{320,448},{384,4},{... | collective-permute-start | bytes 2359304 | tf_op jit(solution)/shard_map/ppermute | solution.py:277
  19.3 5.0 %collective-permute-start.3 = (bf16[2,1536,128]{2,1,0:T(8,128)(2,1)S(1)}, bf16[2,1536,128]{2,1,0:T(8,128)(2,1)}, u32[]{:S(2)}, u32[]{:S(2)}) collective-permute-start(bf16[2,1536,128]{2,1,0:T(8,128)(2,1)S(1)} %get-tuple-element.12.refs_1_), channel_id=1, source_target_pairs={{0,64},{64,0},{128,192},{192,128},{256,320},{320,256},{384,448},{4... | collective-permute-start | bytes 2359304 | tf_op jit(solution)/shard_map/ppermute | solution.py:277
  24.3 4.9 %collective-permute-start = (bf16[2,1536,128]{2,1,0:T(8,128)(2,1)S(1)}, bf16[2,1536,128]{2,1,0:T(8,128)(2,1)}, u32[]{:S(2)}, u32[]{:S(2)}) collective-permute-start(bf16[2,1536,128]{2,1,0:T(8,128)(2,1)S(1)} %get-tuple-element.12.refs_1_), channel_id=1, source_target_pairs={{0,388},{64,452},{128,0},{192,64},{256,128},{320,192},{384,256},{4... | collective-permute-start | bytes 2359304 | tf_op jit(solution)/shard_map/ppermute | solution.py:277
  29.2 2.2 %collective-permute-start.2 = (bf16[2,1536,128]{2,1,0:T(8,128)(2,1)S(1)}, bf16[2,1536,128]{2,1,0:T(8,128)(2,1)}, u32[]{:S(2)}, u32[]{:S(2)}) collective-permute-start(bf16[2,1536,128]{2,1,0:T(8,128)(2,1)S(1)} %get-tuple-element.13.refs_0_), channel_id=1, source_target_pairs={{0,64},{64,0},{128,192},{192,128},{256,320},{320,256},{384,448},{4... | collective-permute-start | bytes 2359304 | tf_op jit(solution)/shard_map/ppermute | solution.py:277
  31.4 0.0 all-to-all-done.refs_16_
  31.4 2.1 %collective-permute-start.1 = (bf16[4,528,128]{2,1,0:T(8,128)(2,1)S(1)}, bf16[4,528,128]{2,1,0:T(8,128)(2,1)S(1)}, u32[]{:S(2)}, u32[]{:S(2)}) collective-permute-start(bf16[4,528,128]{2,1,0:T(8,128)(2,1)S(1)} %all-to-all-done.refs_16_), channel_id=1, source_target_pairs={{0,64},{64,0},{128,192},{192,128},{256,320},{320,256},{384,448},{4... | collective-permute-start | bytes 1622024 | tf_op jit(solution)/shard_map/ppermute | solution.py:277
  33.6 7.2 %collective-permute-done.4.refs_2_ = bf16[2,1536,128]{2,1,0:T(8,128)(2,1)S(1)} collective-permute-done((bf16[2,1536,128]{2,1,0:T(8,128)(2,1)S(1)}, bf16[2,1536,128]{2,1,0:T(8,128)(2,1)S(1)}, u32[]{:S(2)}, u32[]{:S(2)}) %collective-permute-start.4) | collective-permute-done | bytes 786464 | tf_op jit(solution)/shard_map/ppermute | solution.py:277
  40.7 3.8 %collective-permute-start.9 = (bf16[2,1536,128]{2,1,0:T(8,128)(2,1)S(1)}, bf16[2,1536,128]{2,1,0:T(8,128)(2,1)S(1)}, u32[]{:S(2)}, u32[]{:S(2)}) collective-permute-start(bf16[2,1536,128]{2,1,0:T(8,128)(2,1)S(1)} %collective-permute-done.4.refs_2_), channel_id=1, source_target_pairs={{0,64},{64,0},{128,192},{192,128},{256,320},{320,256},{384,448},{4... | collective-permute-start | bytes 2359304 | tf_op jit(solution)/shard_map/ppermute | solution.py:277
  44.5 0.0 collective-permute-done.3.refs_9_
  44.5 1.9 %collective-permute-start.6 = (bf16[2,1536,128]{2,1,0:T(8,128)(2,1)S(1)}, bf16[2,1536,128]{2,1,0:T(8,128)(2,1)S(1)}, u32[]{:S(2)}, u32[]{:S(2)}) collective-permute-start(bf16[2,1536,128]{2,1,0:T(8,128)(2,1)S(1)} %collective-permute-done.4.refs_2_), channel_id=1, source_target_pairs={{0,128},{64,192},{128,256},{192,320},{256,384},{320,448},{384,4},{... | collective-permute-start | bytes 2359304 | tf_op jit(solution)/shard_map/ppermute | solution.py:277
  46.4 0.0 collective-permute-done.refs_3_
  46.4 3.1 %collective-permute-start.5 = (bf16[2,1536,128]{2,1,0:T(8,128)(2,1)S(1)}, bf16[2,1536,128]{2,1,0:T(8,128)(2,1)S(1)}, u32[]{:S(2)}, u32[]{:S(2)}) collective-permute-start(bf16[2,1536,128]{2,1,0:T(8,128)(2,1)S(1)} %collective-permute-done.4.refs_2_), channel_id=1, source_target_pairs={{0,1},{64,65},{128,129},{192,193},{256,257},{320,321},{384,385},{4... | collective-permute-start | bytes 2359304 | tf_op jit(solution)/shard_map/ppermute | solution.py:277
  49.6 0.0 collective-permute-done.2.refs_8_
  49.6 0.0 collective-permute-done.1.refs_17_
  49.6 3.2 %collective-permute-start.8 = (bf16[2,1536,128]{2,1,0:T(8,128)(2,1)}, bf16[2,1536,128]{2,1,0:T(8,128)(2,1)S(1)}, u32[]{:S(2)}, u32[]{:S(2)}) collective-permute-start(bf16[2,1536,128]{2,1,0:T(8,128)(2,1)} %collective-permute-done.refs_3_), channel_id=1, source_target_pairs={{0,8},{64,72},{128,136},{192,200},{256,264},{320,328},{384,392},{4... | collective-permute-start | bytes 2359304 | tf_op jit(solution)/shard_map/ppermute | solution.py:277
  52.8 5.6 %collective-permute-start.7 = (bf16[2,1536,128]{2,1,0:T(8,128)(2,1)}, bf16[2,1536,128]{2,1,0:T(8,128)(2,1)S(1)}, u32[]{:S(2)}, u32[]{:S(2)}) collective-permute-start(bf16[2,1536,128]{2,1,0:T(8,128)(2,1)} %collective-permute-done.refs_3_), channel_id=1, source_target_pairs={{0,388},{64,452},{128,0},{192,64},{256,128},{320,192},{384,256},{4... | collective-permute-start | bytes 2359304 | tf_op jit(solution)/shard_map/ppermute | solution.py:277
  58.5 8.5 %collective-permute-done.5.refs_6_ = bf16[2,1536,128]{2,1,0:T(8,128)(2,1)S(1)} collective-permute-done((bf16[2,1536,128]{2,1,0:T(8,128)(2,1)S(1)}, bf16[2,1536,128]{2,1,0:T(8,128)(2,1)S(1)}, u32[]{:S(2)}, u32[]{:S(2)}) %collective-permute-start.5) | collective-permute-done | bytes 786464 | tf_op jit(solution)/shard_map/ppermute | solution.py:277
  67.0 3.2 %collective-permute-start.10 = (bf16[2,1536,128]{2,1,0:T(8,128)(2,1)}, bf16[2,1536,128]{2,1,0:T(8,128)(2,1)S(1)}, u32[]{:S(2)}, u32[]{:S(2)}) collective-permute-start(bf16[2,1536,128]{2,1,0:T(8,128)(2,1)} %collective-permute-done.refs_3_), channel_id=1, source_target_pairs={{0,64},{64,0},{128,192},{192,128},{256,320},{320,256},{384,448},{4... | collective-permute-start | bytes 2359304 | tf_op jit(solution)/shard_map/ppermute | solution.py:277
  70.2 0.0 collective-permute-done.9.refs_10_
  70.2 1.9 %collective-permute-start.13 = (bf16[2,1536,128]{2,1,0:T(8,128)(2,1)S(1)}, bf16[2,1536,128]{2,1,0:T(8,128)(2,1)S(1)}, u32[]{:S(2)}, u32[]{:S(2)}) collective-permute-start(bf16[2,1536,128]{2,1,0:T(8,128)(2,1)S(1)} %collective-permute-done.5.refs_6_), channel_id=1, source_target_pairs={{0,64},{64,0},{128,192},{192,128},{256,320},{320,256},{384,448},{4... | collective-permute-start | bytes 2359304 | tf_op jit(solution)/shard_map/ppermute | solution.py:277
  72.1 0.0 collective-permute-done.6.refs_4_
  72.2 2.4 %collective-permute-start.11 = (bf16[2,1536,128]{2,1,0:T(8,128)(2,1)S(1)}, bf16[2,1536,128]{2,1,0:T(8,128)(2,1)S(1)}, u32[]{:S(2)}, u32[]{:S(2)}) collective-permute-start(bf16[2,1536,128]{2,1,0:T(8,128)(2,1)S(1)} %collective-permute-done.6.refs_4_), channel_id=1, source_target_pairs={{0,64},{64,0},{128,192},{192,128},{256,320},{320,256},{384,448},{4... | collective-permute-start | bytes 2359304 | tf_op jit(solution)/shard_map/ppermute | solution.py:277
  74.6 0.0 collective-permute-done.8.refs_7_
  74.6 1.9 %collective-permute-start.14 = (bf16[2,1536,128]{2,1,0:T(8,128)(2,1)S(1)}, bf16[2,1536,128]{2,1,0:T(8,128)(2,1)S(1)}, u32[]{:S(2)}, u32[]{:S(2)}) collective-permute-start(bf16[2,1536,128]{2,1,0:T(8,128)(2,1)S(1)} %collective-permute-done.8.refs_7_), channel_id=1, source_target_pairs={{0,64},{64,0},{128,192},{192,128},{256,320},{320,256},{384,448},{4... | collective-permute-start | bytes 2359304 | tf_op jit(solution)/shard_map/ppermute | solution.py:277
  76.5 0.0 collective-permute-done.7.refs_5_
  76.5 2.6 %collective-permute-start.12 = (bf16[2,1536,128]{2,1,0:T(8,128)(2,1)S(1)}, bf16[2,1536,128]{2,1,0:T(8,128)(2,1)S(1)}, u32[]{:S(2)}, u32[]{:S(2)}) collective-permute-start(bf16[2,1536,128]{2,1,0:T(8,128)(2,1)S(1)} %collective-permute-done.7.refs_5_), channel_id=1, source_target_pairs={{0,64},{64,0},{128,192},{192,128},{256,320},{320,256},{384,448},{4... | collective-permute-start | bytes 2359304 | tf_op jit(solution)/shard_map/ppermute | solution.py:277
  79.1 0.0 collective-permute-done.10.refs_11_
  79.1 0.0 collective-permute-done.11.refs_12_
  79.1 0.0 collective-permute-done.13.refs_14_
  79.1 0.0 collective-permute-done.14.refs_15_
  79.2 1.7 %collective-permute-done.12.refs_13_ = bf16[2,1536,128]{2,1,0:T(8,128)(2,1)S(1)} collective-permute-done((bf16[2,1536,128]{2,1,0:T(8,128)(2,1)S(1)}, bf16[2,1536,128]{2,1,0:T(8,128)(2,1)S(1)}, u32[]{:S(2)}, u32[]{:S(2)}) %collective-permute-start.12) | collective-permute-done | bytes 786464 | tf_op jit(solution)/shard_map/ppermute | solution.py:277
  80.8 19.1 %shard_map.61 = (bf16[4,128,128]{2,1,0:T(8,128)(2,1)}, f32[4,4096]{1,0:T(4,128)S(1)}) custom-call(s32[32,27]{1,0:T(8,128)S(1)} %bitcast.9, bf16[2,1536,128]{2,1,0:T(8,128)(2,1)S(1)} %get-tuple-element.13.refs_0_, bf16[2,1536,128]{2,1,0:T(8,128)(2,1)S(1)} %get-tuple-element.12.refs_1_, bf16[2,1536,128]{2,1,0:T(8,128)(2,1)S(1)} %collective-permute-done.4.refs_2_, ...), custom_call_target="tpu_custom_call" | custom-call | tf_op jit(solution)/shard_map/pallas_call | solution.py:217
  99.9 0.1 reshape.17
  100.0 0.1 copy.9
  100.1 0.1 reshape.18
  100.2 28.6 %all_to_all.10 = f32[64,2,128]{2,1,0:T(2,128)S(1)} all-to-all(f32[64,2,128]{2,1,0:T(2,128)S(1)} %reshape.18), channel_id=1, replica_groups=mesh['elem'=8,'band'=64] {'band'}, dimensions={0} | all-to-all | bytes 131072 | tf_op jit(solution)/shard_map/all_to_all | solution.py:312
  128.8 0.1 reduce_sum.9
  128.9 0.7 reshape.19
  (6 shorter events, 0.0 us)
Async XLA Ops:
  1.3 0.9 copy-start.1
  3.1 28.3 %all-to-all-start = ((bf16[4,528,128]{2,1,0:T(8,128)(2,1)}), bf16[4,528,128]{2,1,0:T(8,128)(2,1)S(1)}, u32[]{:S(2)}, u32[]{:S(2)}) async-start(bf16[4,528,128]{2,1,0:T(8,128)(2,1)} %shard_map.59), calls=%async_computation | async-start | bytes 1081344 | tf_op jit(solution)/shard_map/all_to_all | solution.py:286
  11.0 2.0 %copy-start = (bf16[4,27,128,128]{3,2,1,0:T(8,128)(2,1)S(1)}, bf16[4,27,128,128]{3,2,1,0:T(8,128)(2,1)}, u32[]{:S(2)}) copy-start(bf16[4,27,128,128]{3,2,1,0:T(8,128)(2,1)} %h2_ref.1) | copy-start | bytes 10616836
  13.0 0.7 copy-start.2
  15.9 24.8 %collective-permute-start.4 = (bf16[2,1536,128]{2,1,0:T(8,128)(2,1)S(1)}, bf16[2,1536,128]{2,1,0:T(8,128)(2,1)S(1)}, u32[]{:S(2)}, u32[]{:S(2)}) collective-permute-start(bf16[2,1536,128]{2,1,0:T(8,128)(2,1)S(1)} %get-tuple-element.13.refs_0_), channel_id=1, source_target_pairs={{0,128},{64,192},{128,256},{192,320},{256,384},{320,448},{384,4},{... | collective-permute-start | bytes 2359304 | tf_op jit(solution)/shard_map/ppermute | solution.py:277
  19.3 25.2 %collective-permute-start.3 = (bf16[2,1536,128]{2,1,0:T(8,128)(2,1)S(1)}, bf16[2,1536,128]{2,1,0:T(8,128)(2,1)}, u32[]{:S(2)}, u32[]{:S(2)}) collective-permute-start(bf16[2,1536,128]{2,1,0:T(8,128)(2,1)S(1)} %get-tuple-element.12.refs_1_), channel_id=1, source_target_pairs={{0,64},{64,0},{128,192},{192,128},{256,320},{320,256},{384,448},{4... | collective-permute-start | bytes 2359304 | tf_op jit(solution)/shard_map/ppermute | solution.py:277
  24.3 22.2 %collective-permute-start = (bf16[2,1536,128]{2,1,0:T(8,128)(2,1)S(1)}, bf16[2,1536,128]{2,1,0:T(8,128)(2,1)}, u32[]{:S(2)}, u32[]{:S(2)}) collective-permute-start(bf16[2,1536,128]{2,1,0:T(8,128)(2,1)S(1)} %get-tuple-element.12.refs_1_), channel_id=1, source_target_pairs={{0,388},{64,452},{128,0},{192,64},{256,128},{320,192},{384,256},{4... | collective-permute-start | bytes 2359304 | tf_op jit(solution)/shard_map/ppermute | solution.py:277
  29.2 20.4 %collective-permute-start.2 = (bf16[2,1536,128]{2,1,0:T(8,128)(2,1)S(1)}, bf16[2,1536,128]{2,1,0:T(8,128)(2,1)}, u32[]{:S(2)}, u32[]{:S(2)}) collective-permute-start(bf16[2,1536,128]{2,1,0:T(8,128)(2,1)S(1)} %get-tuple-element.13.refs_0_), channel_id=1, source_target_pairs={{0,64},{64,0},{128,192},{192,128},{256,320},{320,256},{384,448},{4... | collective-permute-start | bytes 2359304 | tf_op jit(solution)/shard_map/ppermute | solution.py:277
  31.4 18.2 %collective-permute-start.1 = (bf16[4,528,128]{2,1,0:T(8,128)(2,1)S(1)}, bf16[4,528,128]{2,1,0:T(8,128)(2,1)S(1)}, u32[]{:S(2)}, u32[]{:S(2)}) collective-permute-start(bf16[4,528,128]{2,1,0:T(8,128)(2,1)S(1)} %all-to-all-done.refs_16_), channel_id=1, source_target_pairs={{0,64},{64,0},{128,192},{192,128},{256,320},{320,256},{384,448},{4... | collective-permute-start | bytes 1622024 | tf_op jit(solution)/shard_map/ppermute | solution.py:277
  40.7 29.5 %collective-permute-start.9 = (bf16[2,1536,128]{2,1,0:T(8,128)(2,1)S(1)}, bf16[2,1536,128]{2,1,0:T(8,128)(2,1)S(1)}, u32[]{:S(2)}, u32[]{:S(2)}) collective-permute-start(bf16[2,1536,128]{2,1,0:T(8,128)(2,1)S(1)} %collective-permute-done.4.refs_2_), channel_id=1, source_target_pairs={{0,64},{64,0},{128,192},{192,128},{256,320},{320,256},{384,448},{4... | collective-permute-start | bytes 2359304 | tf_op jit(solution)/shard_map/ppermute | solution.py:277
  44.5 27.6 %collective-permute-start.6 = (bf16[2,1536,128]{2,1,0:T(8,128)(2,1)S(1)}, bf16[2,1536,128]{2,1,0:T(8,128)(2,1)S(1)}, u32[]{:S(2)}, u32[]{:S(2)}) collective-permute-start(bf16[2,1536,128]{2,1,0:T(8,128)(2,1)S(1)} %collective-permute-done.4.refs_2_), channel_id=1, source_target_pairs={{0,128},{64,192},{128,256},{192,320},{256,384},{320,448},{384,4},{... | collective-permute-start | bytes 2359304 | tf_op jit(solution)/shard_map/ppermute | solution.py:277
  46.4 20.5 %collective-permute-start.5 = (bf16[2,1536,128]{2,1,0:T(8,128)(2,1)S(1)}, bf16[2,1536,128]{2,1,0:T(8,128)(2,1)S(1)}, u32[]{:S(2)}, u32[]{:S(2)}) collective-permute-start(bf16[2,1536,128]{2,1,0:T(8,128)(2,1)S(1)} %collective-permute-done.4.refs_2_), channel_id=1, source_target_pairs={{0,1},{64,65},{128,129},{192,193},{256,257},{320,321},{384,385},{4... | collective-permute-start | bytes 2359304 | tf_op jit(solution)/shard_map/ppermute | solution.py:277
  49.6 25.0 %collective-permute-start.8 = (bf16[2,1536,128]{2,1,0:T(8,128)(2,1)}, bf16[2,1536,128]{2,1,0:T(8,128)(2,1)S(1)}, u32[]{:S(2)}, u32[]{:S(2)}) collective-permute-start(bf16[2,1536,128]{2,1,0:T(8,128)(2,1)} %collective-permute-done.refs_3_), channel_id=1, source_target_pairs={{0,8},{64,72},{128,136},{192,200},{256,264},{320,328},{384,392},{4... | collective-permute-start | bytes 2359304 | tf_op jit(solution)/shard_map/ppermute | solution.py:277
  52.8 23.7 %collective-permute-start.7 = (bf16[2,1536,128]{2,1,0:T(8,128)(2,1)}, bf16[2,1536,128]{2,1,0:T(8,128)(2,1)S(1)}, u32[]{:S(2)}, u32[]{:S(2)}) collective-permute-start(bf16[2,1536,128]{2,1,0:T(8,128)(2,1)} %collective-permute-done.refs_3_), channel_id=1, source_target_pairs={{0,388},{64,452},{128,0},{192,64},{256,128},{320,192},{384,256},{4... | collective-permute-start | bytes 2359304 | tf_op jit(solution)/shard_map/ppermute | solution.py:277
  67.0 12.1 %collective-permute-start.10 = (bf16[2,1536,128]{2,1,0:T(8,128)(2,1)}, bf16[2,1536,128]{2,1,0:T(8,128)(2,1)S(1)}, u32[]{:S(2)}, u32[]{:S(2)}) collective-permute-start(bf16[2,1536,128]{2,1,0:T(8,128)(2,1)} %collective-permute-done.refs_3_), channel_id=1, source_target_pairs={{0,64},{64,0},{128,192},{192,128},{256,320},{320,256},{384,448},{4... | collective-permute-start | bytes 2359304 | tf_op jit(solution)/shard_map/ppermute | solution.py:277
  70.2 8.9 %collective-permute-start.13 = (bf16[2,1536,128]{2,1,0:T(8,128)(2,1)S(1)}, bf16[2,1536,128]{2,1,0:T(8,128)(2,1)S(1)}, u32[]{:S(2)}, u32[]{:S(2)}) collective-permute-start(bf16[2,1536,128]{2,1,0:T(8,128)(2,1)S(1)} %collective-permute-done.5.refs_6_), channel_id=1, source_target_pairs={{0,64},{64,0},{128,192},{192,128},{256,320},{320,256},{384,448},{4... | collective-permute-start | bytes 2359304 | tf_op jit(solution)/shard_map/ppermute | solution.py:277
  72.2 7.0 %collective-permute-start.11 = (bf16[2,1536,128]{2,1,0:T(8,128)(2,1)S(1)}, bf16[2,1536,128]{2,1,0:T(8,128)(2,1)S(1)}, u32[]{:S(2)}, u32[]{:S(2)}) collective-permute-start(bf16[2,1536,128]{2,1,0:T(8,128)(2,1)S(1)} %collective-permute-done.6.refs_4_), channel_id=1, source_target_pairs={{0,64},{64,0},{128,192},{192,128},{256,320},{320,256},{384,448},{4... | collective-permute-start | bytes 2359304 | tf_op jit(solution)/shard_map/ppermute | solution.py:277
  74.6 4.6 %collective-permute-start.14 = (bf16[2,1536,128]{2,1,0:T(8,128)(2,1)S(1)}, bf16[2,1536,128]{2,1,0:T(8,128)(2,1)S(1)}, u32[]{:S(2)}, u32[]{:S(2)}) collective-permute-start(bf16[2,1536,128]{2,1,0:T(8,128)(2,1)S(1)} %collective-permute-done.8.refs_7_), channel_id=1, source_target_pairs={{0,64},{64,0},{128,192},{192,128},{256,320},{320,256},{384,448},{4... | collective-permute-start | bytes 2359304 | tf_op jit(solution)/shard_map/ppermute | solution.py:277
  76.5 4.3 %collective-permute-start.12 = (bf16[2,1536,128]{2,1,0:T(8,128)(2,1)S(1)}, bf16[2,1536,128]{2,1,0:T(8,128)(2,1)S(1)}, u32[]{:S(2)}, u32[]{:S(2)}) collective-permute-start(bf16[2,1536,128]{2,1,0:T(8,128)(2,1)S(1)} %collective-permute-done.7.refs_5_), channel_id=1, source_target_pairs={{0,64},{64,0},{128,192},{192,128},{256,320},{320,256},{384,448},{4... | collective-permute-start | bytes 2359304 | tf_op jit(solution)/shard_map/ppermute | solution.py:277
